TPU v7x, 32 devices: a whole 2x2x4 slice. The times are simulated.
32 devices in a mesh: batch: 2 (over x), seq: 16 (over z, y, core).
Axes of the slice: x: 2, y: 2, z: 4, core: 2. Of those that a mesh axis runs over, the one named last changes fastest.
Arguments:
- hidden_in: bfloat16 [4096, 2048], P(('batch', 'seq')), may hold values from -6 to 6
- cotangent: bfloat16 [4096, 2048], P(('batch', 'seq')), may hold values from -6 to 6
- master: float32 [2048, 24579], P(('batch', 'seq'))
- first: float32 [2048, 24579], P(('batch', 'seq'))
- second: float32 [2048, 24579], P(('batch', 'seq'))
- average: float32 [2048, 24579], P(('batch', 'seq'))
- lengths: int32 [2, 4], P('batch'), may hold values from 50 to 1024, as said below
- prefix: int32 [2, 4], P('batch'), may hold values from 1 to 1023, as said below
- padding: int32 [2, 4], P('batch'), may hold values from 0 to 256, as said below
Outputs:
- output: bfloat16 [4096, 2048], P(('batch', 'seq'))
- input_grad: bfloat16 [4096, 2048], P(('batch', 'seq'))
- new_master: float32 [2048, 24579], P(('batch', 'seq'))
- new_first: float32 [2048, 24579], P(('batch', 'seq'))
- new_second: float32 [2048, 24579], P(('batch', 'seq'))
- new_average: float32 [2048, 24579], P(('batch', 'seq'))
Inputs may be any that keep to these rules, and one draw needn't show every extreme that they name: The lengths of each group sum to 2048; one of them is 1024. Each prefix is below its chain's length. Each padding is at most a quarter of its chain's length, rounded down.
All inputs are finite; a program needn't handle non-finite values.
Results may differ from a plain program's by a relative error of at most 0.0087.
Values may be sent and summed in bfloat16 or wider, within the bound.
A program may use at most 320 MiB of HBM per device.

v0:
```python
import math

import jax
import jax.numpy as jnp
from jax import lax
from jax.sharding import PartitionSpec as P

D = 2048
H = 16
HD = 128
FF = 5461
CHAIN_MAX = 1024
STEP = 10


DEEP_ALPHA = math.sqrt(48.0)
ROPE_BASE = 10000.0
NEG_LARGE = -1e30
LN_EPS = 1e-05
BETA_ONE = 0.9
BETA_TWO = 0.95
ADAM_EPS = 1e-08
LR_MAT = 0.01
LR_VEC = 0.2
DECAY_MAT = 0.1
EMA_RATE = 0.9


def layer_norm(values, gain_vec, bias_vec):
    centre = values - jnp.mean(values, axis=-1, keepdims=True)
    spread = jnp.mean(centre * centre, axis=-1, keepdims=True)
    return centre * lax.rsqrt(spread + LN_EPS) * gain_vec + bias_vec


def geglu(gate_up):
    return jax.nn.gelu(gate_up[:, :FF]) * gate_up[:, FF:]


def chain_tables(chain_len, chain_prefix, chain_pad, total):
    ends_at = jnp.cumsum(chain_len, dtype=jnp.int32)
    starts_at = ends_at - chain_len
    tokens_at = jnp.arange(total, dtype=jnp.int32)
    member = (
        (tokens_at[:, None] >= starts_at[None, :]) & (tokens_at[:, None] < ends_at[None, :])
    ).astype(jnp.int32)
    chain_ids = jnp.arange(chain_len.shape[0], dtype=jnp.int32)
    segment = jnp.sum(member * chain_ids[None, :], axis=1, dtype=jnp.int32)
    position = tokens_at - jnp.sum(member * starts_at[None, :], axis=1, dtype=jnp.int32)
    prefix_tok = jnp.sum(member * chain_prefix[None, :], axis=1, dtype=jnp.int32)
    live_len = jnp.sum(member * (chain_len - chain_pad)[None, :], axis=1, dtype=jnp.int32)
    return (segment, position, prefix_tok, position < live_len)


def rotate(values, position, sign):
    half = values.shape[-1] // 2
    freq = ROPE_BASE ** (-jnp.arange(half, dtype=jnp.float32) / half)
    angles = position.astype(jnp.float32)[:, None] * freq[None, :]
    cosine = jnp.cos(angles)[:, None, :]
    sine = sign * jnp.sin(angles)[:, None, :]
    first_half = values[..., :half]
    second_half = values[..., half:]
    return jnp.concatenate(
        [first_half * cosine - second_half * sine, first_half * sine + second_half * cosine],
        axis=-1,
    )


def block_mask(row_start, key_start, block_rows, key_span, tables):
    segment, position, prefix_tok, live_tok = tables
    q_index = row_start + jnp.arange(block_rows, dtype=jnp.int32)
    k_index = key_start + jnp.arange(key_span, dtype=jnp.int32)
    seg_q = lax.dynamic_slice_in_dim(segment, row_start, block_rows)
    same = seg_q[:, None] == segment[None, :]
    order = (position < prefix_tok)[None, :] | (k_index[None, :] <= q_index[:, None])
    return same & live_tok[None, :] & order


def block_scores(query_h, key_h, block_idx, block_rows, key_span, tables):
    group_rows = query_h.shape[0]
    row_start = block_idx * block_rows
    key_start = jnp.clip(row_start - CHAIN_MAX, 0, group_rows - key_span)
    q_blk = lax.dynamic_slice_in_dim(query_h, row_start, block_rows, 0)
    scores = jnp.einsum(
        "qhd,khd->hqk", q_blk, key_h, preferred_element_type=jnp.float32
    ) * query_h.shape[-1] ** (-0.5)
    mask_blk = block_mask(row_start, key_start, block_rows, key_span, tables)
    return (jnp.where(mask_blk[None], scores, NEG_LARGE), row_start, key_start, q_blk, key_h)


def attention_forward(query_h, key_h, value_h, tables, key_span):
    group_rows = query_h.shape[0]
    block_rows = min(512, group_rows)
    block_count = group_rows // block_rows

    def one_block(block_idx):
        scores, row_start, key_start, q_blk, k_blk = block_scores(
            query_h, key_h, block_idx, block_rows, key_span, tables
        )
        row_max = jnp.max(scores, axis=-1, keepdims=True)
        log_total = row_max + jnp.log(jnp.sum(jnp.exp(scores - row_max), axis=-1, keepdims=True))
        probs = jnp.exp(scores - log_total)
        attended = jnp.einsum(
            "hqk,khd->qhd", probs.astype(jnp.bfloat16), value_h, preferred_element_type=jnp.float32
        )
        return (attended.astype(jnp.bfloat16), log_total[..., 0])

    outs, totals = lax.map(one_block, jnp.arange(block_count, dtype=jnp.int32))
    return (outs.reshape(group_rows, query_h.shape[1], query_h.shape[2]), totals)


def attention_backward(query_h, key_h, value_h, grad_h, totals, tables, key_span):
    group_rows = query_h.shape[0]
    block_rows = min(512, group_rows)
    block_count = group_rows // block_rows
    scale = query_h.shape[-1] ** (-0.5)
    zeros_f = jnp.zeros(query_h.shape, jnp.float32)

    def one_step(block_idx, carry):
        q_grad, k_grad, v_grad = carry
        scores, row_start, key_start, q_blk, k_blk = block_scores(
            query_h, key_h, block_idx, block_rows, key_span, tables
        )
        g_blk = lax.dynamic_slice_in_dim(grad_h, row_start, block_rows, 0)
        log_total = lax.dynamic_index_in_dim(totals, block_idx, 0, keepdims=False)
        probs = jnp.exp(scores - log_total[..., None])
        prob_grad = jnp.einsum("qhd,khd->hqk", g_blk, value_h, preferred_element_type=jnp.float32)
        inner = jnp.sum(probs * prob_grad, axis=-1, keepdims=True)
        score_grad = (probs * (prob_grad - inner)).astype(jnp.bfloat16)
        q_part = (
            jnp.einsum("hqk,khd->qhd", score_grad, k_blk, preferred_element_type=jnp.float32)
            * scale
        )
        k_part = (
            jnp.einsum("hqk,qhd->khd", score_grad, q_blk, preferred_element_type=jnp.float32)
            * scale
        )
        v_part = jnp.einsum(
            "hqk,qhd->khd", probs.astype(jnp.bfloat16), g_blk, preferred_element_type=jnp.float32
        )
        q_grad = lax.dynamic_update_slice_in_dim(q_grad, q_part, row_start, 0)
        k_grad = k_grad + k_part
        v_grad = v_grad + v_part
        return (q_grad, k_grad, v_grad)

    q_grad, k_grad, v_grad = lax.fori_loop(0, block_count, one_step, (zeros_f, zeros_f, zeros_f))
    return jnp.stack([q_grad, k_grad, v_grad], axis=1)


def split_weights(gathered):
    w_qkv = gathered[:, : 3 * D]
    w_out = gathered[:, 3 * D : 4 * D]
    w_up = gathered[:, 4 * D : 4 * D + 2 * FF]
    w_down = gathered[:, 4 * D + 2 * FF : 4 * D + 3 * FF]
    vectors = gathered[:, 4 * D + 3 * FF :].astype(jnp.float32)
    return (w_qkv, w_out, w_up, w_down, vectors)


def contract_last(left, right):
    return lax.dot_general(
        left, right, (((1,), (1,)), ((), ())), preferred_element_type=jnp.float32
    )


def contract_first(left, right):
    return lax.dot_general(
        left, right, (((0,), (0,)), ((), ())), preferred_element_type=jnp.float32
    )


def pad_columns(values, parts_count):
    surplus = -values.shape[1] % parts_count
    return jnp.pad(values, ((0, 0), (0, surplus)))


def on_device(hidden_in, cotangent, master, first, second, average, lengths, prefix, padding):
    seq_count = lax.axis_size("seq")
    seq_place = lax.axis_index("seq")
    tok_rows = hidden_in.shape[0]
    group_rows = tok_rows * seq_count
    gathered = lax.all_gather(master.astype(jnp.bfloat16), ("batch", "seq"), axis=0, tiled=True)
    w_qkv, w_out, w_up, w_down, vectors = split_weights(gathered)
    tables = chain_tables(lengths[0], prefix[0], padding[0], group_rows)
    local_pos = lax.dynamic_slice_in_dim(tables[1], seq_place * tok_rows, tok_rows)
    states_in = hidden_in.astype(jnp.float32)
    normed = layer_norm(states_in, vectors[:, 0], vectors[:, 1])
    normed_low = normed.astype(jnp.bfloat16)
    projected = jnp.dot(normed_low, w_qkv, preferred_element_type=jnp.float32).reshape(
        tok_rows, 3, H, HD
    )
    rotated = jnp.stack(
        [
            rotate(projected[:, 0], local_pos, 1.0),
            rotate(projected[:, 1], local_pos, 1.0),
            projected[:, 2],
        ],
        axis=1,
    ).astype(jnp.bfloat16)
    head_qkv = lax.all_to_all(rotated, "seq", split_axis=2, concat_axis=0, tiled=True)
    query_h = head_qkv[:, 0]
    key_h = head_qkv[:, 1]
    value_h = head_qkv[:, 2]
    attended_h, totals = attention_forward(query_h, key_h, value_h, tables, group_rows)
    attended = lax.all_to_all(attended_h, "seq", split_axis=0, concat_axis=1, tiled=True).reshape(
        tok_rows, D
    )
    branch = jnp.dot(attended, w_out, preferred_element_type=jnp.float32)
    residual = DEEP_ALPHA * normed + branch
    normed_two = layer_norm(residual, vectors[:, 2], vectors[:, 3])
    normed_two_low = normed_two.astype(jnp.bfloat16)
    gate_up = jnp.dot(normed_two_low, w_up, preferred_element_type=jnp.float32)
    hidden = geglu(gate_up).astype(jnp.bfloat16)
    output = DEEP_ALPHA * normed_two + contract_last(hidden, w_down)
    back_qkv, back_out, back_up, back_down, back_vectors = (w_qkv, w_out, w_up, w_down, vectors)
    cot_f = cotangent.astype(jnp.float32)
    hidden_grad = jnp.dot(cotangent, back_down, preferred_element_type=jnp.float32)
    geglu_pull = jax.vjp(geglu, gate_up)[1]
    gate_up_grad = geglu_pull(hidden_grad)[0].astype(jnp.bfloat16)
    normed_two_grad = DEEP_ALPHA * cot_f + contract_last(gate_up_grad, back_up)
    norm_two_pull = jax.vjp(layer_norm, residual, back_vectors[:, 2], back_vectors[:, 3])[1]
    residual_grad, gain_two_grad, bias_two_grad = norm_two_pull(normed_two_grad)
    residual_low = residual_grad.astype(jnp.bfloat16)
    attended_grad = (
        contract_last(residual_low, back_out).astype(jnp.bfloat16).reshape(tok_rows, H, HD)
    )
    head_grad = lax.all_to_all(attended_grad, "seq", split_axis=1, concat_axis=0, tiled=True)
    head_qkv_grad = attention_backward(
        query_h, key_h, value_h, head_grad, totals, tables, group_rows
    ).astype(jnp.bfloat16)
    local_grad = lax.all_to_all(head_qkv_grad, "seq", split_axis=0, concat_axis=2, tiled=True)
    unrotated = jnp.stack(
        [
            rotate(local_grad[:, 0].astype(jnp.float32), local_pos, -1.0),
            rotate(local_grad[:, 1].astype(jnp.float32), local_pos, -1.0),
            local_grad[:, 2].astype(jnp.float32),
        ],
        axis=1,
    )
    projected_grad = unrotated.reshape(tok_rows, 3 * D).astype(jnp.bfloat16)
    normed_grad = DEEP_ALPHA * residual_grad + contract_last(projected_grad, back_qkv)
    norm_one_pull = jax.vjp(layer_norm, states_in, back_vectors[:, 0], back_vectors[:, 1])[1]
    input_grad, gain_one_grad, bias_one_grad = norm_one_pull(normed_grad)
    vector_grad = jnp.stack([gain_one_grad, bias_one_grad, gain_two_grad, bias_two_grad], axis=1)
    right_cols = (
        lax.all_to_all(projected_grad, "seq", split_axis=1, concat_axis=0, tiled=True),
        lax.all_to_all(residual_low, "seq", split_axis=1, concat_axis=0, tiled=True),
        lax.all_to_all(
            pad_columns(gate_up_grad, seq_count), "seq", split_axis=1, concat_axis=0, tiled=True
        ),
        lax.all_to_all(
            pad_columns(hidden, seq_count), "seq", split_axis=1, concat_axis=0, tiled=True
        ),
    )
    widths = [part_cols.shape[1] for part_cols in right_cols]
    block_width = sum(widths)
    pieces = (
        lax.all_gather(normed_low, "seq", axis=0, tiled=True),
        lax.all_gather(attended, "seq", axis=0, tiled=True),
        lax.all_gather(normed_two_low, "seq", axis=0, tiled=True),
        lax.all_gather(cotangent, "seq", axis=0, tiled=True),
    )
    products = [contract_first(left_op, right_op) for left_op, right_op in zip(pieces, right_cols)]
    partial_sum = jnp.concatenate(products, axis=1)
    batch_rows = lax.psum_scatter(
        partial_sum.astype(jnp.bfloat16), "batch", scatter_dimension=0, tiled=True
    ).astype(jnp.float32)
    owned = lax.all_to_all(
        batch_rows.astype(jnp.bfloat16), "seq", split_axis=0, concat_axis=1, tiled=True
    ).astype(batch_rows.dtype)
    own_rows = owned.shape[0]
    blocks = owned.reshape(own_rows, seq_count, block_width)
    pieces_out = []
    column_start = 0
    for width_k, true_width in zip(widths, (3 * D, D, 2 * FF, FF)):
        segment_cols = blocks[:, :, column_start : column_start + width_k].reshape(
            own_rows, seq_count * width_k
        )
        pieces_out.append(segment_cols[:, :true_width])
        column_start = column_start + width_k
    vector_rows = lax.psum_scatter(vector_grad, ("batch", "seq"), scatter_dimension=0, tiled=True)
    grad_shard = jnp.concatenate(pieces_out + [vector_rows], axis=1)
    column = jnp.arange(master.shape[1])
    matrix_col = column < master.shape[1] - 4
    rate = jnp.where(matrix_col, LR_MAT, LR_VEC).astype(jnp.float32)
    decay = jnp.where(matrix_col, DECAY_MAT, 0.0).astype(jnp.float32)
    new_first = BETA_ONE * first + (1.0 - BETA_ONE) * grad_shard
    new_second = BETA_TWO * second + (1.0 - BETA_TWO) * grad_shard * grad_shard
    corrected = (
        new_first
        / (1.0 - BETA_ONE**STEP)
        / (jnp.sqrt(new_second / (1.0 - BETA_TWO**STEP)) + ADAM_EPS)
    )
    new_master = master - rate[None, :] * (corrected + decay[None, :] * master)
    new_average = EMA_RATE * average + (1.0 - EMA_RATE) * new_master
    return (
        output.astype(jnp.bfloat16),
        input_grad.astype(jnp.bfloat16),
        new_master,
        new_first,
        new_second,
        new_average,
    )


def solution(mesh):
    placed = (
        P(("batch", "seq"), None),
        P(("batch", "seq"), None),
        P(("batch", "seq"), None),
        P(("batch", "seq"), None),
        P(("batch", "seq"), None),
        P(("batch", "seq"), None),
        P("batch", None),
        P("batch", None),
        P("batch", None),
    )
    return jax.shard_map(
        on_device,
        mesh=mesh,
        in_specs=placed,
        out_specs=(
            P(("batch", "seq"), None),
            P(("batch", "seq"), None),
            P(("batch", "seq"), None),
            P(("batch", "seq"), None),
            P(("batch", "seq"), None),
            P(("batch", "seq"), None),
        ),
        check_vma=False,
    )
```

profile of v0, /device:TPU:9, one launch (start us, length us, event | category | flops | bytes accessed | tf_op | source)
XLA Modules:
  0.0 1400.5 jit_solution(9210749570094667694)
XLA Ops:
  7.2 4.8 convert_element_type.138
  13.4 518.0 %all-gather.6.cloned.1.call-done = bf16[2048,24579]{1,0:T(8,128)(2,1)} async-done(((bf16[64,24579]{1,0:T(8,128)(2,1)}), bf16[2048,24579]{1,0:T(8,128)(2,1)}) %all-gather.6.cloned.1.call-update) | async-done | bytes 100675600 | tf_op jit(solution)/shard_map/all_gather | solution.py:180
  537.6 10.7 fusion.74
  552.7 6.0 all-to-all-start
  559.0 65.4 %all-to-all-done = bf16[128,3,16,128]{3,0,1,2:T(8,128)(2,1)S(1)} async-done(((bf16[128,3,16,128]{3,0,1,2:T(8,128)(2,1)}), bf16[128,3,16,128]{3,0,1,2:T(8,128)(2,1)S(1)}, u32[]{:S(2)}, u32[]{:S(2)}) %all-to-all-start) | async-done | bytes 1572896 | tf_op jit(solution)/shard_map/all_to_all | solution.py:198
  624.6 21.4 %while.34 = (s32[]{:T(128)}, bf16[4,512,1,128]{3,1,2,0:T(8,128)(2,1)}, f32[4,1,512]{2,1,0:T(1,128)S(1)}, s32[4]{0:T(128)S(1)}, s32[2048]{0:T(1024)S(1)}, /*index...) while((s32[]{:T(128)}, ...), condition=%wide.region_10.11_spmd, body=%wide.region_7.10_spmd.sunk | while | flops 549521408 | bytes 13955348 | solution.py:107
  646.6 2.1 reduce.27
  648.8 24.4 %all_to_all.155 = bf16[16,2,8192]{2,1,0:T(2,128)(2,1)} all-to-all(bf16[16,2,8192]{2,1,0:T(2,128)(2,1)S(1)} %reshape.529), channel_id=1, replica_groups=mesh['batch'=2,'seq'=16] {'seq'}, dimensions={0} | all-to-all | bytes 1048576 | tf_op jit(solution)/shard_map/all_to_all | solution.py:203
  673.1 2.2 reshape.530
  678.3 5.2 fusion.109
  684.1 25.0 %fusion.34 = f32[128,10922]{0,1:T(8,128)} fusion(bf16[128,2048]{1,0:T(8,128)(2,1)S(1)} %fusion.93, bf16[2048,24579]{1,0:T(8,128)(2,1)} %all-gather.6.cloned.1.call-done), kind=kOutput, calls=%fused_computation.50 | convolution fusion | flops 5726273536 | bytes 51205120 | tf_op jit(solution)/shard_map/dot_general | solution.py:210
  709.1 27.5 %fusion.92 = (f32[128,5461]{0,1:T(8,128)}, f32[128,5461]{0,1:T(8,128)}, bf16[128,5461]{0,1:T(8,128)(2,1)}) fusion(f32[128,10922]{0,1:T(8,128)} %fusion.34, bf16[128,2048]{1,0:T(8,128)(2,1)S(1)} %copy-done.18, bf16[2048,24579]{1,0:T(8,128)(2,1)} %all-gather.6.cloned.1.call-done), kind=kOutput, calls=%fused_computation.139 | convolution fusion | flops 2879910912 | bytes 35653888 | tf_op jit(solution)/shard_map/dot_general | solution.py:215
  736.6 6.3 add_convert_fusion
  743.0 24.0 %multiply_reduce_fusion.1 = (f32[2048]{0:T(1024)}, f32[128]{0:T(128)S(1)}, f32[2048]{0:T(1024)}, f32[128,2048]{1,0:T(8,128)}) fusion(f32[128,2048]{1,0:T(8,128)S(1)} %get-tuple-element.595, f32[128]{0:T(128)S(1)} %fusion.101, f32[128]{0:T(128)S(1)} %broadcast_multiply_fusion.1, f32[2048]{0:T(1024)S(1)} %get-tuple-element.502, ...), kind=kOutput, calls=%fused_computation.125 | convolution fusion | flops 5729153024 | bytes 50532352 | tf_op jit(solution)/shard_map/dot_general | solution.py:159
  768.6 6.7 fusion.81
  776.2 4.6 all-to-all-start.2
  784.2 13.8 all-to-all-done.2
  798.0 5.1 all-to-all-start.7
  804.0 67.1 %while.35 = (s32[]{:T(128)}, bf16[2048,1,128]{2,0,1:T(8,128)(2,1)}, f32[2048,1,128]{0,2,1:T(8,128)}, f32[2048,1,128]{0,2,1:T(8,128)}, s32[2048]{0:T(1024)S(1)}, ...) while((s32[]{:T(128)}, bf16[2048,1,128]{2,0,1:T(8,128)(2,1)}, ...), condition=%wide.region_17.18_spmd.clone, body=%wide.region_15.17_spmd.clone.sunk | while | flops 1358235648 | bytes 96784880 | solution.py:145
  804.0 2.7 fusion.154
  806.9 5.0 multiply_reduce_fusion.5
  815.5 2.5 fusion.156
  818.1 2.4 fusion.157
  820.5 2.7 fusion.154
  823.3 4.7 multiply_reduce_fusion.5
  831.7 2.9 fusion.156
  834.6 2.8 fusion.157
  837.4 2.7 fusion.154
  840.2 4.7 multiply_reduce_fusion.5
  848.6 2.9 fusion.156
  851.5 2.8 fusion.157
  854.3 2.7 fusion.154
  857.1 4.7 multiply_reduce_fusion.5
  865.4 2.9 fusion.156
  868.3 2.8 fusion.157
  875.4 10.7 copy.116
  886.1 6.5 all-to-all-start.3
  892.7 2.5 pad.16
  897.1 41.4 %all-to-all-done.3 = bf16[2048,3,1,128]{3,1,2,0:T(4,128)(2,1)} async-done(((bf16[2048,3,1,128]{3,1,2,0:T(4,128)(2,1)}), bf16[2048,3,1,128]{3,1,2,0:T(4,128)(2,1)}, u32[]{:S(2)}, u32[]{:S(2)}) %all-to-all-start.3) | async-done | bytes 1572896 | tf_op jit(solution)/shard_map/all_to_all | solution.py:229
  938.6 6.3 all-to-all-start.6
  949.7 2.6 copy.118
  952.3 53.4 %all-to-all-done.6 = bf16[128,16,683]{0,2,1:T(8,128)(2,1)S(1)} async-done(((bf16[128,16,683]{0,2,1:T(8,128)(2,1)}), bf16[128,16,683]{0,2,1:T(8,128)(2,1)S(1)}, u32[]{:S(2)}, u32[]{:S(2)}) %all-to-all-start.6) | async-done | bytes 2797600 | tf_op jit(solution)/shard_map/all_to_all | solution.py:246
  1005.7 7.0 all-to-all-start.4
  1012.7 2.2 copy_bitcast_fusion.5
  1018.1 30.1 %all-to-all-done.4 = bf16[128,16,384]{0,2,1:T(8,128)(2,1)} async-done(((bf16[128,16,384]{0,2,1:T(8,128)(2,1)}), bf16[128,16,384]{0,2,1:T(8,128)(2,1)}, u32[]{:S(2)}, u32[]{:S(2)}) %all-to-all-start.4) | async-done | bytes 1572896 | tf_op jit(solution)/shard_map/all_to_all | solution.py:244
  1048.2 5.6 all-to-all-start.5
  1054.0 8.0 fusion.55
  1063.9 2.8 copy.120
  1066.7 8.4 convolution_convert_fusion.1
  1075.1 6.3 convolution_convert_fusion.3
  1081.5 10.7 convolution_convert_fusion
  1092.2 29.0 %concatenate.34 = bf16[2048,1537]{0,1:T(8,128)(2,1)} concatenate(bf16[2048,384]{0,1:T(8,128)(2,1)} %convolution_convert_fusion.1, bf16[2048,128]{0,1:T(8,128)(2,1)S(1)} %convolution_convert_fusion.3, bf16[2048,683]{0,1:T(8,128)(2,1)} %convolution_convert_fusion, bf16[2048,342]{0,1:T(8,128)(2,1)} %fusion.55), dimensions={1} | concatenate | bytes 12591104 | tf_op jit(solution)/shard_map/concatenate | solution.py:262
  1121.9 77.5 %reduce-scatter.3.cloned.1.call-done = bf16[1024,1537]{0,1:T(8,128)(2,1)} async-done(((bf16[2048,1537]{0,1:T(8,128)(2,1)}), bf16[1024,1537]{0,1:T(8,128)(2,1)}) %reduce-scatter.3.cloned.1.call-update) | async-done | bytes 3147792 | tf_op jit(solution)/shard_map/reduce_scatter | solution.py:263
  1199.3 5.3 copy.124
  1204.6 6.5 all-to-all-start.8
  1211.2 16.7 %fusion.68 = bf16[128,2048]{1,0:T(8,128)(2,1)} fusion(bf16[128,5461]{0,1:T(8,128)(2,1)} %get-tuple-element.568, bf16[2048,24579]{1,0:T(8,128)(2,1)} %all-gather.6.cloned.1.call-done, f32[128,2048]{1,0:T(8,128)} %copy-done.6, f32[2048]{0:T(1024)S(1)} %copy-done.23, f32[2048]{0:T(1024)S(1)} %get-tuple-element.502, f32[128]{0:T(128)S(1)} %fusion.101, ...), kind=kOutput, calls=%fused_computation.91 | convolution fusion | flops 2864971776 | bytes 25533440 | tf_op jit(solution)/shard_map/dot_general | solution.py:159
  1227.9 15.7 %fusion.89 = (f32[2048]{0:T(1024)}, f32[128]{0:T(128)}, f32[2048]{0:T(1024)}, f32[128,2048]{1,0:T(8,128)}) fusion(bf16[128,2048]{1,0:T(8,128)(2,1)} %param.13, f32[128]{0:T(128)S(1)} %copy-done.27, f32[128]{0:T(128)S(1)} %copy-done.25, f32[2048]{0:T(1024)S(1)} %copy-done.21, bf16[128,6144]{0,1:T(8,128)(2,1)} %bitcast.261, ...), kind=kOutput, calls=%fused_computation.113 | convolution fusion | flops 3224367104 | bytes 29386752 | tf_op jit(solution)/shard_map/dot_general | solution.py:159
  1249.2 37.0 %all-to-all-done.8 = bf16[16,64,1537]{2,1,0:T(8,128)(2,1)S(1)} async-done(((bf16[16,64,1537]{2,1,0:T(8,128)(2,1)}), bf16[16,64,1537]{2,1,0:T(8,128)(2,1)S(1)}, u32[]{:S(2)}, u32[]{:S(2)}) %all-to-all-start.8) | async-done | bytes 3147808 | tf_op jit(solution)/shard_map/all_to_all | solution.py:266
  1295.7 2.8 reshape.515
  1298.5 3.6 copy.128
  1302.1 2.8 reshape.516
  1304.9 61.8 %reduce-scatter.5.cloned.1.call-done = f32[64,4]{1,0:T(8,128)} async-done(((f32[2048,4]{1,0:T(8,128)}), f32[64,4]{1,0:T(8,128)}) %reduce-scatter.5.cloned.1.call-update) | async-done | bytes 1040 | tf_op jit(solution)/shard_map/reduce_scatter | solution.py:279
  1366.7 7.1 concatenate.35
  1373.8 19.4 %multiply_add_fusion = (f32[64,24579]{1,0:T(8,128)}, f32[64,24579]{1,0:T(8,128)}, f32[64,24579]{1,0:T(8,128)}, f32[64,24579]{1,0:T(8,128)}) fusion(f32[64,24579]{1,0:T(8,128)} %param.18, f32[64,24579]{1,0:T(8,128)} %param.15, f32[24579]{0:T(1024)S(1)} %get-tuple-element.600, f32[24579]{0:T(1024)} %get-tuple-element.601, f32[64,24579]{1,0:T(8,128)} %concatenate.35, ...), kind=kLoop, calls=%fused_computation.67 | loop fusion | flops 28315008 | bytes 56826648 | tf_op jit(solution)/shard_map/add | solution.py:293
  (273 shorter events, 88.5 us)
Async XLA Ops:
  7.2 5.8 copy-start.7
  7.2 524.3 %all-gather.6.cloned.1.call-start = ((), (), s32[]{:S(2)}) async-start(), calls=%async_computation.11 | async-start | bytes 104349696 | tf_op jit(solution)/shard_map/all_gather | solution.py:180
  12.1 1041.9 %all-gather.14.cloned.1.call-start = ((), (), s32[]{:S(2)}) async-start(), calls=%async_computation.15 | async-start | bytes 8912896 | tf_op jit(solution)/shard_map/all_gather | solution.py:259
  12.8 523.3 %copy-start.29 = (s32[1,4]{1,0:T(1,128)S(1)}, s32[1,4]{1,0:T(1,128)}, u32[]{:S(2)}) copy-start(s32[1,4]{1,0:T(1,128)} %param.19) | copy-start | bytes 52
  12.9 523.5 %copy-start.30 = (s32[1,4]{1,0:T(1,128)S(1)}, s32[1,4]{1,0:T(1,128)}, u32[]{:S(2)}) copy-start(s32[1,4]{1,0:T(1,128)} %param.21) | copy-start | bytes 52
  12.9 523.5 %copy-start.28 = (s32[1,4]{1,0:T(1,128)S(1)}, s32[1,4]{1,0:T(1,128)}, u32[]{:S(2)}) copy-start(s32[1,4]{1,0:T(1,128)} %param.20) | copy-start | bytes 52
  12.9 1053.8 %all-gather.8.cloned.1.call-start = ((), (), s32[]{:S(2)}) async-start(), calls=%async_computation.12 | async-start | bytes 8912896 | tf_op jit(solution)/shard_map/all_gather | solution.py:256
  13.1 665.2 %copy-start.24 = (f32[128]{0:T(128)}, f32[128]{0:T(128)S(1)}, u32[]{:S(2)}) copy-start(f32[128]{0:T(128)S(1)} %broadcast_multiply_fusion.2) | copy-start | bytes 1540
  13.4 522.9 %copy-start.31 = (f32[128]{0:T(128)}, f32[128]{0:T(128)S(1)}, u32[]{:S(2)}) copy-start(f32[128]{0:T(128)S(1)} %fusion.90) | copy-start | bytes 1540
  13.4 664.9 %copy-start.26 = (f32[128]{0:T(128)}, f32[128]{0:T(128)S(1)}, u32[]{:S(2)}) copy-start(f32[128]{0:T(128)S(1)} %fusion.100) | copy-start | bytes 1540
  534.9 143.4 %copy-start.20 = (f32[2048]{0:T(1024)}, f32[2048]{0:T(1024)S(1)}, u32[]{:S(2)}) copy-start(f32[2048]{0:T(1024)S(1)} %get-tuple-element.505) | copy-start | bytes 24580
  534.9 148.9 %copy-start.22 = (f32[2048]{0:T(1024)}, f32[2048]{0:T(1024)S(1)}, u32[]{:S(2)}) copy-start(f32[2048]{0:T(1024)S(1)} %get-tuple-element.503) | copy-start | bytes 24580
  537.6 12.3 copy-start.16
  552.7 71.7 %all-to-all-start = ((bf16[128,3,16,128]{3,0,1,2:T(8,128)(2,1)}), bf16[128,3,16,128]{3,0,1,2:T(8,128)(2,1)S(1)}, u32[]{:S(2)}, u32[]{:S(2)}) async-start(bf16[128,3,16,128]{3,0,1,2:T(8,128)(2,1)} %copy.109), calls=%async_computation | async-start | bytes 3145728 | tf_op jit(solution)/shard_map/all_to_all | solution.py:198
  558.7 516.5 %all-gather.10.cloned.1.call-start = ((), (), s32[]{:S(2)}) async-start(), calls=%async_computation.13 | async-start | bytes 8912896 | tf_op jit(solution)/shard_map/all_gather | solution.py:257
  646.0 37.5 %copy-start.11 = (bf16[2048,1,128]{2,0,1:T(8,128)(2,1)}, bf16[2048,1,128]{2,0,1:T(8,128)(2,1)S(1)}, u32[]{:S(2)}) copy-start(bf16[2048,1,128]{2,0,1:T(8,128)(2,1)S(1)} %get-tuple-element.875) | copy-start | bytes 1572868
  683.5 83.5 %copy-start.6 = (f32[128,2048]{1,0:T(8,128)}, f32[128,2048]{1,0:T(8,128)S(1)}, u32[]{:S(2)}) copy-start(f32[128,2048]{1,0:T(8,128)S(1)} %get-tuple-element.595) | copy-start | bytes 3145732
  684.0 25.0 %copy-start.13 = (bf16[128,2048]{1,0:T(8,128)(2,1)}, bf16[128,2048]{1,0:T(8,128)(2,1)S(1)}, u32[]{:S(2)}) copy-start(bf16[128,2048]{1,0:T(8,128)(2,1)S(1)} %fusion.93) | copy-start | bytes 1572868
  684.1 25.0 %copy-start.18 = (bf16[128,2048]{1,0:T(8,128)(2,1)S(1)}, bf16[128,2048]{1,0:T(8,128)(2,1)}, u32[]{:S(2)}) copy-start(bf16[128,2048]{1,0:T(8,128)(2,1)} %param.14) | copy-start | bytes 1572868
  742.9 24.0 %copy-start.5 = (bf16[128,10922]{0,1:T(8,128)(2,1)}, bf16[128,10922]{0,1:T(8,128)(2,1)S(1)}, u32[]{:S(2)}) copy-start(bf16[128,10922]{0,1:T(8,128)(2,1)S(1)} %add_convert_fusion) | copy-start | bytes 8388100
  768.6 6.7 copy-start.10
  776.2 21.8 %all-to-all-start.2 = ((bf16[128,16,128]{2,0,1:T(8,128)(2,1)}), bf16[128,16,128]{2,0,1:T(8,128)(2,1)S(1)}, u32[]{:S(2)}, u32[]{:S(2)}) async-start(bf16[128,16,128]{2,0,1:T(8,128)(2,1)} %bitcast.211), calls=%async_computation.2 | async-start | bytes 1048576 | tf_op jit(solution)/shard_map/all_to_all | solution.py:225
  780.8 300.7 %all-gather.12.cloned.1.call-start = ((), (), s32[]{:S(2)}) async-start(), calls=%async_computation.14 | async-start | bytes 8912896 | tf_op jit(solution)/shard_map/all_gather | solution.py:258
  798.0 88.1 %all-to-all-start.7 = ((bf16[128,16,342]{0,2,1:T(8,128)(2,1)}), bf16[128,16,342]{0,2,1:T(8,128)(2,1)}, u32[]{:S(2)}, u32[]{:S(2)}) async-start(bf16[128,16,342]{0,2,1:T(8,128)(2,1)} %all_to_all.140), calls=%async_computation.7 | async-start | bytes 2818048 | tf_op jit(solution)/shard_map/all_to_all | solution.py:249
  804.0 7.9 copy-start.8
  806.9 5.1 copy-start
  811.9 2.0 copy-start.1
  812.0 2.0 copy-start.14
  815.5 2.5 copy-start.2
  818.1 2.4 copy-start.9
  820.5 7.6 copy-start.8
  823.3 4.8 copy-start
  828.1 2.0 copy-start.1
  828.1 2.0 copy-start.14
  831.7 2.9 copy-start.2
  834.6 2.8 copy-start.9
  837.4 7.6 copy-start.8
  840.2 4.7 copy-start
  845.0 2.0 copy-start.1
  845.0 2.0 copy-start.14
  848.6 2.9 copy-start.2
  851.5 2.8 copy-start.9
  854.3 7.6 copy-start.8
  857.1 4.8 copy-start
  861.8 2.0 copy-start.1
  865.4 2.9 copy-start.2
  868.3 2.8 copy-start.9
  886.1 52.5 %all-to-all-start.3 = ((bf16[2048,3,1,128]{3,1,2,0:T(4,128)(2,1)}), bf16[2048,3,1,128]{3,1,2,0:T(4,128)(2,1)}, u32[]{:S(2)}, u32[]{:S(2)}) async-start(bf16[2048,3,1,128]{3,1,2,0:T(4,128)(2,1)} %copy.116), calls=%async_computation.3 | async-start | bytes 4194304 | tf_op jit(solution)/shard_map/all_to_all | solution.py:229
  938.6 67.2 %all-to-all-start.6 = ((bf16[128,16,683]{0,2,1:T(8,128)(2,1)}), bf16[128,16,683]{0,2,1:T(8,128)(2,1)S(1)}, u32[]{:S(2)}, u32[]{:S(2)}) async-start(bf16[128,16,683]{0,2,1:T(8,128)(2,1)} %all_to_all.136), calls=%async_computation.6 | async-start | bytes 5636096 | tf_op jit(solution)/shard_map/all_to_all | solution.py:246
  944.9 2.1 copy-start.17
  944.9 2.1 copy-start.19
  1005.7 42.5 %all-to-all-start.4 = ((bf16[128,16,384]{0,2,1:T(8,128)(2,1)}), bf16[128,16,384]{0,2,1:T(8,128)(2,1)}, u32[]{:S(2)}, u32[]{:S(2)}) async-start(bf16[128,16,384]{0,2,1:T(8,128)(2,1)} %bitcast.260), calls=%async_computation.4 | async-start | bytes 3145728 | tf_op jit(solution)/shard_map/all_to_all | solution.py:244
  1048.2 26.9 %all-to-all-start.5 = ((bf16[128,16,128]{2,0,1:T(8,128)(2,1)}), bf16[128,16,128]{2,0,1:T(8,128)(2,1)}, u32[]{:S(2)}, u32[]{:S(2)}) async-start(bf16[128,16,128]{2,0,1:T(8,128)(2,1)} %copy_bitcast_fusion.5), calls=%async_computation.5 | async-start | bytes 1048576 | tf_op jit(solution)/shard_map/all_to_all | solution.py:245
  1053.9 145.4 %reduce-scatter.3.cloned.1.call-start = ((), (), s32[]{:S(2)}) async-start(), calls=%async_computation.16 | async-start | bytes 9486336 | tf_op jit(solution)/shard_map/reduce_scatter | solution.py:263
  1204.6 6.6 copy-start.23
  1204.6 81.5 %all-to-all-start.8 = ((bf16[16,64,1537]{2,1,0:T(8,128)(2,1)}), bf16[16,64,1537]{2,1,0:T(8,128)(2,1)S(1)}, u32[]{:S(2)}, u32[]{:S(2)}) async-start(bf16[16,64,1537]{2,1,0:T(8,128)(2,1)} %bitcast.252), calls=%async_computation.9 | async-start | bytes 6815744 | tf_op jit(solution)/shard_map/all_to_all | solution.py:266
  1211.1 16.8 %copy-start.21 = (f32[2048]{0:T(1024)S(1)}, f32[2048]{0:T(1024)}, u32[]{:S(2)}) copy-start(f32[2048]{0:T(1024)} %copy-done.20) | copy-start | bytes 24580
  1211.1 16.8 %copy-start.25 = (f32[128]{0:T(128)S(1)}, f32[128]{0:T(128)}, u32[]{:S(2)}) copy-start(f32[128]{0:T(128)} %copy-done.24) | copy-start | bytes 1540
  1211.1 16.8 %copy-start.27 = (f32[128]{0:T(128)S(1)}, f32[128]{0:T(128)}, u32[]{:S(2)}) copy-start(f32[128]{0:T(128)} %copy-done.26) | copy-start | bytes 1540
  1211.1 155.6 %reduce-scatter.5.cloned.1.call-start = ((), (), s32[]{:S(2)}) async-start(), calls=%async_computation.17 | async-start | bytes 1081344 | tf_op jit(solution)/shard_map/reduce_scatter | solution.py:279
  1286.8 2.9 copy-start.3
  1291.4 2.5 slice-start
  1298.4 68.3 %copy-start.4 = (f32[64,10928]{1,0:T(8,128)S(1)}, f32[64,10928]{1,0:T(8,128)}, u32[]{:S(2)}) copy-start(f32[64,10928]{1,0:T(8,128)} %reshape.515) | copy-start | bytes 8392708
  1298.4 68.3 %copy-start.12 = (f32[64,2048]{1,0:T(8,128)S(1)}, f32[64,2048]{1,0:T(8,128)}, u32[]{:S(2)}) copy-start(f32[64,2048]{1,0:T(8,128)} %copy_bitcast_fusion.4) | copy-start | bytes 1572868
  (5 other events, 5.2 us)
Sparse Core Ops, SparseCore 0:
  12.2 519.2 all-gather.5
  533.6 93.2 all-gather.13
  629.7 82.4 all-gather.7
  714.1 79.0 all-gather.9
  795.3 100.1 all-gather.11
  1121.3 77.9 reduce-scatter.2
  1245.9 120.7 reduce-scatter.4
where the time goes:
time: 1430 us; the launch traced here: 1400 us
  waiting for transfers between devices  900 us (63%)
  matrix products  233 us (16%)
  local copies, waits for them, and re-layouts  119 us (8%)
  other arithmetic  57.7 us (4%)
  starting transfers between devices  48.2 us (3%)
  blocking collectives  24.4 us (2%)
  between operations  15.3 us (1%)
    all_gather x1, waiting for transfers between devices, on_device(): lax.all_gather(master.astype(jnp.bfloat16), ('batch', 'seq'), axis=0, til...  518 us
    reduce_scatter x1, waiting for transfers between devices, on_device(): lax.psum_scatter(partial_sum.astype(jnp.bfloat16), 'batch', scatter_dimen...  77.5 us
    all_to_all x1, waiting for transfers between devices, on_device(): lax.all_to_all(rotated, 'seq', split_axis=2, concat_axis=0, tiled=True)  65.4 us
    dot_general x4, matrix products, contract_last(): lax.dot_general(left, right, (((1,), (1,)), ((), ())), preferred_element_...  63.1 us
    reduce_scatter x1, waiting for transfers between devices, on_device(): lax.psum_scatter(vector_grad, ('batch', 'seq'), scatter_dimension=0, tile...  61.8 us
    all_to_all x1, waiting for transfers between devices, on_device(): lax.all_to_all(pad_columns(gate_up_grad, seq_count), 'seq', split_axis=1,...  53.4 us
    all_to_all x1, waiting for transfers between devices, on_device(): lax.all_to_all(head_qkv_grad, 'seq', split_axis=0, concat_axis=2, tiled=T...  41.4 us
    all_to_all x1, waiting for transfers between devices, on_device(): lax.all_to_all(batch_rows.astype(jnp.bfloat16), 'seq', split_axis=0, conc...  37 us
  transfers between devices with their start and end apart: 15, of which 9 were waited for; matrix products, arithmetic and copies ran while one was open for 23% of the time, Pallas kernels for 0%

commit v1 on v0

v1 whole, which is shorter than its diff:
```python
import functools
import math

import jax
import jax.numpy as jnp
from jax import lax
from jax.experimental import pallas as pl
from jax.experimental.pallas import tpu as pltpu
from jax.sharding import PartitionSpec as P

D = 2048
H = 16
HD = 128
FF = 5461
STEP = 10

DEEP_ALPHA = math.sqrt(48.0)
ROPE_BASE = 10000.0
NEG_LARGE = -1e30
LN_EPS = 1e-05
BETA_ONE = 0.9
BETA_TWO = 0.95
ADAM_EPS = 1e-08
LR_MAT = 0.01
LR_VEC = 0.2
DECAY_MAT = 0.1
EMA_RATE = 0.9

BF = jnp.bfloat16
F32 = jnp.float32
MESH = pl.DeviceIdType.MESH
ROWS = 256
LANES = 128
SUBS = 4
VMEM_BIG = 56 * 1024 * 1024


def nt(left, right):
    return lax.dot_general(left, right, (((1,), (1,)), ((), ())), preferred_element_type=F32)


def tn(left, right):
    return lax.dot_general(left, right, (((0,), (0,)), ((), ())), preferred_element_type=F32)


def nn(left, right):
    return jnp.dot(left, right, preferred_element_type=F32)


def vmem(limit=VMEM_BIG, **more):
    return pltpu.CompilerParams(vmem_limit_bytes=limit, **more)


class Ring:
    def __init__(self, count):
        self.pairs = count // 2
        self.batch, self.me = lax.axis_index("batch"), lax.axis_index("seq")
        self.core = lax.rem(self.me, 2)
        y, z = lax.rem(self.me // 2, 2), self.me // 4
        self.place = jnp.where(y == 0, z, self.pairs - 1 - z)
        self.sibling = self.me + 1 - 2 * self.core

    def at(self, steps, core=None):
        place = lax.rem(self.place + (1 - 2 * self.core) * steps + 4 * self.pairs, self.pairs)
        half = self.pairs // 2
        pair = jnp.where(place < half, 2 * place, 2 * (self.pairs - 1 - place) + 1)
        return pair * 2 + (self.core if core is None else core)

    def greet(self):
        barrier = pltpu.get_barrier_semaphore()
        for device in (self.at(-1), self.sibling):
            pl.semaphore_signal(barrier, inc=1, device_id=(self.batch, device), device_id_type=MESH)
        pl.semaphore_wait(barrier, 2)

    def greet_all(self, count):
        barrier = pltpu.get_barrier_semaphore()
        groups = lax.axis_size("batch")
        for step in range(1, count):
            device = lax.rem(self.me + step, count)
            pl.semaphore_signal(barrier, inc=1, device_id=(self.batch, device), device_id_type=MESH)
        for shift in range(1, groups):
            group = lax.rem(self.batch + shift, groups)
            pl.semaphore_signal(barrier, inc=1, device_id=(group, self.me), device_id_type=MESH)
        pl.semaphore_wait(barrier, count + groups - 2)

    def copy(self, src, dst, send, recv, device):
        return pltpu.make_async_remote_copy(
            src_ref=src,
            dst_ref=dst,
            send_sem=send,
            recv_sem=recv,
            device_id=(self.batch, device),
            device_id_type=MESH,
        )


class Columns:
    def __init__(self, ring, count, src, out, sems):
        self.ring, self.count, self.src, self.out = ring, count, src, out
        self.send, self.recv, self.on_send, self.on_recv, self.own = sems
        self.groups = lax.axis_size("batch")

    def piece(self, device):
        return self.src.at[device] if self.src.shape[0] == self.count else self.src.at[0]

    def group(self, shift):
        return lax.rem(self.ring.batch + shift + self.groups, self.groups)

    def start(self):
        ring, sends = self.ring, []
        self.mine = pltpu.make_async_copy(
            self.piece(ring.me), self.out.at[ring.batch, ring.me], self.own
        )
        self.mine.start()
        for step in range(1, self.count):
            device = lax.rem(ring.me + step, self.count)
            go = ring.copy(
                self.piece(device),
                self.out.at[ring.batch, ring.me],
                self.send.at[step],
                self.recv.at[step],
                device,
            )
            go.start()
            sends.append(go)
        self.sends = sends + self.forward(0)

    def forward(self, step):
        ring, sends = self.ring, []
        device = lax.rem(ring.me - step + self.count, self.count)
        here = self.out.at[ring.batch, device]
        for shift in range(1, self.groups):
            go = pltpu.make_async_remote_copy(
                src_ref=self.piece(ring.me) if step == 0 else here,
                dst_ref=here,
                send_sem=self.on_send.at[shift - 1, step],
                recv_sem=self.on_recv.at[shift - 1, step],
                device_id=(self.group(shift), ring.me),
                device_id_type=MESH,
            )
            go.start()
            sends.append(go)
        return sends

    def pass_on(self, step):
        ring = self.ring
        device = lax.rem(ring.me - step + self.count, self.count)
        here = self.out.at[ring.batch, device]
        ring.copy(here, here, self.send.at[step], self.recv.at[step], device).wait_recv()
        self.sends += self.forward(step)

    def finish(self):
        ring = self.ring
        for step in range(self.count):
            device = lax.rem(ring.me - step + self.count, self.count)
            for shift in range(1, self.groups):
                here = self.out.at[self.group(-shift), device]
                pltpu.make_async_remote_copy(
                    src_ref=here,
                    dst_ref=here,
                    send_sem=self.on_send.at[shift - 1, step],
                    recv_sem=self.on_recv.at[shift - 1, step],
                    device_id=(self.group(shift), ring.me),
                    device_id_type=MESH,
                ).wait_recv()
        for go in self.sends:
            go.wait_send()
        self.mine.wait()


def gather_kernel(count, extra, x_ref, *refs):
    parts, (o_ref, *outs), sems = refs[:extra], refs[extra : 2 * extra + 1], refs[2 * extra + 1 :]
    ring_s, ring_r, sib_s, sib_r, own_sem = sems[:5]
    ring = Ring(count)
    piece = x_ref.shape[0] // SUBS
    own = pltpu.make_async_copy(x_ref, o_ref.at[ring.me], own_sem)
    own.start()
    columns = [
        Columns(ring, count, parts[i], outs[i], sems[5 + 5 * i : 10 + 5 * i]) for i in range(extra)
    ]
    ring.greet_all(count)
    following, sends = ring.at(1), []
    ahead = 1
    for step in range(ring.pairs):
        block = ring.at(-step)
        for sub in range(SUBS):
            rows = pl.ds(sub * piece, piece)
            dst = o_ref.at[block].at[rows]
            src = x_ref.at[rows] if step == 0 else dst
            if step > 0:
                ring.copy(
                    dst, dst, ring_s.at[step - 1, sub], ring_r.at[step - 1, sub], following
                ).wait_recv()
            if step < ring.pairs - 1:
                go = ring.copy(src, dst, ring_s.at[step, sub], ring_r.at[step, sub], following)
                go.start()
                sends.append(go)
            go = ring.copy(src, dst, sib_s.at[step, sub], sib_r.at[step, sub], ring.sibling)
            go.start()
            sends.append(go)
        if step == 0:
            for column in columns:
                column.start()
        elif 2 * step >= ring.pairs:
            upto = count if step == ring.pairs - 1 else count * (2 * step - ring.pairs + 1) // ring.pairs
            for passed in range(ahead, max(ahead, upto)):
                for column in columns:
                    column.pass_on(passed)
            ahead = max(ahead, upto)
    for step in range(ring.pairs):
        block = ring.at(step, 1 - ring.core)
        for sub in range(SUBS):
            dst = o_ref.at[block].at[pl.ds(sub * piece, piece)]
            ring.copy(
                dst, dst, sib_s.at[step, sub], sib_r.at[step, sub], ring.sibling
            ).wait_recv()
    for go in sends:
        go.wait_send()
    own.wait()
    for column in columns:
        column.finish()


def ring_gather(values, blocks, count, ident):
    pairs, groups = count // 2, lax.axis_size("batch")
    anywhere = pl.BlockSpec(memory_space=pl.ANY)
    column_sems = [
        pltpu.SemaphoreType.DMA((count,)),
        pltpu.SemaphoreType.DMA((count,)),
        pltpu.SemaphoreType.DMA((groups, count)),
        pltpu.SemaphoreType.DMA((groups, count)),
        pltpu.SemaphoreType.DMA,
    ]
    return pl.pallas_call(
        functools.partial(gather_kernel, count, len(blocks)),
        out_shape=[jax.ShapeDtypeStruct((count,) + values.shape, values.dtype)]
        + [jax.ShapeDtypeStruct((groups, count) + b.shape[1:], b.dtype) for b in blocks],
        in_specs=[anywhere] * (1 + len(blocks)),
        out_specs=[anywhere] * (1 + len(blocks)),
        scratch_shapes=[pltpu.SemaphoreType.DMA((pairs, SUBS)) for _ in range(4)]
        + [pltpu.SemaphoreType.DMA]
        + column_sems * len(blocks),
        compiler_params=pltpu.CompilerParams(collective_id=ident, has_side_effects=True),
        cost_estimate=pl.CostEstimate(flops=0, bytes_accessed=150_000_000, transcendentals=0),
        name=f"ring_gather_{ident}",
    )(values, *blocks)


def scatter_kernel(count, x_ref, o_ref, own, sib, got, ring_s, ring_r, sib_s, sib_r, load):
    ring = Ring(count)
    piece = x_ref.shape[1] // SUBS
    pairs = ring.pairs
    loads = []
    for step in range(pairs):
        go = pltpu.make_async_copy(x_ref.at[ring.at(-1 - step)], own.at[step], load.at[step])
        go.start()
        loads.append(go)
    ring.greet()
    following, sends = ring.at(1), []
    for step in range(pairs):
        block = ring.at(1 + step, 1 - ring.core)
        for sub in range(SUBS):
            rows = pl.ds(sub * piece, piece)
            go = ring.copy(
                x_ref.at[block].at[rows],
                sib.at[step].at[rows],
                sib_s.at[step, sub],
                sib_r.at[step, sub],
                ring.sibling,
            )
            go.start()
            sends.append(go)
    for step in range(pairs):
        loads[step].wait()
        for sub in range(SUBS):
            rows = pl.ds(sub * piece, piece)
            here = own.at[step].at[rows]
            other = sib.at[step].at[rows]
            ring.copy(
                other, other, sib_s.at[step, sub], sib_r.at[step, sub], ring.sibling
            ).wait_recv()
            total = here[...].astype(F32) + other[...].astype(F32)
            if step > 0:
                came = got.at[step - 1].at[rows]
                ring.copy(
                    came, came, ring_s.at[step - 1, sub], ring_r.at[step - 1, sub], following
                ).wait_recv()
                total = total + came[...].astype(F32)
            if step == pairs - 1:
                o_ref[rows, :] = total
            else:
                here[...] = total.astype(BF)
                go = ring.copy(
                    here,
                    got.at[step].at[rows],
                    ring_s.at[step, sub],
                    ring_r.at[step, sub],
                    following,
                )
                go.start()
                sends.append(go)
    for go in sends:
        go.wait_send()


def ring_scatter(terms, count, ident):
    pairs = count // 2
    shape = terms.shape[1:]
    return pl.pallas_call(
        functools.partial(scatter_kernel, count),
        out_shape=jax.ShapeDtypeStruct(shape, F32),
        in_specs=[pl.BlockSpec(memory_space=pl.ANY)],
        out_specs=pl.BlockSpec(memory_space=pltpu.VMEM),
        scratch_shapes=[pltpu.VMEM((pairs,) + shape, BF) for _ in range(3)]
        + [pltpu.SemaphoreType.DMA((pairs, SUBS)) for _ in range(4)]
        + [pltpu.SemaphoreType.DMA((pairs,))],
        compiler_params=vmem(collective_id=ident, has_side_effects=True),
        cost_estimate=pl.CostEstimate(flops=0, bytes_accessed=150_000_000, transcendentals=0),
        name=f"ring_scatter_{ident}",
    )(terms)


def norm_parts(values):
    centre = values - jnp.mean(values, axis=-1, keepdims=True)
    inverse = lax.rsqrt(jnp.mean(centre * centre, axis=-1, keepdims=True) + LN_EPS)
    return centre * inverse, inverse


def qkv_kernel(x_ref, w_ref, vec_ref, cos_ref, sin_ref, a_ref, q_ref, k_ref, v_ref):
    normal, _ = norm_parts(x_ref[...].astype(F32))
    low = (normal * vec_ref[0:1, :] + vec_ref[1:2, :]).astype(BF)
    a_ref[...] = low
    projected = nn(low, w_ref[...])
    for index, ref in enumerate((q_ref, k_ref)):
        part = projected[:, index * HD : (index + 1) * HD]
        turned = part * cos_ref[...] + pltpu.roll(part, HD // 2, 1) * sin_ref[...]
        ref[...] = turned.astype(BF)
    v_ref[...] = projected[:, 2 * HD :].astype(BF)


def norm_and_project(states, w_qkv, vectors, cosine, sine):
    tokens = states.shape[0]
    whole = lambda shape: pl.BlockSpec(shape, lambda i: (0, 0))
    rows = lambda width: pl.BlockSpec((ROWS, width), lambda i: (i, 0))
    return pl.pallas_call(
        qkv_kernel,
        grid=(tokens // ROWS,),
        in_specs=[rows(D), whole((D, 3 * HD)), whole(vectors.shape), rows(HD), rows(HD)],
        out_specs=[rows(D), rows(HD), rows(HD), rows(HD)],
        out_shape=[jax.ShapeDtypeStruct((tokens, D), BF)]
        + [jax.ShapeDtypeStruct((tokens, HD), BF) for _ in range(3)],
        compiler_params=vmem(),
        cost_estimate=pl.CostEstimate(
            flops=2 * tokens * D * 3 * HD, bytes_accessed=24_000_000, transcendentals=0
        ),
        name="norm_and_project",
    )(states, w_qkv, vectors, cosine, sine)


def seen(block, first_ref, last_ref, keys):
    query = block * ROWS + lax.broadcasted_iota(jnp.int32, (ROWS, ROWS), 0)
    return (query >= first_ref[keys]) & (query < last_ref[keys])


def attend_kernel(
    low_ref, high_ref, q_ref, k_ref, v_ref, first_ref, last_ref, o_ref, full_ref, log_ref, held
):
    block = pl.program_id(0)
    query = q_ref[...]
    scale = HD ** (-0.5)

    def score(keys, top):
        scores = nt(query, k_ref[keys]) * scale
        scores = jnp.where(seen(block, first_ref, last_ref, keys), scores, NEG_LARGE)
        held[keys] = scores
        return jnp.maximum(top, jnp.max(scores, axis=-1, keepdims=True))

    def add(keys, carry):
        total, out = carry
        weight = jnp.exp(held[keys] - top)
        total = total + jnp.sum(weight, axis=-1, keepdims=True)
        return total, out + nn(weight.astype(BF), v_ref[keys])

    low, high = low_ref[block], high_ref[block]
    top = lax.fori_loop(low, high, score, jnp.full((ROWS, 1), NEG_LARGE, F32))
    total, out = lax.fori_loop(
        low, high, add, (jnp.zeros((ROWS, 1), F32), jnp.zeros((ROWS, HD), F32))
    )
    out = out / total
    o_ref[...] = out.astype(BF)
    full_ref[...] = out
    log_ref[...] = jnp.broadcast_to(top + jnp.log(total), (ROWS, LANES))


def attend(query, key, value, spans):
    tokens = query.shape[0]
    blocks = tokens // ROWS
    first, last, low, high = spans
    rows = pl.BlockSpec((ROWS, HD), lambda i, *_: (i, 0))
    whole = lambda shape: pl.BlockSpec(shape, lambda i, *_: (0,) * len(shape))
    cut = lambda values: values.reshape(blocks, ROWS, HD)
    return pl.pallas_call(
        attend_kernel,
        grid_spec=pltpu.PrefetchScalarGridSpec(
            num_scalar_prefetch=2,
            grid=(blocks,),
            in_specs=[rows]
            + [whole((blocks, ROWS, HD)) for _ in range(2)]
            + [whole((blocks, 1, ROWS)) for _ in range(2)],
            out_specs=[rows, rows, rows],
            scratch_shapes=[pltpu.VMEM((blocks, ROWS, ROWS), F32)],
        ),
        out_shape=[
            jax.ShapeDtypeStruct((tokens, HD), BF),
            jax.ShapeDtypeStruct((tokens, HD), F32),
            jax.ShapeDtypeStruct((tokens, LANES), F32),
        ],
        compiler_params=vmem(),
        cost_estimate=pl.CostEstimate(
            flops=2 * tokens * tokens * HD, bytes_accessed=4_000_000, transcendentals=0
        ),
        name="attend",
    )(low, high, query, cut(key), cut(value), first, last)


def attend_back_kernel(
    low_ref,
    high_ref,
    q_ref,
    g_ref,
    full_ref,
    log_ref,
    k_ref,
    v_ref,
    first_ref,
    last_ref,
    cos_ref,
    sin_ref,
    o_ref,
    dk_ref,
    dv_ref,
):
    block = pl.program_id(0)
    blocks = pl.num_programs(0)
    scale = HD ** (-0.5)

    @pl.when(block == 0)
    def _():
        dk_ref[...] = jnp.zeros_like(dk_ref)
        dv_ref[...] = jnp.zeros_like(dv_ref)

    query, grad = q_ref[...], g_ref[...]
    inner = jnp.sum(grad.astype(F32) * full_ref[...], axis=-1, keepdims=True)
    log = log_ref[:, 0:1]

    def one(keys, total):
        scores = nt(query, k_ref[keys]) * scale
        scores = jnp.where(seen(block, first_ref, last_ref, keys), scores, NEG_LARGE)
        weight = jnp.exp(scores - log)
        slope = (weight * (nt(grad, v_ref[keys]) - inner)).astype(BF)
        dv_ref[keys] += tn(weight.astype(BF), grad)
        dk_ref[keys] += tn(slope, query)
        return total + nn(slope, k_ref[keys])

    total = lax.fori_loop(
        low_ref[block], high_ref[block], one, jnp.zeros((ROWS, HD), F32)
    )

    def turn_back(values, cosine, sine):
        values = (values * scale).astype(BF).astype(F32)
        return (values * cosine - pltpu.roll(values, HD // 2, 1) * sine).astype(BF)

    rows = pl.ds(pl.multiple_of(block * ROWS, ROWS), ROWS)
    o_ref[rows, 0:HD] = turn_back(total, cos_ref[rows, :], sin_ref[rows, :])

    @pl.when(block == blocks - 1)
    def _():
        for part in range(dk_ref.shape[0]):
            there = pl.ds(part * ROWS, ROWS)
            o_ref[there, HD : 2 * HD] = turn_back(
                dk_ref[part], cos_ref[there, :], sin_ref[there, :]
            )
            o_ref[there, 2 * HD :] = dv_ref[part].astype(BF)


def attend_back(query, key, value, grad, full, log, spans, cosine, sine):
    tokens = query.shape[0]
    blocks = tokens // ROWS
    first, last, low, high = spans
    rows = pl.BlockSpec((ROWS, HD), lambda i, *_: (i, 0))
    whole = lambda shape: pl.BlockSpec(shape, lambda i, *_: (0,) * len(shape))
    cut = lambda values: values.reshape(blocks, ROWS, HD)
    return pl.pallas_call(
        attend_back_kernel,
        grid_spec=pltpu.PrefetchScalarGridSpec(
            num_scalar_prefetch=2,
            grid=(blocks,),
            in_specs=[rows] * 4
            + [whole((blocks, ROWS, HD)) for _ in range(2)]
            + [whole((blocks, 1, ROWS)) for _ in range(2)]
            + [whole((tokens, HD)) for _ in range(2)],
            out_specs=whole((tokens, 3 * HD)),
            scratch_shapes=[pltpu.VMEM((blocks, ROWS, HD), F32) for _ in range(2)],
        ),
        out_shape=jax.ShapeDtypeStruct((tokens, 3 * HD), BF),
        compiler_params=vmem(),
        cost_estimate=pl.CostEstimate(
            flops=5 * tokens * tokens * HD, bytes_accessed=6_000_000, transcendentals=0
        ),
        name="attend_back",
    )(low, high, query, grad, full, log, cut(key), cut(value), first, last, cosine, sine)


def residual_kernel(x_ref, heads_ref, w_ref, vec_ref, b_ref, own_ref):
    tokens = own_ref.shape[0]
    block = pl.program_id(0)
    normal, _ = norm_parts(x_ref[...].astype(F32))
    attended = jnp.concatenate([heads_ref[h] for h in range(heads_ref.shape[0])], axis=1)
    residual = DEEP_ALPHA * (normal * vec_ref[0:1, :] + vec_ref[1:2, :]) + nn(
        attended, w_ref[...]
    )
    second, _ = norm_parts(residual)
    b_ref[...] = (second * vec_ref[2:3, :] + vec_ref[3:4, :]).astype(BF)
    me = lax.axis_index("seq")
    for part in range(ROWS // tokens):

        @pl.when(block * (ROWS // tokens) + part == me)
        def _():
            own_ref[...] = residual[part * tokens : (part + 1) * tokens, :]


def residual_norm(states, heads, w_out, vectors, own_rows):
    tokens = states.shape[0]
    whole = lambda shape: pl.BlockSpec(shape, lambda i: (0,) * len(shape))
    rows = pl.BlockSpec((ROWS, D), lambda i: (i, 0))
    return pl.pallas_call(
        residual_kernel,
        grid=(tokens // ROWS,),
        in_specs=[
            rows,
            pl.BlockSpec((heads.shape[0], ROWS, HD), lambda i: (0, i, 0)),
            whole((D, D)),
            whole(vectors.shape),
        ],
        out_specs=[rows, whole((own_rows, D))],
        out_shape=[
            jax.ShapeDtypeStruct((tokens, D), BF),
            jax.ShapeDtypeStruct((own_rows, D), F32),
        ],
        compiler_params=vmem(),
        cost_estimate=pl.CostEstimate(
            flops=2 * tokens * D * D, bytes_accessed=32_000_000, transcendentals=0
        ),
        name="residual_norm",
    )(states, heads, w_out, vectors)


def feed_kernel(b_ref, cot_ref, w_ref, h_ref, du_ref, out_ref, db_ref):
    span = h_ref.shape[1]
    b, cot = b_ref[...], cot_ref[...]
    gate = nn(b, w_ref[:, :span])
    up = nn(b, w_ref[:, span : 2 * span])
    slope = nn(cot, w_ref[:, 2 * span :])
    coef = math.sqrt(2.0 / math.pi)
    square = gate * gate
    tanh = jnp.tanh(coef * gate * (1.0 + 0.044715 * square))
    half = 0.5 * (1.0 + tanh)
    gelu = gate * half
    gelu_slope = half + 0.5 * gate * (1.0 - tanh * tanh) * (
        coef * (1.0 + 3 * 0.044715 * square)
    )
    hidden = (gelu * up).astype(BF)
    h_ref[...] = hidden
    du = jnp.concatenate([slope * up * gelu_slope, slope * gelu], axis=1).astype(BF)
    du_ref[...] = du
    out_ref[...] = nt(hidden, w_ref[:, 2 * span :]).astype(BF)
    db_ref[...] = nt(du, w_ref[:, : 2 * span]).astype(BF)


def feed_forward(b_low, cot, w_feed):
    tokens = b_low.shape[0]
    span = w_feed.shape[1] // 3
    rows = lambda width: pl.BlockSpec((ROWS, width), lambda i: (i, 0))
    return pl.pallas_call(
        feed_kernel,
        grid=(tokens // ROWS,),
        in_specs=[rows(D), rows(D), pl.BlockSpec(w_feed.shape, lambda i: (0, 0))],
        out_specs=[rows(span), rows(2 * span), rows(D), rows(D)],
        out_shape=[
            jax.ShapeDtypeStruct((tokens, width), BF) for width in (span, 2 * span, D, D)
        ],
        compiler_params=vmem(),
        cost_estimate=pl.CostEstimate(
            flops=12 * tokens * D * span, bytes_accessed=48_000_000, transcendentals=0
        ),
        name="feed_forward",
    )(b_low, cot, w_feed)


def windows(at, span, count):
    total = 4 * D + 3 * FF + 4
    result = []
    for index in range(count):
        width = max(0, min(span, FF - index * span))
        begin = at + index * span
        turn = begin % LANES
        window = -(-(turn + width) // LANES) * LANES if width else 0
        window = min(window, (total - begin + turn) // LANES * LANES)
        result.append((begin - turn, window, turn, width))
    return result


FEED_AT = (4 * D, 4 * D + FF, 4 * D + 2 * FF)


def lay_out_kernel(count, span, m_ref, qkv_ref, out_ref, feed_ref):
    rows = m_ref.shape[0]
    for index in range(count):
        for part in range(3):
            at = part * D + index * HD
            qkv_ref[index, :, part * HD : (part + 1) * HD] = m_ref[:, at : at + HD].astype(BF)
    out_ref[...] = m_ref[:, 3 * D : 4 * D].astype(BF)
    column = lax.broadcasted_iota(jnp.int32, (rows, span), 1)
    for part, at in enumerate(FEED_AT):
        for index, (begin, window, turn, width) in enumerate(windows(at, span, count)):
            if width == 0:
                piece = jnp.zeros((rows, span), F32)
            else:
                piece = m_ref[:, begin : begin + window]
                if window < span:
                    piece = jnp.concatenate(
                        [piece, jnp.zeros((rows, span - window), F32)], axis=1
                    )
                if turn:
                    piece = pltpu.roll(piece, piece.shape[1] - turn, 1)
                piece = piece[:, :span]
                if width < span:
                    piece = jnp.where(column < width, piece, 0.0)
            feed_ref[index, :, part * span : (part + 1) * span] = piece.astype(BF)


def lay_out(master, count, span):
    rows = master.shape[0]
    inside = pl.BlockSpec(memory_space=pltpu.VMEM)
    return pl.pallas_call(
        functools.partial(lay_out_kernel, count, span),
        out_shape=[
            jax.ShapeDtypeStruct((count, rows, 3 * HD), BF),
            jax.ShapeDtypeStruct((rows, D), BF),
            jax.ShapeDtypeStruct((count, rows, 3 * span), BF),
        ],
        in_specs=[inside],
        out_specs=[inside] * 3,
        compiler_params=vmem(),
        cost_estimate=pl.CostEstimate(flops=0, bytes_accessed=10_000_000, transcendentals=0),
        name="lay_out",
    )(master)


STEP_COLS = 3072


def update_kernel(
    count, span, attn_ref, feed_ref, vec_ref, m_ref, f_ref, s_ref, a_ref, nm_ref, nf_ref, ns_ref, na_ref, grad
):
    rows = m_ref.shape[0]
    step = pl.program_id(0)
    total = 4 * D + 3 * FF + 4

    @pl.when(step == 0)
    def _():
        for index in range(count):
            for part in range(4):
                at = part * D + index * HD
                grad[:, at : at + HD] = attn_ref[index, :, part * HD : (part + 1) * HD].astype(F32)
        lane = lax.broadcasted_iota(jnp.int32, (rows, LANES), 1)
        tiles = span // LANES
        last = None
        for part, at in enumerate(FEED_AT):
            turn = at % LANES
            for tile in range(-(-(FF + turn) // LANES)):
                begin = at - turn + tile * LANES
                index, inner = divmod(tile, tiles)
                here = feed_ref[index, :, part * span + inner * LANES : part * span + (inner + 1) * LANES]
                here = here.astype(F32)
                if turn:
                    here = pltpu.roll(here, turn, 1)
                    before = last if tile == 0 else previous
                    value = here if before is None else jnp.where(lane < turn, before, here)
                    previous = here
                else:
                    value = here
                if begin + LANES <= total:
                    grad[:, begin : begin + LANES] = value
                    last = value
        edge = (total - 4) // LANES * LANES
        shift = (total - 4) % LANES
        both = jnp.concatenate([last, jnp.zeros_like(last)], axis=1)
        vec = jnp.concatenate([vec_ref[...], jnp.zeros_like(last)], axis=1)
        vec = pltpu.roll(vec, shift, 1)
        wide = lax.broadcasted_iota(jnp.int32, (rows, 2 * LANES), 1)
        both = jnp.where(wide < shift, both, vec)
        grad[:, edge : edge + 2 * LANES] = both

    begin = pl.multiple_of(step * STEP_COLS, LANES)
    g = grad[:, pl.ds(begin, STEP_COLS)]
    vector = step * STEP_COLS + lax.broadcasted_iota(jnp.int32, (1, STEP_COLS), 1) >= total - 4
    rate = jnp.where(vector, LR_VEC, LR_MAT)
    decay = jnp.where(vector, 0.0, DECAY_MAT)
    new_first = BETA_ONE * f_ref[...] + (1.0 - BETA_ONE) * g
    new_second = BETA_TWO * s_ref[...] + (1.0 - BETA_TWO) * g * g
    nf_ref[...] = new_first
    ns_ref[...] = new_second
    root = jnp.sqrt(new_second * (1.0 / (1.0 - BETA_TWO**STEP))) + ADAM_EPS
    corrected = new_first * (1.0 / (1.0 - BETA_ONE**STEP)) / root
    master = m_ref[...]
    new_master = master - rate * (corrected + decay * master)
    nm_ref[...] = new_master
    na_ref[...] = EMA_RATE * a_ref[...] + (1.0 - EMA_RATE) * new_master


def update(attn, feed, vec, master, first, second, average, span):
    count, rows = feed.shape[:2]
    columns = master.shape[1]
    steps = -(-columns // STEP_COLS)
    whole = lambda values: pl.BlockSpec(values.shape, lambda i: (0,) * values.ndim)
    cols = pl.BlockSpec((rows, STEP_COLS), lambda i: (0, i))
    return pl.pallas_call(
        functools.partial(update_kernel, count, span),
        grid=(steps,),
        in_specs=[whole(attn), whole(feed), whole(vec)] + [cols] * 4,
        out_specs=[cols] * 4,
        out_shape=[jax.ShapeDtypeStruct(master.shape, F32) for _ in range(4)],
        scratch_shapes=[pltpu.VMEM((rows, steps * STEP_COLS), F32)],
        compiler_params=vmem(),
        cost_estimate=pl.CostEstimate(flops=0, bytes_accessed=56_000_000, transcendentals=0),
        name="update",
    )(attn, feed, vec, master, first, second, average)


def chain_spans(lengths, prefix, padding, total):
    ends = jnp.cumsum(lengths, dtype=jnp.int32)
    starts = ends - lengths
    token = jnp.arange(total, dtype=jnp.int32)
    member = (token[:, None] >= starts[None, :]) & (token[:, None] < ends[None, :])
    pick = lambda values: jnp.sum(jnp.where(member, values[None, :], 0), axis=1, dtype=jnp.int32)
    start, end, pre, live = pick(starts), pick(ends), pick(prefix), pick(lengths - padding)
    place = token - start
    first = jnp.where(place < pre, start, token)
    first = jnp.where(place < live, first, 2 * total)
    blocks = total // ROWS
    low = start[::ROWS] // ROWS
    high = (end[ROWS - 1 :: ROWS] + ROWS - 1) // ROWS
    cut = lambda values: values.reshape(blocks, 1, ROWS)
    return (cut(first), cut(end), low, high), place


def rotary_tables(place):
    half = HD // 2
    freq = ROPE_BASE ** (-jnp.arange(half, dtype=F32) / half)
    angles = place.astype(F32)[:, None] * freq[None, :]
    cosine, sine = jnp.cos(angles), jnp.sin(angles)
    return jnp.concatenate([cosine, cosine], axis=1), jnp.concatenate([-sine, sine], axis=1)


def over_batch(block_of, own):
    count = lax.axis_size("batch")
    me = lax.axis_index("batch")
    arrived = [
        lax.ppermute(
            block_of(lax.rem(me + shift, count)),
            "batch",
            [(i, (i + shift) % count) for i in range(count)],
        )
        for shift in range(1, count)
    ]
    return functools.reduce(lambda total, part: total + part.astype(F32), arrived, own())


def rows_of(grad_rows):
    seq = lax.axis_size("seq")
    total = over_batch(
        lambda there: grad_rows(there).astype(BF), lambda: grad_rows(lax.axis_index("batch"))
    )
    blocks = total.astype(BF).reshape(seq, -1, total.shape[1])
    return lax.all_to_all(blocks, "seq", split_axis=0, concat_axis=0, tiled=True)


def vector_rows(sums):
    batch, seq = lax.axis_size("batch"), lax.axis_size("seq")
    me = lax.axis_index("batch")
    kinds = sums.shape[0]
    cut = sums.reshape(kinds, batch, seq, -1).transpose(2, 1, 0, 3)
    came = lax.all_to_all(cut, "seq", split_axis=0, concat_axis=0, tiled=True)
    totals = jnp.sum(came, axis=0)
    part = lambda place: lax.dynamic_index_in_dim(totals, place, 0, keepdims=False)
    return over_batch(part, lambda: part(me)).T


def on_device(hidden_in, cotangent, master, first, second, average, lengths, prefix, padding):
    groups, seq = lax.axis_size("batch"), lax.axis_size("seq")
    own = hidden_in.shape[0]
    tokens = own * seq
    rows = master.shape[0]
    span = -(-FF // (seq * LANES)) * LANES
    vec_cut = master[:, 4 * D + 3 * FF :].astype(BF).astype(F32).T
    vec_cut = jnp.pad(vec_cut, ((0, 8 - vec_cut.shape[0]), (0, LANES - rows)))[None]
    qkv_cut, out_cut, feed_cut = lay_out(master, seq, span)
    states, w_qkv, vectors = ring_gather(hidden_in, [qkv_cut, vec_cut], seq, 1)
    states = states.reshape(tokens, D)
    w_qkv = w_qkv.reshape(D, 3 * HD)
    vectors = vectors[..., :rows].transpose(2, 0, 1, 3).reshape(8, D)
    w_out = lax.all_gather(out_cut, ("batch", "seq"), axis=0, tiled=True)
    cot_all = lax.all_gather(cotangent, "seq", axis=0, tiled=True)

    spans, place = chain_spans(lengths[0], prefix[0], padding[0], tokens)
    cosine, sine = rotary_tables(place)
    a_low, query, key, value = norm_and_project(states, w_qkv, vectors, cosine, sine)
    attended, full, log = attend(query, key, value, spans)
    heads, w_feed = ring_gather(attended, [feed_cut], seq, 2)
    w_feed = w_feed.reshape(D, 3 * span)
    b_low, residual = residual_norm(states, heads, w_out, vectors, own)
    hidden, du, out_terms, db_terms = feed_forward(b_low, cot_all, w_feed)

    db_sum = ring_scatter(db_terms.reshape(seq, own, D), seq, 3)
    out_sum = lax.psum_scatter(out_terms, "seq", scatter_dimension=0, tiled=True)
    gain_one, bias_one, gain_two, bias_two = (vectors[i][None, :] for i in range(4))

    def norm_back(normal, inverse, slope, gain):
        scaled = slope * gain
        back = inverse * (
            scaled
            - jnp.mean(scaled, axis=-1, keepdims=True)
            - normal * jnp.mean(scaled * normal, axis=-1, keepdims=True)
        )
        return back, jnp.stack([jnp.sum(slope * normal, axis=0), jnp.sum(slope, axis=0)])

    normal_two, inverse_two = norm_parts(residual)
    output = DEEP_ALPHA * (normal_two * gain_two + bias_two) + out_sum.astype(F32)
    db = DEEP_ALPHA * cotangent.astype(F32) + db_sum
    dr, sums_two = norm_back(normal_two, inverse_two, db, gain_two)
    dr_low = dr.astype(BF)
    do = nt(dr_low, w_out).astype(BF)
    to_heads = lambda values: lax.all_to_all(
        values.reshape(own, seq, HD).transpose(1, 0, 2), "seq", split_axis=0, concat_axis=0, tiled=True
    ).reshape(tokens, HD)
    do_head = to_heads(do)
    dr_cols = to_heads(dr_low)

    def row_part(values, place):
        return lax.dynamic_slice_in_dim(values, place * (D // groups), D // groups, 1)

    grad_feed = rows_of(
        lambda place: jnp.concatenate(
            [tn(row_part(b_low, place), du), tn(row_part(cot_all, place), hidden)], axis=1
        )
    )
    dp = attend_back(query, key, value, do_head, full, log, spans, cosine, sine)
    da_terms = nt(dp, w_qkv).astype(BF)
    da_sum = ring_scatter(da_terms.reshape(seq, own, D), seq, 5)
    grad_out = jnp.einsum("htd,tn->hdn", heads, dr_cols, preferred_element_type=F32).reshape(D, HD)
    grad_attn = rows_of(
        lambda place: jnp.concatenate(
            [
                tn(row_part(a_low, place), dp),
                lax.dynamic_slice_in_dim(grad_out, place * (D // groups), D // groups, 0),
            ],
            axis=1,
        )
    )
    normal_one, inverse_one = norm_parts(hidden_in.astype(F32))
    da = DEEP_ALPHA * dr + da_sum
    input_grad, sums_one = norm_back(normal_one, inverse_one, da, gain_one)
    vector_grad = vector_rows(jnp.concatenate([sums_one, sums_two]))

    vector_grad = jnp.pad(vector_grad, ((0, 0), (0, LANES - vector_grad.shape[1])))
    updated = update(grad_attn, grad_feed, vector_grad, master, first, second, average, span)
    return (
        output.astype(BF),
        input_grad.astype(BF),
        *updated,
    )


def solution(mesh):
    spread = P(("batch", "seq"), None)
    return jax.shard_map(
        on_device,
        mesh=mesh,
        in_specs=(spread,) * 6 + (P("batch", None),) * 3,
        out_specs=(spread,) * 6,
        check_vma=False,
    )
```

time: 1430 us -> 720 us (0.50); the launches traced: 1400 us -> 711 us
  waiting for transfers between devices: 900 us -> 46.8 us
  Pallas kernels: 0 us -> 516 us
  matrix products: 233 us -> 52.8 us
  local copies, waits for them, and re-layouts: 119 us -> 26.9 us
  other arithmetic: 57.7 us -> 25 us
  blocking collectives: 24.4 us -> 0 us
  starting transfers between devices: 48.2 us -> 28.4 us
    all_gather x5 -> x2, waiting for transfers between devices: 518 us -> 0.02 us  [the longest x1 0.02 us: on_device(): w_out = lax.all_gather(out_cut, ('batch', 'seq'), axis=0, tiled=True)]
    pallas_call x0 -> x11, Pallas kernels: none -> 516 us  [the longest x2 250 us: ring_gather(): pl.pallas_call(functools.partial(gather_kernel, count, len(blocks)), out_...]
    all_to_all x8 -> x5, waiting for transfers between devices: 241 us -> 22.5 us  [the longest x2 19.7 us: rows_of(): lax.all_to_all(blocks, 'seq', split_axis=0, concat_axis=0, tiled=True)]
    dot_general x40 -> x9, matrix products: 233 us -> 52.8 us  [the longest x6 33.2 us: tn(): lax.dot_general(left, right, (((0,), (0,)), ((), ())), preferred_element_...]
    reduce_scatter x2 -> x1, waiting for transfers between devices: 139 us -> 22 us  [on_device(): lax.psum_scatter(out_terms, 'seq', scatter_dimension=0, tiled=True)]
    concatenate x2 -> x4, local copies, waits for them, and re-layouts: 36.1 us -> 0.28 us  [on_device(): vector_grad = vector_rows(jnp.concatenate([sums_one, sums_two]))]
    all_to_all x1 -> x0, blocking collectives: 24.4 us -> none  [on_device(): lax.all_to_all(attended_h, 'seq', split_axis=0, concat_axis=1, tiled=True)]
    all_to_all x8 -> x5, starting transfers between devices: 47.7 us -> 26.5 us  [the longest x2 11.5 us: on_device(): lax.all_to_all(values.reshape(own, seq, HD).transpose(1, 0, 2), 'seq', sp...]
  transfers between devices with their start and end apart: 15 -> 11, of which waited for: 9 -> 5; matrix products, arithmetic and copies ran while one was open for 23% -> 15% of each run, Pallas kernels for 0% -> 64%
where the time goes in v1:
time: 720 us; the launch traced here: 711 us
  Pallas kernels  516 us (72%)
  matrix products  52.8 us (7%)
  waiting for transfers between devices  46.8 us (6%)
  starting transfers between devices  28.4 us (4%)
  local copies, waits for them, and re-layouts  26.9 us (4%)
  other arithmetic  25 us (3%)
  between operations  14.6 us (2%)
    pallas_call x2, Pallas kernels, ring_gather(): pl.pallas_call(functools.partial(gather_kernel, count, len(blocks)), out_...  250 us
    pallas_call x2, Pallas kernels, ring_scatter(): pl.pallas_call(functools.partial(scatter_kernel, count), out_shape=jax.Sh...  125 us
    dot_general x6, matrix products, tn(): lax.dot_general(left, right, (((0,), (0,)), ((), ())), preferred_element_...  33.2 us
    pallas_call x1, Pallas kernels, residual_norm(): pl.pallas_call(residual_kernel, grid=(tokens // ROWS,), in_specs=[rows, p...  31.9 us
    pallas_call x1, Pallas kernels, feed_forward(): pl.pallas_call(feed_kernel, grid=(tokens // ROWS,), in_specs=[rows(D), ro...  30.4 us
    pallas_call x1, Pallas kernels, update(): pl.pallas_call(functools.partial(update_kernel, count, span), grid=(steps...  23.1 us
    reduce_scatter x1, waiting for transfers between devices, on_device(): lax.psum_scatter(out_terms, 'seq', scatter_dimension=0, tiled=True)  22 us
    pallas_call x1, Pallas kernels, attend_back(): pl.pallas_call(attend_back_kernel, grid_spec=pltpu.PrefetchScalarGridSpec...  20.4 us
  transfers between devices with their start and end apart: 11, of which 5 were waited for; matrix products, arithmetic and copies ran while one was open for 15% of the time, Pallas kernels for 64%

profile of v1, /device:TPU:9, one launch (start us, length us, event | category | flops | bytes accessed | tf_op | source)
XLA Modules:
  0.0 710.8 jit_solution(15856407319926307838)
XLA Ops:
  7.2 5.1 lay_out.1
  12.4 0.7 all-gather.5.cloned.1.call-update
  13.2 0.9 slice.41
  14.2 0.2 reduce-window.4
  14.4 0.2 select_reduce_fusion
  14.7 0.6 bitcast_convert_fusion.refs_1_
  15.3 112.3 %ring_gather_1.1 = (bf16[16,128,2048]{2,1,0:T(8,128)(2,1)}, bf16[2,16,64,384]{3,2,1,0:T(8,128)(2,1)}, f32[2,16,8,128]{3,2,1,0:T(8,128)}) custom-call(bf16[128,2048]{1,0:T(8,128)(2,1)} %x_ref.1, bf16[16,64,384]{2,1,0:T(8,128)(2,1)} %get-tuple-element.31.refs_0_, f32[1,8,128]{2,1,0:T(8,128)} %bitcast_convert_fusion.refs_1_), custom_call_target="tpu_custom_call" | custom-call | bytes 150000000 | tf_op jit(solution)/shard_map/ring_gather_1/pallas_call | solution.py:234
  127.6 0.9 slice_bitcast_fusion
  128.5 0.7 reshape.200.vec_ref
  129.3 0.6 and_select_fusion
  129.9 0.6 compare_select_fusion.1.first_ref
  130.5 3.7 fusion.35
  134.2 1.9 pad_maximum_fusion.1
  136.1 14.5 %norm_and_project.1 = (bf16[2048,2048]{1,0:T(8,128)(2,1)}, bf16[2048,128]{1,0:T(8,128)(2,1)}, bf16[2048,128]{1,0:T(8,128)(2,1)}, bf16[2048,128]{1,0:T(8,128)(2,1)}) custom-call(bf16[2048,2048]{1,0:T(8,128)(2,1)} %bitcast.82, bf16[2048,384]{1,0:T(8,128)(2,1)} %bitcast.86, f32[8,2048]{1,0:T(8,128)} %reshape.200.vec_ref, ...), custom_call_target="tpu_custom_call" | custom-call | flops 3221225472 | bytes 24000000 | tf_op jit(solution)/shard_map/norm_and_project/pallas_call | solution.py:345
  150.7 16.2 %attend.1 = (bf16[2048,128]{1,0:T(8,128)(2,1)}, f32[2048,128]{1,0:T(8,128)}, f32[2048,128]{1,0:T(8,128)}) custom-call(s32[8]{0:T(128)} %get-tuple-element.83.low_ref, s32[8]{0:T(128)} %get-tuple-element.82.high_ref, bf16[2048,128]{1,0:T(8,128)(2,1)} %get-tuple-element.35.q_ref, bf16[8,256,128]{2,1,0:T(8,128)(2,1)} %bitcast.101, ...), custom_call_target="tpu_custom_call" | custom-call | flops 1073741824 | bytes 4000000 | tf_op jit(solution)/shard_map/attend/pallas_call | solution.py:402
  166.9 137.4 %ring_gather_2.1 = (bf16[16,2048,128]{2,1,0:T(8,128)(2,1)}, bf16[2,16,64,1152]{3,2,1,0:T(8,128)(2,1)}) custom-call(bf16[2048,128]{1,0:T(8,128)(2,1)} %get-tuple-element.38.x_ref, bf16[16,64,1152]{2,1,0:T(8,128)(2,1)} %get-tuple-element.39.refs_0_), custom_call_target="tpu_custom_call" | custom-call | bytes 150000000 | tf_op jit(solution)/shard_map/ring_gather_2/pallas_call | solution.py:234
  304.3 31.9 %residual_norm.1 = (bf16[2048,2048]{1,0:T(8,128)(2,1)}, f32[128,2048]{1,0:T(8,128)}) custom-call(bf16[2048,2048]{1,0:T(8,128)(2,1)} %bitcast.83, bf16[16,2048,128]{2,1,0:T(8,128)(2,1)} %get-tuple-element.40.heads_ref, bf16[2048,2048]{1,0:T(8,128)(2,1)} %all-gather.3.cloned.1.call-done.w_ref, f32[8,2048]{1,0:T(8,128)} %reshape.200.vec_ref), custom_call_target="tpu_custom_call" | custom-call | flops 17179869184 | bytes 32000000 | tf_op jit(solution)/shard_map/residual_norm/pallas_call | solution.py:536
  336.2 30.4 %feed_forward.1 = (bf16[2048,384]{1,0:T(8,128)(2,1)}, bf16[2048,768]{1,0:T(8,128)(2,1)}, bf16[2048,2048]{1,0:T(8,128)(2,1)}, bf16[2048,2048]{1,0:T(8,128)(2,1)}) custom-call(bf16[2048,2048]{1,0:T(8,128)(2,1)} %get-tuple-element.43.b_ref, bf16[2048,2048]{1,0:T(8,128)(2,1)} %all-gather.5.cloned.1.call-done.cot_ref, bf16[2048,1152]{1,0:T(8,128)(2,1)} %bitcast.100), custom_call_target="tpu_custom_call" | custom-call | flops 19327352832 | bytes 48000000 | tf_op jit(solution)/shard_map/feed_forward/pallas_call | solution.py:584
  366.9 78.0 %ring_scatter_3.1 = f32[128,2048]{1,0:T(8,128)} custom-call(bf16[16,128,2048]{2,1,0:T(8,128)(2,1)} %bitcast.79), custom_call_target="tpu_custom_call" | custom-call | bytes 150000000 | tf_op jit(solution)/shard_map/ring_scatter_3/pallas_call | solution.py:309
  444.9 4.3 fusion.20
  449.2 5.7 fusion.14
  454.9 1.6 pad_maximum_fusion
  456.5 0.3 collective-permute-start.1
  456.9 0.3 multiply_reduce_fusion.2
  457.4 0.5 multiply_reduce_fusion
  457.9 22.0 %reduce-scatter.2.cloned.1.call-done = bf16[128,2048]{1,0:T(8,128)(2,1)} async-done(((bf16[2048,2048]{1,0:T(8,128)(2,1)}), bf16[128,2048]{1,0:T(8,128)(2,1)}) %reduce-scatter.2.cloned.1.call-update) | async-done | bytes 524304 | tf_op jit(solution)/shard_map/reduce_scatter | solution.py:826
  479.9 2.7 convert_bitcast_fusion
  482.7 0.9 copy.78
  483.6 5.5 all-to-all-start.1
  489.1 8.3 %fusion.7 = f32[1024,768]{0,1:T(8,128)} fusion(bf16[2048,768]{1,0:T(8,128)(2,1)} %get-tuple-element.50, bf16[2048,2048]{1,0:T(8,128)(2,1)} %get-tuple-element.43.b_ref, s32[]{:T(128)S(6)} %select_n.70), kind=kOutput, calls=%fused_computation.9 | convolution fusion | flops 3221225472 | bytes 10485764 | tf_op jit(solution)/shard_map/dot_general | solution.py:43
  497.4 6.3 fusion.28
  503.6 0.9 copy.79
  504.6 6.0 all-to-all-start
  510.6 4.6 fusion.5
  515.3 3.9 fusion
  519.2 4.3 copy.68
  523.5 1.2 all-to-all-done
  524.7 5.2 all-to-all-start.3
  530.0 12.4 %copy.65 = bf16[16,128,2048]{2,1,0:T(8,128)(2,1)} copy(bf16[16,128,2048]{1,2,0:T(8,128)(2,1)} %bitcast.81) | data formatting | bytes 16777216 | tf_op jit(solution)/shard_map/htd,tn->hdn/dot_general | solution.py:861
  542.6 0.3 fusion.34
  543.0 6.3 fusion.47
  549.4 20.4 %attend_back.1 = bf16[2048,384]{1,0:T(8,128)(2,1)} custom-call(s32[8]{0:T(128)} %get-tuple-element.83.low_ref, s32[8]{0:T(128)} %get-tuple-element.82.high_ref, bf16[2048,128]{1,0:T(8,128)(2,1)} %get-tuple-element.35.q_ref, bf16[2048,128]{1,0:T(8,128)(2,1)} %bitcast.88, f32[2048,128]{1,0:T(8,128)} %get-tuple-element.47.full_ref, ...), custom_call_target="tpu_custom_call" | custom-call | flops 2684354560 | bytes 6000000 | tf_op jit(solution)/shard_map/attend_back/pallas_call | solution.py:493
  569.7 4.7 fusion.17
  574.4 1.0 pad_maximum_fusion.3
  575.4 1.2 collective-permute-start
  576.6 7.1 convolution_convert_fusion
  583.7 47.0 %ring_scatter_5.1 = f32[128,2048]{1,0:T(8,128)} custom-call(bf16[16,128,2048]{2,1,0:T(8,128)(2,1)} %bitcast.80), custom_call_target="tpu_custom_call" | custom-call | bytes 150000000 | tf_op jit(solution)/shard_map/ring_scatter_5/pallas_call | solution.py:309
  630.7 2.5 fusion.33
  633.4 0.7 reshape.231
  634.2 5.7 fusion.11
  639.9 4.7 all-to-all-start.4
  644.5 2.0 fusion.13
  646.6 1.3 copy.67
  647.9 1.6 all-to-all-done.4
  649.5 5.2 all-to-all-start.2
  654.7 0.5 broadcast.175
  655.3 0.7 reduce.12
  656.2 0.3 collective-permute-start.2
  656.6 1.2 fusion.32
  657.9 1.5 collective-permute-done.2
  659.3 0.6 pad.10.vec_ref
  659.9 19.7 %all-to-all-done.2.attn_ref = bf16[16,64,512]{2,1,0:T(8,128)(2,1)S(1)} async-done(((bf16[16,64,512]{2,1,0:T(8,128)(2,1)}), bf16[16,64,512]{2,1,0:T(8,128)(2,1)S(1)}, u32[]{:S(2)}, u32[]{:S(2)}) %all-to-all-start.2) | async-done | bytes 1048608 | tf_op jit(solution)/shard_map/all_to_all | solution.py:786
  679.6 1.0 copy-done.5
  680.6 23.1 %update.1 = (f32[64,24579]{1,0:T(8,128)}, f32[64,24579]{1,0:T(8,128)}, f32[64,24579]{1,0:T(8,128)}, f32[64,24579]{1,0:T(8,128)}) custom-call(bf16[16,64,512]{2,1,0:T(8,128)(2,1)} %copy-done.5, bf16[16,64,1152]{2,1,0:T(8,128)(2,1)} %all-to-all-done.3.feed_ref, f32[64,128]{1,0:T(8,128)} %pad.10.vec_ref, f32[64,24579]{1,0:T(8,128)} %m_ref.3, ...), custom_call_target="tpu_custom_call" | custom-call | bytes 56000000 | tf_op jit(solution)/shard_map/update/pallas_call | solution.py:728
  (77 shorter events, 2.2 us)
Async XLA Ops:
  7.2 7.0 copy-start.11
  7.2 7.2 %copy-start.12 = (s32[1,4]{1,0:T(1,128)S(1)}, s32[1,4]{1,0:T(1,128)}, u32[]{:S(2)}) copy-start(s32[1,4]{1,0:T(1,128)} %param.17) | copy-start | bytes 52
  7.2 7.2 %copy-start.10 = (s32[1,4]{1,0:T(1,128)S(1)}, s32[1,4]{1,0:T(1,128)}, u32[]{:S(2)}) copy-start(s32[1,4]{1,0:T(1,128)} %param.16) | copy-start | bytes 52
  7.2 297.1 %all-gather.3.cloned.1.call-start = ((), (), s32[]{:S(2)}) async-start(), calls=%async_computation.6 | async-start | bytes 8650752 | tf_op jit(solution)/shard_map/all_gather | solution.py:813
  12.4 323.8 %all-gather.5.cloned.1.call-start = ((), (), s32[]{:S(2)}) async-start(), calls=%async_computation.7 | async-start | bytes 8912896 | tf_op jit(solution)/shard_map/all_gather | solution.py:814
  13.1 466.8 %reduce-scatter.2.cloned.1.call-start = ((), (), s32[]{:S(2)}) async-start(), calls=%async_computation.8 | async-start | bytes 8912896 | tf_op jit(solution)/shard_map/reduce_scatter | solution.py:826
  14.5 121.6 %copy-start.9 = (s32[2048]{0:T(1024)}, s32[2048]{0:T(1024)S(1)}, u32[]{:S(2)}) copy-start(s32[2048]{0:T(1024)S(1)} %get-tuple-element.69) | copy-start | bytes 24580
  366.9 78.0 %copy-start.14 = (bf16[2048,384]{1,0:T(8,128)(2,1)S(1)}, bf16[2048,384]{1,0:T(8,128)(2,1)}, u32[]{:S(2)}) copy-start(bf16[2048,384]{1,0:T(8,128)(2,1)} %get-tuple-element.51) | copy-start | bytes 4718596
  444.9 4.3 copy-start.15
  454.8 1.9 copy-start
  454.8 2.4 copy-start.2
  454.9 2.5 copy-start.3
  456.5 58.8 %collective-permute-start.1 = (bf16[1024,1152]{0,1:T(8,128)(2,1)}, bf16[1024,1152]{0,1:T(8,128)(2,1)}, u32[]{:S(2)}, u32[]{:S(2)}) collective-permute-start(bf16[1024,1152]{0,1:T(8,128)(2,1)} %pad_maximum_fusion), channel_id=1, source_target_pairs={{0,16},{16,0},{1,17},{17,1},{2,18},{18,2},{3,19},{19,3},{4,20},{20... | collective-permute-start | bytes 7077896 | tf_op jit(solution)/shard_map/ppermute | solution.py:770
  483.6 21.0 %all-to-all-start.1 = ((bf16[16,128,128]{2,1,0:T(8,128)(2,1)}), bf16[16,128,128]{2,1,0:T(8,128)(2,1)S(1)}, u32[]{:S(2)}, u32[]{:S(2)}) async-start(bf16[16,128,128]{2,1,0:T(8,128)(2,1)} %bitcast.73), calls=%async_computation.2 | async-start | bytes 1048576 | tf_op jit(solution)/shard_map/all_to_all | solution.py:844
  504.6 20.2 %all-to-all-start = ((bf16[16,128,128]{2,1,0:T(8,128)(2,1)}), bf16[16,128,128]{2,1,0:T(8,128)(2,1)S(1)}, u32[]{:S(2)}, u32[]{:S(2)}) async-start(bf16[16,128,128]{2,1,0:T(8,128)(2,1)} %bitcast.75), calls=%async_computation.1 | async-start | bytes 1048576 | tf_op jit(solution)/shard_map/all_to_all | solution.py:844
  510.6 4.7 copy-start.6
  524.7 5.3 copy-start.8
  524.7 115.1 %all-to-all-start.3 = ((bf16[16,64,1152]{2,1,0:T(8,128)(2,1)}), bf16[16,64,1152]{2,1,0:T(8,128)(2,1)}, u32[]{:S(2)}, u32[]{:S(2)}) async-start(bf16[16,64,1152]{2,1,0:T(8,128)(2,1)} %bitcast.78), calls=%async_computation.4 | async-start | bytes 4718592 | tf_op jit(solution)/shard_map/all_to_all | solution.py:786
  530.0 12.4 %copy-start.1 = (bf16[128,2048]{1,0:T(8,128)(2,1)S(1)}, bf16[128,2048]{1,0:T(8,128)(2,1)}, u32[]{:S(2)}) copy-start(bf16[128,2048]{1,0:T(8,128)(2,1)} %x_ref.1) | copy-start | bytes 1572868
  569.7 6.9 copy-start.7
  569.7 6.9 copy-start.13
  575.4 69.1 %collective-permute-start = (bf16[1024,512]{0,1:T(8,128)(2,1)}, bf16[1024,512]{0,1:T(8,128)(2,1)}, u32[]{:S(2)}, u32[]{:S(2)}) collective-permute-start(bf16[1024,512]{0,1:T(8,128)(2,1)} %pad_maximum_fusion.3), channel_id=1, source_target_pairs={{0,16},{16,0},{1,17},{17,1},{2,18},{18,2},{3,19},{19,3},{4,20},{20... | collective-permute-start | bytes 3145736 | tf_op jit(solution)/shard_map/ppermute | solution.py:770
  639.9 9.7 %all-to-all-start.4 = ((f32[16,1,512]{2,1,0:T(1,128)}), f32[16,1,512]{2,1,0:T(1,128)S(1)}, u32[]{:S(2)}, u32[]{:S(2)}) async-start(f32[16,1,512]{2,1,0:T(1,128)} %reshape.231), calls=%async_computation.5 | async-start | bytes 65536 | tf_op jit(solution)/shard_map/all_to_all | solution.py:794
  646.6 10.0 %copy-start.4 = (f32[128,2048]{1,0:T(8,128)S(1)}, f32[128,2048]{1,0:T(8,128)}, u32[]{:S(2)}) copy-start(f32[128,2048]{1,0:T(8,128)} %get-tuple-element.73) | copy-start | bytes 3145732
  649.5 30.1 %all-to-all-start.2 = ((bf16[16,64,512]{2,1,0:T(8,128)(2,1)}), bf16[16,64,512]{2,1,0:T(8,128)(2,1)S(1)}, u32[]{:S(2)}, u32[]{:S(2)}) async-start(bf16[16,64,512]{2,1,0:T(8,128)(2,1)} %bitcast.84), calls=%async_computation.3 | async-start | bytes 2097152 | tf_op jit(solution)/shard_map/all_to_all | solution.py:786
  656.2 3.1 collective-permute-start.2
  679.6 1.0 copy-start.5
Sparse Core Ops, SparseCore 0:
  12.5 94.7 all-gather.2
  109.4 82.5 all-gather.4
  366.7 113.1 reduce-scatter.1

commit v2 on v1

--- a/solution.py
+++ b/solution.py
@@ -66,12 +66,6 @@
         pair = jnp.where(place < half, 2 * place, 2 * (self.pairs - 1 - place) + 1)
         return pair * 2 + (self.core if core is None else core)
 
-    def greet(self):
-        barrier = pltpu.get_barrier_semaphore()
-        for device in (self.at(-1), self.sibling):
-            pl.semaphore_signal(barrier, inc=1, device_id=(self.batch, device), device_id_type=MESH)
-        pl.semaphore_wait(barrier, 2)
-
     def greet_all(self, count):
         barrier = pltpu.get_barrier_semaphore()
         groups = lax.axis_size("batch")
@@ -82,6 +76,15 @@
             group = lax.rem(self.batch + shift, groups)
             pl.semaphore_signal(barrier, inc=1, device_id=(group, self.me), device_id_type=MESH)
         pl.semaphore_wait(barrier, count + groups - 2)
+
+    def greet_groups(self, groups):
+        barrier = pltpu.get_barrier_semaphore()
+        for device in (self.at(-1), self.sibling):
+            pl.semaphore_signal(barrier, inc=1, device_id=(self.batch, device), device_id_type=MESH)
+        for shift in range(1, groups):
+            group = lax.rem(self.batch + shift, groups)
+            pl.semaphore_signal(barrier, inc=1, device_id=(group, self.me), device_id_type=MESH)
+        pl.semaphore_wait(barrier, 1 + groups)
 
     def copy(self, src, dst, send, recv, device):
         return pltpu.make_async_remote_copy(
@@ -168,16 +171,11 @@
         self.mine.wait()
 
 
-def gather_kernel(count, extra, x_ref, *refs):
-    parts, (o_ref, *outs), sems = refs[:extra], refs[extra : 2 * extra + 1], refs[2 * extra + 1 :]
-    ring_s, ring_r, sib_s, sib_r, own_sem = sems[:5]
-    ring = Ring(count)
+def pass_round(ring, count, x_ref, o_ref, sems, columns, work):
+    ring_s, ring_r, sib_s, sib_r, own_sem = sems
     piece = x_ref.shape[0] // SUBS
     own = pltpu.make_async_copy(x_ref, o_ref.at[ring.me], own_sem)
     own.start()
-    columns = [
-        Columns(ring, count, parts[i], outs[i], sems[5 + 5 * i : 10 + 5 * i]) for i in range(extra)
-    ]
     ring.greet_all(count)
     following, sends = ring.at(1), []
     ahead = 1
@@ -201,22 +199,32 @@
         if step == 0:
             for column in columns:
                 column.start()
-        elif 2 * step >= ring.pairs:
-            upto = count if step == ring.pairs - 1 else count * (2 * step - ring.pairs + 1) // ring.pairs
+            own.wait()
+        else:
+            upto = count if step == ring.pairs - 1 else min(count, 1 + 2 * step)
             for passed in range(ahead, max(ahead, upto)):
                 for column in columns:
                     column.pass_on(passed)
             ahead = max(ahead, upto)
-    for step in range(ring.pairs):
-        block = ring.at(step, 1 - ring.core)
+        other = ring.at(step, 1 - ring.core)
         for sub in range(SUBS):
-            dst = o_ref.at[block].at[pl.ds(sub * piece, piece)]
+            dst = o_ref.at[other].at[pl.ds(sub * piece, piece)]
             ring.copy(
                 dst, dst, sib_s.at[step, sub], sib_r.at[step, sub], ring.sibling
             ).wait_recv()
+        work(step, block, other)
+    return sends
+
+
+def gather_kernel(count, extra, x_ref, *refs):
+    parts, (o_ref, *outs), sems = refs[:extra], refs[extra : 2 * extra + 1], refs[2 * extra + 1 :]
+    ring = Ring(count)
+    columns = [
+        Columns(ring, count, parts[i], outs[i], sems[5 + 5 * i : 10 + 5 * i]) for i in range(extra)
+    ]
+    sends = pass_round(ring, count, x_ref, o_ref, sems[:5], columns, lambda *_: None)
     for go in sends:
         go.wait_send()
-    own.wait()
     for column in columns:
         column.finish()
 
@@ -224,100 +232,622 @@
 def ring_gather(values, blocks, count, ident):
     pairs, groups = count // 2, lax.axis_size("batch")
     anywhere = pl.BlockSpec(memory_space=pl.ANY)
-    column_sems = [
+    return pl.pallas_call(
+        functools.partial(gather_kernel, count, len(blocks)),
+        out_shape=[jax.ShapeDtypeStruct((count,) + values.shape, values.dtype)]
+        + [jax.ShapeDtypeStruct((groups, count) + b.shape[1:], b.dtype) for b in blocks],
+        in_specs=[anywhere] * (1 + len(blocks)),
+        out_specs=[anywhere] * (1 + len(blocks)),
+        scratch_shapes=ring_sems(pairs) + column_sems(count, groups) * len(blocks),
+        compiler_params=pltpu.CompilerParams(collective_id=ident, has_side_effects=True),
+        cost_estimate=pl.CostEstimate(flops=0, bytes_accessed=150_000_000, transcendentals=0),
+        name=f"ring_gather_{ident}",
+    )(values, *blocks)
+
+
+def ring_sems(pairs):
+    return [pltpu.SemaphoreType.DMA((pairs, SUBS)) for _ in range(4)] + [pltpu.SemaphoreType.DMA]
+
+
+def column_sems(count, groups):
+    return [
         pltpu.SemaphoreType.DMA((count,)),
         pltpu.SemaphoreType.DMA((count,)),
         pltpu.SemaphoreType.DMA((groups, count)),
         pltpu.SemaphoreType.DMA((groups, count)),
         pltpu.SemaphoreType.DMA,
     ]
-    return pl.pallas_call(
-        functools.partial(gather_kernel, count, len(blocks)),
-        out_shape=[jax.ShapeDtypeStruct((count,) + values.shape, values.dtype)]
-        + [jax.ShapeDtypeStruct((groups, count) + b.shape[1:], b.dtype) for b in blocks],
-        in_specs=[anywhere] * (1 + len(blocks)),
-        out_specs=[anywhere] * (1 + len(blocks)),
-        scratch_shapes=[pltpu.SemaphoreType.DMA((pairs, SUBS)) for _ in range(4)]
-        + [pltpu.SemaphoreType.DMA]
-        + column_sems * len(blocks),
-        compiler_params=pltpu.CompilerParams(collective_id=ident, has_side_effects=True),
-        cost_estimate=pl.CostEstimate(flops=0, bytes_accessed=150_000_000, transcendentals=0),
-        name=f"ring_gather_{ident}",
-    )(values, *blocks)
-
-
-def scatter_kernel(count, x_ref, o_ref, own, sib, got, ring_s, ring_r, sib_s, sib_r, load):
+
+
+def residual_kernel(
+    count,
+    x_ref,
+    part_ref,
+    states_ref,
+    w_ref,
+    vec_ref,
+    heads_ref,
+    feed_ref,
+    b_ref,
+    own_ref,
+    heads,
+    w_out,
+    total,
+    states,
+    low,
+    w_sem,
+    load_sem,
+    store_sem,
+    heads_sem,
+    *sems,
+):
     ring = Ring(count)
-    piece = x_ref.shape[1] // SUBS
-    pairs = ring.pairs
-    loads = []
-    for step in range(pairs):
-        go = pltpu.make_async_copy(x_ref.at[ring.at(-1 - step)], own.at[step], load.at[step])
-        go.start()
-        loads.append(go)
-    ring.greet()
-    following, sends = ring.at(1), []
-    for step in range(pairs):
-        block = ring.at(1 + step, 1 - ring.core)
-        for sub in range(SUBS):
-            rows = pl.ds(sub * piece, piece)
-            go = ring.copy(
-                x_ref.at[block].at[rows],
-                sib.at[step].at[rows],
-                sib_s.at[step, sub],
-                sib_r.at[step, sub],
-                ring.sibling,
-            )
+    tokens, own = total.shape[0], own_ref.shape[0]
+    blocks = tokens // ROWS
+    weights = pltpu.make_async_copy(w_ref, w_out, w_sem)
+    weights.start()
+    columns = [Columns(ring, count, part_ref, feed_ref, sems[5:10])]
+
+    def rows_of(block):
+        return pl.ds(pl.multiple_of(block * ROWS, ROWS), ROWS)
+
+    def load(block):
+        slot = lax.rem(block, 2)
+        return pltpu.make_async_copy(
+            states_ref.at[rows_of(block)], states.at[slot], load_sem.at[slot]
+        )
+
+    def store(block):
+        slot = lax.rem(block, 2)
+        return pltpu.make_async_copy(low.at[slot], b_ref.at[rows_of(block)], store_sem.at[slot])
+
+    load(0).start()
+
+    def begin():
+        @pl.loop(0, blocks)
+        def _(block):
+            @pl.when(block + 1 < blocks)
+            def _():
+                load(block + 1).start()
+
+            load(block).wait()
+            normal, _ = norm_parts(states[lax.rem(block, 2)].astype(F32))
+            total[rows_of(block), :] = DEEP_ALPHA * (normal * vec_ref[0:1, :] + vec_ref[1:2, :])
+
+        weights.wait()
+
+    def saves(step, block, other):
+        return [
+            pltpu.make_async_copy(heads.at[head], heads_ref.at[head], heads_sem.at[step, part])
+            for part, head in enumerate((block, other))
+        ]
+
+    kept = []
+
+    def work(step, block, other):
+        if step == 0:
+            begin()
+        for go in saves(step, block, other):
             go.start()
-            sends.append(go)
-    for step in range(pairs):
-        loads[step].wait()
-        for sub in range(SUBS):
-            rows = pl.ds(sub * piece, piece)
-            here = own.at[step].at[rows]
-            other = sib.at[step].at[rows]
-            ring.copy(
-                other, other, sib_s.at[step, sub], sib_r.at[step, sub], ring.sibling
-            ).wait_recv()
-            total = here[...].astype(F32) + other[...].astype(F32)
-            if step > 0:
-                came = got.at[step - 1].at[rows]
-                ring.copy(
-                    came, came, ring_s.at[step - 1, sub], ring_r.at[step - 1, sub], following
-                ).wait_recv()
-                total = total + came[...].astype(F32)
-            if step == pairs - 1:
-                o_ref[rows, :] = total
-            else:
-                here[...] = total.astype(BF)
-                go = ring.copy(
-                    here,
-                    got.at[step].at[rows],
-                    ring_s.at[step, sub],
-                    ring_r.at[step, sub],
-                    following,
+            kept.append(go)
+        wide = 512
+
+        @pl.loop(0, blocks)
+        def _(part):
+            rows = rows_of(part)
+            left = jnp.concatenate([heads[block, rows, :], heads[other, rows, :]], axis=1)
+            for at in range(0, D, wide):
+                right = jnp.concatenate(
+                    [
+                        w_out[pl.ds(pl.multiple_of(head * HD, HD), HD), at : at + wide]
+                        for head in (block, other)
+                    ],
+                    axis=0,
                 )
-                go.start()
-                sends.append(go)
+                total[rows, at : at + wide] += nn(left, right)
+
+    sends = pass_round(ring, count, x_ref, heads, sems[:5], columns, work)
+
+    @pl.loop(0, blocks)
+    def _(block):
+        @pl.when(block >= 2)
+        def _():
+            store(block - 2).wait()
+
+        normal, _ = norm_parts(total[rows_of(block), :])
+        low[lax.rem(block, 2)] = (normal * vec_ref[2:3, :] + vec_ref[3:4, :]).astype(BF)
+        store(block).start()
+
+    own_ref[...] = total[pl.ds(pl.multiple_of(ring.me * own, own), own), :]
+    for block in (blocks - 2, blocks - 1):
+        store(block).wait()
+    for go in kept:
+        go.wait()
     for go in sends:
         go.wait_send()
-
-
-def ring_scatter(terms, count, ident):
-    pairs = count // 2
-    shape = terms.shape[1:]
+    for column in columns:
+        column.finish()
+
+
+def gather_residual(attended, feed_cut, states, w_out, vectors, own, count, ident):
+    tokens = attended.shape[0]
+    pairs, groups = count // 2, lax.axis_size("batch")
+    inside, anywhere = pl.BlockSpec(memory_space=pltpu.VMEM), pl.BlockSpec(memory_space=pl.ANY)
     return pl.pallas_call(
-        functools.partial(scatter_kernel, count),
-        out_shape=jax.ShapeDtypeStruct(shape, F32),
-        in_specs=[pl.BlockSpec(memory_space=pl.ANY)],
-        out_specs=pl.BlockSpec(memory_space=pltpu.VMEM),
-        scratch_shapes=[pltpu.VMEM((pairs,) + shape, BF) for _ in range(3)]
-        + [pltpu.SemaphoreType.DMA((pairs, SUBS)) for _ in range(4)]
-        + [pltpu.SemaphoreType.DMA((pairs,))],
+        functools.partial(residual_kernel, count),
+        out_shape=[
+            jax.ShapeDtypeStruct((count, tokens, HD), BF),
+            jax.ShapeDtypeStruct((groups,) + feed_cut.shape, BF),
+            jax.ShapeDtypeStruct((tokens, D), BF),
+            jax.ShapeDtypeStruct((own, D), F32),
+        ],
+        in_specs=[anywhere] * 4 + [inside],
+        out_specs=[anywhere] * 3 + [inside],
+        scratch_shapes=[
+            pltpu.VMEM((count, tokens, HD), BF),
+            pltpu.VMEM((D, D), BF),
+            pltpu.VMEM((tokens, D), F32),
+            pltpu.VMEM((2, ROWS, D), BF),
+            pltpu.VMEM((2, ROWS, D), BF),
+            pltpu.SemaphoreType.DMA,
+            pltpu.SemaphoreType.DMA((2,)),
+            pltpu.SemaphoreType.DMA((2,)),
+            pltpu.SemaphoreType.DMA((pairs, 2)),
+        ]
+        + ring_sems(pairs)
+        + column_sems(count, groups),
         compiler_params=vmem(collective_id=ident, has_side_effects=True),
-        cost_estimate=pl.CostEstimate(flops=0, bytes_accessed=150_000_000, transcendentals=0),
-        name=f"ring_scatter_{ident}",
-    )(terms)
+        cost_estimate=pl.CostEstimate(
+            flops=2 * tokens * D * D, bytes_accessed=200_000_000, transcendentals=0
+        ),
+        name="gather_residual",
+    )(attended, feed_cut, states, w_out, vectors)
+
+
+class RingSum:
+    def __init__(self, ring, own, sib, got, sems, out):
+        self.ring, self.own, self.sib, self.got, self.out = ring, own, sib, got, out
+        self.ring_s, self.ring_r, self.sib_s, self.sib_r = sems
+        self.piece = own.shape[1] // SUBS
+
+    def clear(self):
+        self.got[0] = jnp.zeros_like(self.got[0])
+
+    def given(self, step, src):
+        return self.ring.copy(
+            src, self.sib.at[step], self.sib_s.at[step], self.sib_r.at[step], self.ring.sibling
+        )
+
+    def passed(self, step, sub):
+        rows = pl.ds(sub * self.piece, self.piece)
+        return self.ring.copy(
+            self.own.at[step].at[rows],
+            self.got.at[step + 1].at[rows],
+            self.ring_s.at[step, sub],
+            self.ring_r.at[step, sub],
+            self.ring.at(1),
+        )
+
+    def advance(self, step):
+        last = self.ring.pairs - 1
+        self.given(step, self.sib.at[step]).wait_recv()
+        for sub in range(SUBS):
+            rows = pl.ds(sub * self.piece, self.piece)
+
+            @pl.when(step > 0)
+            def _():
+                self.passed(step - 1, sub).wait_recv()
+
+            total = self.own[step, rows, :].astype(F32) + self.sib[step, rows, :].astype(F32)
+            total = total + self.got[step, rows, :].astype(F32)
+
+            @pl.when(step < last)
+            def _():
+                self.own[step, rows, :] = total.astype(BF)
+                self.passed(step, sub).start()
+
+            @pl.when(step == last)
+            def _():
+                self.out[rows, :] = total
+
+    def finish(self):
+        @pl.loop(0, self.ring.pairs - 1)
+        def _(step):
+            for sub in range(SUBS):
+                self.passed(step, sub).wait_send()
+
+    @staticmethod
+    def scratch(pairs, rows):
+        return [pltpu.VMEM((pairs, rows, D), BF) for _ in range(3)] + [
+            pltpu.SemaphoreType.DMA((pairs, SUBS)),
+            pltpu.SemaphoreType.DMA((pairs, SUBS)),
+            pltpu.SemaphoreType.DMA((pairs,)),
+            pltpu.SemaphoreType.DMA((pairs,)),
+        ]
+
+
+class Exchange:
+    def __init__(self, ring, count, src, out, sems):
+        self.ring, self.count, self.src, self.out = ring, count, src, out
+        self.send, self.recv, self.own = sems
+
+    def copies(self):
+        ring = self.ring
+        for step in range(1, self.count):
+            device = lax.rem(ring.me + step, self.count)
+            yield ring.copy(
+                self.src.at[device],
+                self.out.at[ring.me],
+                self.send.at[step],
+                self.recv.at[step],
+                device,
+            )
+
+    def start(self):
+        pltpu.make_async_copy(self.src.at[self.ring.me], self.out.at[self.ring.me], self.own).start()
+        for go in self.copies():
+            go.start()
+
+    def finish(self):
+        for go in self.copies():
+            go.wait()
+        pltpu.make_async_copy(self.src.at[self.ring.me], self.out.at[self.ring.me], self.own).wait()
+
+    @staticmethod
+    def scratch(count):
+        return [pltpu.SemaphoreType.DMA((count,)) for _ in range(2)] + [pltpu.SemaphoreType.DMA]
+
+
+class GroupSum:
+    def __init__(self, ring, groups, sent, came, sems, out):
+        self.ring, self.groups, self.sent, self.came, self.out = ring, groups, sent, came, out
+        self.send, self.recv = sems
+        self.tiles, self.each = D // ROWS, D // ROWS // groups
+
+    def group(self, tile):
+        return lax.rem(self.ring.batch + 1 + tile // self.each, self.groups)
+
+    def column(self, tile):
+        return (self.group(tile) * self.each + lax.rem(tile, self.each)) * ROWS
+
+    def copy(self, tile):
+        return pltpu.make_async_remote_copy(
+            src_ref=self.sent.at[tile],
+            dst_ref=self.came.at[tile],
+            send_sem=self.send.at[tile],
+            recv_sem=self.recv.at[tile],
+            device_id=(self.group(tile), self.ring.me),
+            device_id_type=MESH,
+        )
+
+    def put(self, tile, values):
+        away = self.tiles - self.each
+
+        @pl.when(tile < away)
+        def _():
+            self.sent[tile] = values.astype(BF)
+            self.copy(tile).start()
+
+        @pl.when(tile >= away)
+        def _():
+            self.out[tile - away] = values.astype(BF)
+
+    def finish(self):
+        @pl.loop(0, self.each)
+        def _(tile):
+            total = self.out[tile].astype(F32)
+            for shift in range(self.groups - 1):
+                self.copy(shift * self.each + tile).wait_recv()
+                total = total + self.came[shift * self.each + tile].astype(F32)
+            self.out[tile] = total.astype(BF)
+
+        @pl.loop(0, self.tiles - self.each)
+        def _(tile):
+            self.copy(tile).wait_send()
+
+    @staticmethod
+    def scratch(groups, width):
+        away = D // ROWS - D // ROWS // groups
+        return [pltpu.VMEM((away, ROWS, width), BF) for _ in range(2)] + [
+            pltpu.SemaphoreType.DMA((away,)) for _ in range(2)
+        ]
+
+
+def feed_kernel(
+    count, groups, span, b_ref, cot_ref, w_ref, db_ref, out_ref, grad_ref, bs, cs, stage, h, du, tiles, *rest
+):
+    ring = Ring(count)
+    own = db_ref.shape[0]
+    sums = [
+        RingSum(ring, *rest[7 * i : 7 * i + 3], rest[7 * i + 3 : 7 * i + 7], ref)
+        for i, ref in enumerate((db_ref, out_ref))
+    ]
+    grads = GroupSum(ring, groups, rest[14], rest[15], rest[16:18], grad_ref)
+    row_sem, tile_sem = rest[18:]
+    pairs = ring.pairs
+
+    def places(step):
+        return ring.at(-1 - step) * own, ring.at(1 + step, 1 - ring.core) * own
+
+    def row_loads(step):
+        slot = lax.rem(step, 2)
+        return [
+            pltpu.make_async_copy(
+                ref.at[pl.ds(pl.multiple_of(place, own), own)],
+                held.at[slot, pl.ds(half * own, own)],
+                row_sem.at[slot, 2 * which + half],
+            )
+            for which, (ref, held) in enumerate(((b_ref, bs), (cot_ref, cs)))
+            for half, place in enumerate(places(step))
+        ]
+
+    def tile_loads(tile):
+        slot = lax.rem(tile, 2)
+        cols = pl.ds(pl.multiple_of(grads.column(tile), ROWS), ROWS)
+        return [
+            pltpu.make_async_copy(ref.at[:, cols], tiles.at[slot, which], tile_sem.at[slot, which])
+            for which, ref in enumerate((b_ref, cot_ref))
+        ]
+
+    for go in row_loads(0):
+        go.start()
+    ring.greet_groups(groups)
+    for each in sums:
+        each.clear()
+
+    def feed(step):
+        slot = lax.rem(step, 2)
+
+        @pl.when(step + 1 < pairs)
+        def _():
+            for go in row_loads(step + 1):
+                go.start()
+
+        for go in row_loads(step):
+            go.wait()
+        gate = nn(bs[slot], w_ref[:, :span])
+        up = nn(bs[slot], w_ref[:, span : 2 * span])
+        slope = nn(cs[slot], w_ref[:, 2 * span :])
+        coef = math.sqrt(2.0 / math.pi)
+        square = gate * gate
+        tanh = jnp.tanh(coef * gate * (1.0 + 0.044715 * square))
+        half = 0.5 * (1.0 + tanh)
+        gelu = gate * half
+        gelu_slope = half + 0.5 * gate * (1.0 - tanh * tanh) * (coef * (1.0 + 3 * 0.044715 * square))
+        hidden = (gelu * up).astype(BF)
+        both = jnp.concatenate([slope * up * gelu_slope, slope * gelu], axis=1).astype(BF)
+        for part, place in enumerate(places(step)):
+            rows = pl.ds(pl.multiple_of(place, own), own)
+            h[rows, :] = hidden[part * own : (part + 1) * own]
+            du[rows, :] = both[part * own : (part + 1) * own]
+
+        @pl.when(step >= 2)
+        def _():
+            for which, each in enumerate(sums):
+                each.given(step - 2, stage.at[slot, which]).wait_send()
+
+        wide = 512
+        for which, (each, left, low, high) in enumerate(
+            ((sums[0], both, 0, 2 * span), (sums[1], hidden, 2 * span, 3 * span))
+        ):
+            for at in range(0, D, wide):
+                terms = nt(left, w_ref[at : at + wide, low:high]).astype(BF)
+                each.own[step, :, at : at + wide] = terms[:own]
+                stage[slot, which, :, at : at + wide] = terms[own:]
+            each.given(step, stage.at[slot, which]).start()
+
+    @pl.loop(0, pairs)
+    def _(step):
+        feed(step)
+
+        @pl.when(lax.rem(step, 2) == 0)
+        def _():
+            sums[0].advance(step // 2)
+
+    for go in tile_loads(0):
+        go.start()
+
+    @pl.loop(0, grads.tiles)
+    def _(tile):
+        slot = lax.rem(tile, 2)
+
+        @pl.when(tile + 1 < grads.tiles)
+        def _():
+            for go in tile_loads(tile + 1):
+                go.start()
+
+        for go in tile_loads(tile):
+            go.wait()
+        values = jnp.concatenate([tn(tiles[slot, 0], du[...]), tn(tiles[slot, 1], h[...])], axis=1)
+        grads.put(tile, values)
+        later = pairs // 2 + tile // 3
+
+        @pl.when((lax.rem(tile, 3) == 1) & (later < pairs))
+        def _():
+            sums[0].advance(later)
+
+    passed = pairs // 2 + len([t for t in range(grads.tiles) if t % 3 == 1])
+
+    @pl.loop(min(passed, pairs), pairs)
+    def _(step):
+        sums[0].advance(step)
+
+    @pl.loop(0, pairs)
+    def _(step):
+        sums[1].advance(step)
+
+    grads.finish()
+    for step in (pairs - 2, pairs - 1):
+        for which, each in enumerate(sums):
+            each.given(step, stage.at[step % 2, which]).wait_send()
+    for each in sums:
+        each.finish()
+
+
+def feed_forward(b_low, cot, w_feed, own, count, groups, ident):
+    tokens, span, pairs = b_low.shape[0], w_feed.shape[1] // 3, count // 2
+    inside, anywhere = pl.BlockSpec(memory_space=pltpu.VMEM), pl.BlockSpec(memory_space=pl.ANY)
+    return pl.pallas_call(
+        functools.partial(feed_kernel, count, groups, span),
+        in_specs=[anywhere, anywhere, inside],
+        out_specs=[inside] * 3,
+        out_shape=[
+            jax.ShapeDtypeStruct((own, D), F32),
+            jax.ShapeDtypeStruct((own, D), F32),
+            jax.ShapeDtypeStruct((D // groups // ROWS, ROWS, 3 * span), BF),
+        ],
+        scratch_shapes=[
+            pltpu.VMEM((2, 2 * own, D), BF),
+            pltpu.VMEM((2, 2 * own, D), BF),
+            pltpu.VMEM((2, 2, own, D), BF),
+            pltpu.VMEM((tokens, span), BF),
+            pltpu.VMEM((tokens, 2 * span), BF),
+            pltpu.VMEM((2, 2, tokens, ROWS), BF),
+        ]
+        + RingSum.scratch(pairs, own) * 2
+        + GroupSum.scratch(groups, 3 * span)
+        + [pltpu.SemaphoreType.DMA((2, 4)), pltpu.SemaphoreType.DMA((2, 2))],
+        compiler_params=vmem(60 * 1024 * 1024, collective_id=ident, has_side_effects=True),
+        cost_estimate=pl.CostEstimate(
+            flops=18 * tokens * D * span, bytes_accessed=250_000_000, transcendentals=0
+        ),
+        name="feed_forward",
+    )(b_low, cot, w_feed)
+
+
+def project_kernel(
+    count,
+    groups,
+    dp_ref,
+    w_ref,
+    a_ref,
+    heads_ref,
+    dr_ref,
+    feed_ref,
+    da_ref,
+    grad_ref,
+    feed_out_ref,
+    stage,
+    tiles,
+    *rest,
+):
+    ring = Ring(count)
+    own = da_ref.shape[0]
+    sums = RingSum(ring, *rest[:3], rest[3:7], da_ref)
+    grads = GroupSum(ring, groups, rest[7], rest[8], rest[9:11], grad_ref)
+    tile_sem = rest[11]
+    feed = Exchange(ring, count, feed_ref, feed_out_ref, rest[12:15])
+    pairs, width = ring.pairs, heads_ref.shape[2]
+
+    def places(step):
+        return ring.at(-1 - step) * own, ring.at(1 + step, 1 - ring.core) * own
+
+    def tile_loads(tile):
+        slot = lax.rem(tile, 2)
+        begin = pl.multiple_of(grads.column(tile), ROWS)
+        loads = [
+            pltpu.make_async_copy(
+                a_ref.at[:, pl.ds(begin, ROWS)], tiles.at[slot, 0], tile_sem.at[slot, 0]
+            )
+        ]
+        for part in range(ROWS // width):
+            loads.append(
+                pltpu.make_async_copy(
+                    heads_ref.at[begin // width + part],
+                    tiles.at[slot, 1, :, pl.ds(part * width, width)],
+                    tile_sem.at[slot, 1 + part],
+                )
+            )
+        return loads
+
+    for go in tile_loads(0):
+        go.start()
+    ring.greet_all(count)
+    feed.start()
+    sums.clear()
+
+    def terms_of(step):
+        slot = lax.rem(step, 2)
+
+        @pl.when(step >= 2)
+        def _():
+            sums.given(step - 2, stage.at[slot]).wait_send()
+
+        left = jnp.concatenate(
+            [dp_ref[pl.ds(pl.multiple_of(place, own), own), :] for place in places(step)], axis=0
+        )
+        wide = 512
+        for at in range(0, D, wide):
+            terms = nt(left, w_ref[at : at + wide, :]).astype(BF)
+            sums.own[step, :, at : at + wide] = terms[:own]
+            stage[slot, :, at : at + wide] = terms[own:]
+        sums.given(step, stage.at[slot]).start()
+
+    terms_of(0)
+    sums.advance(0)
+
+    @pl.loop(0, grads.tiles)
+    def _(tile):
+        slot = lax.rem(tile, 2)
+
+        @pl.when(tile + 1 < grads.tiles)
+        def _():
+            for go in tile_loads(tile + 1):
+                go.start()
+
+        for go in tile_loads(tile):
+            go.wait()
+        values = jnp.concatenate(
+            [tn(tiles[slot, 0], dp_ref[...]), tn(tiles[slot, 1], dr_ref[...])], axis=1
+        )
+        grads.put(tile, values)
+
+        @pl.when(tile + 1 < pairs)
+        def _():
+            terms_of(tile + 1)
+
+        @pl.when((lax.rem(tile, 4) == 3) & (tile // 4 + 1 < pairs))
+        def _():
+            sums.advance(tile // 4 + 1)
+
+    @pl.loop(1 + grads.tiles // 4, pairs)
+    def _(step):
+        sums.advance(step)
+
+    grads.finish()
+    for step in (pairs - 2, pairs - 1):
+        sums.given(step, stage.at[step % 2]).wait_send()
+    sums.finish()
+    feed.finish()
+
+
+def project_back(dp, w_qkv, a_low, heads, dr_cols, grad_feed, own, count, groups, ident):
+    tokens, pairs = dp.shape[0], count // 2
+    width = 3 * HD + dr_cols.shape[1]
+    inside, anywhere = pl.BlockSpec(memory_space=pltpu.VMEM), pl.BlockSpec(memory_space=pl.ANY)
+    return pl.pallas_call(
+        functools.partial(project_kernel, count, groups),
+        in_specs=[inside, inside, anywhere, anywhere, inside, anywhere],
+        out_specs=[inside, inside, anywhere],
+        out_shape=[
+            jax.ShapeDtypeStruct((own, D), F32),
+            jax.ShapeDtypeStruct((D // groups // ROWS, ROWS, width), BF),
+            jax.ShapeDtypeStruct(grad_feed.shape, BF),
+        ],
+        scratch_shapes=[
+            pltpu.VMEM((2, own, D), BF),
+            pltpu.VMEM((2, 2, tokens, ROWS), BF),
+        ]
+        + RingSum.scratch(pairs, own)
+        + GroupSum.scratch(groups, width)
+        + [pltpu.SemaphoreType.DMA((2, 1 + ROWS // HD))]
+        + Exchange.scratch(count),
+        compiler_params=vmem(collective_id=ident, has_side_effects=True),
+        cost_estimate=pl.CostEstimate(
+            flops=4 * tokens * D * 3 * HD, bytes_accessed=200_000_000, transcendentals=0
+        ),
+        name="project_back",
+    )(dp, w_qkv, a_low, heads, dr_cols, grad_feed)
 
 
 def norm_parts(values):
@@ -509,92 +1039,6 @@
         ),
         name="attend_back",
     )(low, high, query, grad, full, log, cut(key), cut(value), first, last, cosine, sine)
-
-
-def residual_kernel(x_ref, heads_ref, w_ref, vec_ref, b_ref, own_ref):
-    tokens = own_ref.shape[0]
-    block = pl.program_id(0)
-    normal, _ = norm_parts(x_ref[...].astype(F32))
-    attended = jnp.concatenate([heads_ref[h] for h in range(heads_ref.shape[0])], axis=1)
-    residual = DEEP_ALPHA * (normal * vec_ref[0:1, :] + vec_ref[1:2, :]) + nn(
-        attended, w_ref[...]
-    )
-    second, _ = norm_parts(residual)
-    b_ref[...] = (second * vec_ref[2:3, :] + vec_ref[3:4, :]).astype(BF)
-    me = lax.axis_index("seq")
-    for part in range(ROWS // tokens):
-
-        @pl.when(block * (ROWS // tokens) + part == me)
-        def _():
-            own_ref[...] = residual[part * tokens : (part + 1) * tokens, :]
-
-
-def residual_norm(states, heads, w_out, vectors, own_rows):
-    tokens = states.shape[0]
-    whole = lambda shape: pl.BlockSpec(shape, lambda i: (0,) * len(shape))
-    rows = pl.BlockSpec((ROWS, D), lambda i: (i, 0))
-    return pl.pallas_call(
-        residual_kernel,
-        grid=(tokens // ROWS,),
-        in_specs=[
-            rows,
-            pl.BlockSpec((heads.shape[0], ROWS, HD), lambda i: (0, i, 0)),
-            whole((D, D)),
-            whole(vectors.shape),
-        ],
-        out_specs=[rows, whole((own_rows, D))],
-        out_shape=[
-            jax.ShapeDtypeStruct((tokens, D), BF),
-            jax.ShapeDtypeStruct((own_rows, D), F32),
-        ],
-        compiler_params=vmem(),
-        cost_estimate=pl.CostEstimate(
-            flops=2 * tokens * D * D, bytes_accessed=32_000_000, transcendentals=0
-        ),
-        name="residual_norm",
-    )(states, heads, w_out, vectors)
-
-
-def feed_kernel(b_ref, cot_ref, w_ref, h_ref, du_ref, out_ref, db_ref):
-    span = h_ref.shape[1]
-    b, cot = b_ref[...], cot_ref[...]
-    gate = nn(b, w_ref[:, :span])
-    up = nn(b, w_ref[:, span : 2 * span])
-    slope = nn(cot, w_ref[:, 2 * span :])
-    coef = math.sqrt(2.0 / math.pi)
-    square = gate * gate
-    tanh = jnp.tanh(coef * gate * (1.0 + 0.044715 * square))
-    half = 0.5 * (1.0 + tanh)
-    gelu = gate * half
-    gelu_slope = half + 0.5 * gate * (1.0 - tanh * tanh) * (
-        coef * (1.0 + 3 * 0.044715 * square)
-    )
-    hidden = (gelu * up).astype(BF)
-    h_ref[...] = hidden
-    du = jnp.concatenate([slope * up * gelu_slope, slope * gelu], axis=1).astype(BF)
-    du_ref[...] = du
-    out_ref[...] = nt(hidden, w_ref[:, 2 * span :]).astype(BF)
-    db_ref[...] = nt(du, w_ref[:, : 2 * span]).astype(BF)
-
-
-def feed_forward(b_low, cot, w_feed):
-    tokens = b_low.shape[0]
-    span = w_feed.shape[1] // 3
-    rows = lambda width: pl.BlockSpec((ROWS, width), lambda i: (i, 0))
-    return pl.pallas_call(
-        feed_kernel,
-        grid=(tokens // ROWS,),
-        in_specs=[rows(D), rows(D), pl.BlockSpec(w_feed.shape, lambda i: (0, 0))],
-        out_specs=[rows(span), rows(2 * span), rows(D), rows(D)],
-        out_shape=[
-            jax.ShapeDtypeStruct((tokens, width), BF) for width in (span, 2 * span, D, D)
-        ],
-        compiler_params=vmem(),
-        cost_estimate=pl.CostEstimate(
-            flops=12 * tokens * D * span, bytes_accessed=48_000_000, transcendentals=0
-        ),
-        name="feed_forward",
-    )(b_low, cot, w_feed)
 
 
 def windows(at, span, count):
@@ -777,12 +1221,8 @@
     return functools.reduce(lambda total, part: total + part.astype(F32), arrived, own())
 
 
-def rows_of(grad_rows):
-    seq = lax.axis_size("seq")
-    total = over_batch(
-        lambda there: grad_rows(there).astype(BF), lambda: grad_rows(lax.axis_index("batch"))
-    )
-    blocks = total.astype(BF).reshape(seq, -1, total.shape[1])
+def to_rows(grad):
+    blocks = grad.reshape(lax.axis_size("seq"), -1, grad.shape[-1])
     return lax.all_to_all(blocks, "seq", split_axis=0, concat_axis=0, tiled=True)
 
 
@@ -817,13 +1257,12 @@
     cosine, sine = rotary_tables(place)
     a_low, query, key, value = norm_and_project(states, w_qkv, vectors, cosine, sine)
     attended, full, log = attend(query, key, value, spans)
-    heads, w_feed = ring_gather(attended, [feed_cut], seq, 2)
+    heads, w_feed, b_low, residual = gather_residual(
+        attended, feed_cut, states, w_out, vectors, own, seq, 2
+    )
     w_feed = w_feed.reshape(D, 3 * span)
-    b_low, residual = residual_norm(states, heads, w_out, vectors, own)
-    hidden, du, out_terms, db_terms = feed_forward(b_low, cot_all, w_feed)
-
-    db_sum = ring_scatter(db_terms.reshape(seq, own, D), seq, 3)
-    out_sum = lax.psum_scatter(out_terms, "seq", scatter_dimension=0, tiled=True)
+    db_sum, out_sum, grad_feed = feed_forward(b_low, cot_all, w_feed, own, seq, groups, 3)
+    grad_feed = grad_feed.reshape(seq, rows, 3 * span)
     gain_one, bias_one, gain_two, bias_two = (vectors[i][None, :] for i in range(4))
 
     def norm_back(normal, inverse, slope, gain):
@@ -836,7 +1275,7 @@
         return back, jnp.stack([jnp.sum(slope * normal, axis=0), jnp.sum(slope, axis=0)])
 
     normal_two, inverse_two = norm_parts(residual)
-    output = DEEP_ALPHA * (normal_two * gain_two + bias_two) + out_sum.astype(F32)
+    output = DEEP_ALPHA * (normal_two * gain_two + bias_two) + out_sum
     db = DEEP_ALPHA * cotangent.astype(F32) + db_sum
     dr, sums_two = norm_back(normal_two, inverse_two, db, gain_two)
     dr_low = dr.astype(BF)
@@ -847,27 +1286,12 @@
     do_head = to_heads(do)
     dr_cols = to_heads(dr_low)
 
-    def row_part(values, place):
-        return lax.dynamic_slice_in_dim(values, place * (D // groups), D // groups, 1)
-
-    grad_feed = rows_of(
-        lambda place: jnp.concatenate(
-            [tn(row_part(b_low, place), du), tn(row_part(cot_all, place), hidden)], axis=1
-        )
+    dp = attend_back(query, key, value, do_head, full, log, spans, cosine, sine)
+    da_sum, grad_attn, grad_feed = project_back(
+        dp, w_qkv, a_low, heads, dr_cols, grad_feed, own, seq, groups, 4
     )
-    dp = attend_back(query, key, value, do_head, full, log, spans, cosine, sine)
-    da_terms = nt(dp, w_qkv).astype(BF)
-    da_sum = ring_scatter(da_terms.reshape(seq, own, D), seq, 5)
-    grad_out = jnp.einsum("htd,tn->hdn", heads, dr_cols, preferred_element_type=F32).reshape(D, HD)
-    grad_attn = rows_of(
-        lambda place: jnp.concatenate(
-            [
-                tn(row_part(a_low, place), dp),
-                lax.dynamic_slice_in_dim(grad_out, place * (D // groups), D // groups, 0),
-            ],
-            axis=1,
-        )
-    )
+    grad_attn = to_rows(grad_attn)
+
     normal_one, inverse_one = norm_parts(hidden_in.astype(F32))
     da = DEEP_ALPHA * dr + da_sum
     input_grad, sums_one = norm_back(normal_one, inverse_one, da, gain_one)

time: 720 us -> 645 us (0.90)
  matrix products: 52.8 us -> 6.32 us
  local copies, waits for them, and re-layouts: 26.9 us -> 8.71 us
  waiting for transfers between devices: 46.8 us -> 32.2 us
  blocking collectives: 0 us -> 11.4 us
  starting transfers between devices: 28.4 us -> 20.5 us
    pallas_call x4 -> x3, Pallas kernels: 187 us -> 333 us  [the longest x1 124 us: gather_residual(): pl.pallas_call(functools.partial(residual_kernel, count), out_shape=[jax....]
    pallas_call x2 -> x1, Pallas kernels: 250 us -> 110 us  [ring_gather(): pl.pallas_call(functools.partial(gather_kernel, count, len(blocks)), out_...]
    dot_general x7 -> x0, matrix products: 39.5 us -> none  [the longest x6 33.2 us: tn(): lax.dot_general(left, right, (((0,), (0,)), ((), ())), preferred_element_...]
    reduce_scatter x1 -> x0, waiting for transfers between devices: 22 us -> none  [on_device(): lax.psum_scatter(out_terms, 'seq', scatter_dimension=0, tiled=True)]
    dot_general x1 -> x0, local copies, waits for them, and re-layouts: 12.4 us -> none  [on_device(): jnp.einsum('htd,tn->hdn', heads, dr_cols, preferred_element_type=F32)]
    all_to_all x2, waiting for transfers between devices: 1.25 us -> 13.2 us  [on_device(): lax.all_to_all(values.reshape(own, seq, HD).transpose(1, 0, 2), 'seq', sp...]
    all_to_all x0 -> x1, blocking collectives: none -> 11.4 us  [vector_rows(): came = lax.all_to_all(cut, 'seq', split_axis=0, concat_axis=0, tiled=True)]
    all_to_all x3 -> x1, starting transfers between devices: 15 us -> 5.18 us  [to_rows(): lax.all_to_all(blocks, 'seq', split_axis=0, concat_axis=0, tiled=True)]
  transfers between devices with their start and end apart: 11 -> 6, of which waited for: 5 -> 2; matrix products, arithmetic and copies ran while one was open for 15% -> 3% of each run, Pallas kernels for 64% -> 45%
where the time goes in v2:
time: 645 us; the launch traced here: 636 us
  Pallas kernels  523 us (81%)
  waiting for transfers between devices  32.2 us (5%)
  starting transfers between devices  20.5 us (3%)
  other arithmetic  19.6 us (3%)
  between operations  14.5 us (2%)
  blocking collectives  11.4 us (2%)
  local copies, waits for them, and re-layouts  8.71 us (1%)
    pallas_call x1, Pallas kernels, gather_residual(): pl.pallas_call(functools.partial(residual_kernel, count), out_shape=[jax....  124 us
    pallas_call x1, Pallas kernels, ring_gather(): pl.pallas_call(functools.partial(gather_kernel, count, len(blocks)), out_...  110 us
    pallas_call x1, Pallas kernels, feed_forward(): pl.pallas_call(functools.partial(feed_kernel, count, groups, span), in_sp...  106 us
    pallas_call x1, Pallas kernels, project_back(): pl.pallas_call(functools.partial(project_kernel, count, groups), in_specs...  104 us
    pallas_call x1, Pallas kernels, update(): pl.pallas_call(functools.partial(update_kernel, count, span), grid=(steps...  23.1 us
    pallas_call x1, Pallas kernels, attend_back(): pl.pallas_call(attend_back_kernel, grid_spec=pltpu.PrefetchScalarGridSpec...  20.4 us
    all_to_all x1, waiting for transfers between devices, to_rows(): lax.all_to_all(blocks, 'seq', split_axis=0, concat_axis=0, tiled=True)  18.3 us
    pallas_call x1, Pallas kernels, attend(): pl.pallas_call(attend_kernel, grid_spec=pltpu.PrefetchScalarGridSpec(num_...  16.2 us
  transfers between devices with their start and end apart: 6, of which 2 were waited for; matrix products, arithmetic and copies ran while one was open for 3% of the time, Pallas kernels for 45%

profile of v2, /device:TPU:9, one launch (start us, length us, event | category | flops | bytes accessed | tf_op | source)
XLA Modules:
  0.0 636.1 jit_solution(14939318571675621880)
XLA Ops:
  7.2 0.0 all-gather.3.cloned.1.call-start
  7.2 5.1 lay_out.1
  12.3 0.0 all-gather.3.cloned.1.call-update
  12.4 0.0 all-gather.5.cloned.1.call-start
  12.4 0.7 all-gather.5.cloned.1.call-update
  13.1 0.9 slice.41
  14.0 0.1 copy.49
  14.1 0.6 bitcast_convert_fusion.refs_1_
  14.7 110.2 %ring_gather_1.1 = (bf16[16,128,2048]{2,1,0:T(8,128)(2,1)}, bf16[2,16,64,384]{3,2,1,0:T(8,128)(2,1)}, f32[2,16,8,128]{3,2,1,0:T(8,128)}) custom-call(bf16[128,2048]{1,0:T(8,128)(2,1)} %x_ref.1, bf16[16,64,384]{2,1,0:T(8,128)(2,1)} %get-tuple-element.33.refs_0_, f32[1,8,128]{2,1,0:T(8,128)} %bitcast_convert_fusion.refs_1_), custom_call_target="tpu_custom_call" | custom-call | bytes 150000000 | tf_op jit(solution)/shard_map/ring_gather_1/pallas_call | solution.py:235
  124.9 0.9 slice_bitcast_fusion
  125.9 0.7 reshape.192.vec_ref
  126.6 0.2 reduce-window.4
  126.8 0.2 select_reduce_fusion
  126.9 0.1 slice.25
  127.0 0.1 slice.26
  127.1 0.1 slice_reduce_fusion
  127.3 0.1 mul.116
  127.3 0.1 add.69
  127.4 0.6 and_select_fusion
  128.0 0.6 compare_select_fusion.1.first_ref
  128.7 3.7 fusion.12
  132.4 1.9 pad_maximum_fusion
  134.3 14.4 %norm_and_project.1 = (bf16[2048,2048]{1,0:T(8,128)(2,1)}, bf16[2048,128]{1,0:T(8,128)(2,1)}, bf16[2048,128]{1,0:T(8,128)(2,1)}, bf16[2048,128]{1,0:T(8,128)(2,1)}) custom-call(bf16[2048,2048]{1,0:T(8,128)(2,1)} %bitcast.63, bf16[2048,384]{1,0:T(8,128)(2,1)} %bitcast.65, f32[8,2048]{1,0:T(8,128)} %reshape.192.vec_ref, ...), custom_call_target="tpu_custom_call" | custom-call | flops 3221225472 | bytes 24000000 | tf_op jit(solution)/shard_map/norm_and_project/pallas_call | solution.py:875
  148.7 16.2 %attend.1 = (bf16[2048,128]{1,0:T(8,128)(2,1)}, f32[2048,128]{1,0:T(8,128)}, f32[2048,128]{1,0:T(8,128)}) custom-call(s32[8]{0:T(128)} %get-tuple-element.87.low_ref, s32[8]{0:T(128)} %get-tuple-element.86.high_ref, bf16[2048,128]{1,0:T(8,128)(2,1)} %get-tuple-element.37.q_ref, bf16[8,256,128]{2,1,0:T(8,128)(2,1)} %bitcast.81, ...), custom_call_target="tpu_custom_call" | custom-call | flops 1073741824 | bytes 4000000 | tf_op jit(solution)/shard_map/attend/pallas_call | solution.py:932
  164.9 123.6 %gather_residual.1 = (bf16[16,2048,128]{2,1,0:T(8,128)(2,1)}, bf16[2,16,64,1152]{3,2,1,0:T(8,128)(2,1)}, bf16[2048,2048]{1,0:T(8,128)(2,1)}, f32[128,2048]{1,0:T(8,128)}) custom-call(bf16[2048,128]{1,0:T(8,128)(2,1)} %get-tuple-element.40.x_ref, bf16[16,64,1152]{2,1,0:T(8,128)(2,1)} %get-tuple-element.41.part_ref, bf16[2048,2048]{1,0:T(8,128)(2,1)} %bitcast.64, ...), custom_call_target="tpu_custom_call" | custom-call | flops 17179869184 | bytes 200000000 | tf_op jit(solution)/shard_map/gather_residual/pallas_call | solution.py:376
  288.5 1.4 reduce_sum.166
  289.9 1.5 multiply_reduce_fusion.2
  291.4 0.0 all-gather.5.cloned.1.call-done.cot_ref
  291.4 0.0 copy-start.2
  291.5 105.9 %feed_forward.1 = (f32[128,2048]{1,0:T(8,128)}, f32[128,2048]{1,0:T(8,128)}, bf16[4,256,1152]{2,1,0:T(8,128)(2,1)}) custom-call(bf16[2048,2048]{1,0:T(8,128)(2,1)} %get-tuple-element.44.b_ref, bf16[2048,2048]{1,0:T(8,128)(2,1)} %all-gather.5.cloned.1.call-done.cot_ref, bf16[2048,1152]{1,0:T(8,128)(2,1)} %bitcast.85), custom_call_target="tpu_custom_call" | custom-call | flops 28991029248 | bytes 250000000 | tf_op jit(solution)/shard_map/feed_forward/pallas_call | solution.py:690
  397.4 1.8 multiply_reduce_fusion
  399.1 3.0 convert_bitcast_fusion
  402.1 6.3 fusion.5
  408.5 0.9 copy.56
  409.4 7.4 %all-to-all-start = ((bf16[16,128,128]{2,1,0:T(8,128)(2,1)}), bf16[16,128,128]{2,1,0:T(8,128)(2,1)S(1)}, u32[]{:S(2)}, u32[]{:S(2)}) async-start(bf16[16,128,128]{2,1,0:T(8,128)(2,1)} %bitcast.61), calls=%async_computation | async-start | bytes 1048576 | tf_op jit(solution)/shard_map/all_to_all | solution.py:1283
  416.8 0.1 mul.129
  416.9 0.9 copy.55
  417.8 13.2 %all-to-all-done = bf16[16,128,128]{2,1,0:T(8,128)(2,1)S(1)} async-done(((bf16[16,128,128]{2,1,0:T(8,128)(2,1)}), bf16[16,128,128]{2,1,0:T(8,128)(2,1)S(1)}, u32[]{:S(2)}, u32[]{:S(2)}) %all-to-all-start) | async-done | bytes 524320 | tf_op jit(solution)/shard_map/all_to_all | solution.py:1283
  431.0 4.7 all-to-all-start.1
  435.7 0.2 convert_reduce_fusion
  435.8 0.3 fusion.11
  436.1 0.1 concatenate.22
  436.2 0.1 concatenate.23
  436.3 20.4 %attend_back.1.dp_ref = bf16[2048,384]{1,0:T(8,128)(2,1)} custom-call(s32[8]{0:T(128)} %get-tuple-element.87.low_ref, s32[8]{0:T(128)} %get-tuple-element.86.high_ref, bf16[2048,128]{1,0:T(8,128)(2,1)} %get-tuple-element.37.q_ref, bf16[2048,128]{1,0:T(8,128)(2,1)} %bitcast.69, f32[2048,128]{1,0:T(8,128)} %get-tuple-element.48.full_ref, ...), custom_call_target="tpu_custom_call" | custom-call | flops 2684354560 | bytes 6000000 | tf_op jit(solution)/shard_map/attend_back/pallas_call | solution.py:1023
  456.7 0.0 copy-start.4
  456.7 0.8 copy-done.4
  457.5 103.9 %project_back.1 = (f32[128,2048]{1,0:T(8,128)}, bf16[4,256,512]{2,1,0:T(8,128)(2,1)}, bf16[16,64,1152]{2,1,0:T(8,128)(2,1)}) custom-call(bf16[2048,384]{1,0:T(8,128)(2,1)} %attend_back.1.dp_ref, bf16[2048,384]{1,0:T(8,128)(2,1)} %bitcast.66, bf16[2048,2048]{1,0:T(8,128)(2,1)} %get-tuple-element.50.a_ref, bf16[16,2048,128]{2,1,0:T(8,128)(2,1)} %get-tuple-element.51.heads_ref, ...), custom_call_target="tpu_custom_call" | custom-call | flops 6442450944 | bytes 200000000 | tf_op jit(solution)/shard_map/project_back/pallas_call | solution.py:828
  561.4 1.8 fusion.10
  563.1 0.1 concatenate.20
  563.2 0.1 concatenate.21
  563.3 0.1 reshape.221
  563.4 11.4 %all_to_all.20 = f32[16,1,512]{2,1,0:T(1,128)S(1)} all-to-all(f32[16,1,512]{2,1,0:T(1,128)S(1)} %reshape.221), channel_id=1, replica_groups=mesh['batch'=2,'seq'=16] {'seq'}, dimensions={0} | all-to-all | bytes 65536 | tf_op jit(solution)/shard_map/all_to_all | solution.py:1234
  574.9 5.2 all-to-all-start.2
  580.1 0.5 broadcast.175
  580.6 0.7 reduce.12
  581.3 0.1 reshape.222
  581.5 0.1 copy.48
  581.6 3.1 collective-permute-start
  584.7 1.2 fusion.9
  585.9 0.1 copy.47
  586.0 0.6 pad.10.vec_ref
  586.6 18.3 %all-to-all-done.2.attn_ref = bf16[16,64,512]{2,1,0:T(8,128)(2,1)S(1)} async-done(((bf16[16,64,512]{2,1,0:T(8,128)(2,1)}), bf16[16,64,512]{2,1,0:T(8,128)(2,1)S(1)}, u32[]{:S(2)}, u32[]{:S(2)}) %all-to-all-start.2) | async-done | bytes 1048608 | tf_op jit(solution)/shard_map/all_to_all | solution.py:1226
  604.9 1.0 copy-done.3
  605.9 23.1 %update.1 = (f32[64,24579]{1,0:T(8,128)}, f32[64,24579]{1,0:T(8,128)}, f32[64,24579]{1,0:T(8,128)}, f32[64,24579]{1,0:T(8,128)}) custom-call(bf16[16,64,512]{2,1,0:T(8,128)(2,1)} %copy-done.3, bf16[16,64,1152]{2,1,0:T(8,128)(2,1)} %get-tuple-element.55.feed_ref, f32[64,128]{1,0:T(8,128)} %pad.10.vec_ref, f32[64,24579]{1,0:T(8,128)} %m_ref.3, ...), custom_call_target="tpu_custom_call" | custom-call | bytes 56000000 | tf_op jit(solution)/shard_map/update/pallas_call | solution.py:1172
  (36 shorter events, 0.2 us)
Async XLA Ops:
  7.2 119.4 %copy-start.8 = (s32[1,4]{1,0:T(1,128)S(1)}, s32[1,4]{1,0:T(1,128)}, u32[]{:S(2)}) copy-start(s32[1,4]{1,0:T(1,128)} %param.15) | copy-start | bytes 52
  7.2 119.6 %copy-start.9 = (s32[1,4]{1,0:T(1,128)S(1)}, s32[1,4]{1,0:T(1,128)}, u32[]{:S(2)}) copy-start(s32[1,4]{1,0:T(1,128)} %param.17) | copy-start | bytes 52
  7.2 119.6 %copy-start.7 = (s32[1,4]{1,0:T(1,128)S(1)}, s32[1,4]{1,0:T(1,128)}, u32[]{:S(2)}) copy-start(s32[1,4]{1,0:T(1,128)} %param.16) | copy-start | bytes 52
  7.2 157.7 %all-gather.3.cloned.1.call-start = ((), (), s32[]{:S(2)}) async-start(), calls=%async_computation.4 | async-start | bytes 8650752 | tf_op jit(solution)/shard_map/all_gather | solution.py:1253
  12.4 279.1 %all-gather.5.cloned.1.call-start = ((), (), s32[]{:S(2)}) async-start(), calls=%async_computation.5 | async-start | bytes 8912896 | tf_op jit(solution)/shard_map/all_gather | solution.py:1254
  126.9 21.8 %copy-start.6 = (s32[2048]{0:T(1024)}, s32[2048]{0:T(1024)S(1)}, u32[]{:S(2)}) copy-start(s32[2048]{0:T(1024)S(1)} %get-tuple-element.73) | copy-start | bytes 24580
  291.4 105.9 %copy-start = (f32[128,2048]{1,0:T(8,128)S(1)}, f32[128,2048]{1,0:T(8,128)}, u32[]{:S(2)}) copy-start(f32[128,2048]{1,0:T(8,128)} %get-tuple-element.43) | copy-start | bytes 3145732
  291.4 105.9 %copy-start.2 = (bf16[128,2048]{1,0:T(8,128)(2,1)S(1)}, bf16[128,2048]{1,0:T(8,128)(2,1)}, u32[]{:S(2)}) copy-start(bf16[128,2048]{1,0:T(8,128)(2,1)} %param.10) | copy-start | bytes 1572868
  402.1 33.5 %copy-start.1 = (bf16[128,2048]{1,0:T(8,128)(2,1)S(1)}, bf16[128,2048]{1,0:T(8,128)(2,1)}, u32[]{:S(2)}) copy-start(bf16[128,2048]{1,0:T(8,128)(2,1)} %x_ref.1) | copy-start | bytes 1572868
  409.4 21.6 %all-to-all-start = ((bf16[16,128,128]{2,1,0:T(8,128)(2,1)}), bf16[16,128,128]{2,1,0:T(8,128)(2,1)S(1)}, u32[]{:S(2)}, u32[]{:S(2)}) async-start(bf16[16,128,128]{2,1,0:T(8,128)(2,1)} %bitcast.61), calls=%async_computation | async-start | bytes 1048576 | tf_op jit(solution)/shard_map/all_to_all | solution.py:1283
  431.0 5.3 copy-start.5
  431.0 25.7 %all-to-all-start.1 = ((bf16[16,128,128]{2,1,0:T(8,128)(2,1)}), bf16[16,128,128]{2,1,0:T(8,128)(2,1)S(1)}, u32[]{:S(2)}, u32[]{:S(2)}) async-start(bf16[16,128,128]{2,1,0:T(8,128)(2,1)} %bitcast.59), calls=%async_computation.1 | async-start | bytes 1048576 | tf_op jit(solution)/shard_map/all_to_all | solution.py:1283
  456.7 0.8 copy-start.4
  574.9 30.1 %all-to-all-start.2 = ((bf16[16,64,512]{2,1,0:T(8,128)(2,1)}), bf16[16,64,512]{2,1,0:T(8,128)(2,1)S(1)}, u32[]{:S(2)}, u32[]{:S(2)}) async-start(bf16[16,64,512]{2,1,0:T(8,128)(2,1)} %bitcast.67), calls=%async_computation.2 | async-start | bytes 2097152 | tf_op jit(solution)/shard_map/all_to_all | solution.py:1226
  581.6 4.4 collective-permute-start
  604.9 1.0 copy-start.3
Sparse Core Ops, SparseCore 0:
  12.5 94.6 all-gather.2
  109.4 82.9 all-gather.4

commit v3 on v2

--- a/solution.py
+++ b/solution.py
@@ -30,6 +30,7 @@
 F32 = jnp.float32
 MESH = pl.DeviceIdType.MESH
 ROWS = 256
+KEYS = 512
 LANES = 128
 SUBS = 4
 VMEM_BIG = 56 * 1024 * 1024
@@ -85,6 +86,15 @@
             group = lax.rem(self.batch + shift, groups)
             pl.semaphore_signal(barrier, inc=1, device_id=(group, self.me), device_id_type=MESH)
         pl.semaphore_wait(barrier, 1 + groups)
+
+    def greet_whole(self, count):
+        barrier = pltpu.get_barrier_semaphore()
+        total = count * lax.axis_size("batch")
+        for step in range(1, total):
+            flat = lax.rem(self.batch * count + self.me + step, total)
+            there = (flat // count, lax.rem(flat, count))
+            pl.semaphore_signal(barrier, inc=1, device_id=there, device_id_type=MESH)
+        pl.semaphore_wait(barrier, total - 1)
 
     def copy(self, src, dst, send, recv, device):
         return pltpu.make_async_remote_copy(
@@ -410,9 +420,6 @@
         self.ring_s, self.ring_r, self.sib_s, self.sib_r = sems
         self.piece = own.shape[1] // SUBS
 
-    def clear(self):
-        self.got[0] = jnp.zeros_like(self.got[0])
-
     def given(self, step, src):
         return self.ring.copy(
             src, self.sib.at[step], self.sib_s.at[step], self.sib_r.at[step], self.ring.sibling
@@ -422,7 +429,7 @@
         rows = pl.ds(sub * self.piece, self.piece)
         return self.ring.copy(
             self.own.at[step].at[rows],
-            self.got.at[step + 1].at[rows],
+            self.got.at[step].at[rows],
             self.ring_s.at[step, sub],
             self.ring_r.at[step, sub],
             self.ring.at(1),
@@ -434,21 +441,28 @@
         for sub in range(SUBS):
             rows = pl.ds(sub * self.piece, self.piece)
 
+            total = self.own[step, rows, :].astype(F32) + self.sib[step, rows, :].astype(F32)
+
+            @pl.when(step == 0)
+            def _():
+                self.own[step, rows, :] = total.astype(BF)
+
             @pl.when(step > 0)
             def _():
                 self.passed(step - 1, sub).wait_recv()
-
-            total = self.own[step, rows, :].astype(F32) + self.sib[step, rows, :].astype(F32)
-            total = total + self.got[step, rows, :].astype(F32)
+                more = total + self.got[step - 1, rows, :].astype(F32)
+
+                @pl.when(step < last)
+                def _():
+                    self.own[step, rows, :] = more.astype(BF)
+
+                @pl.when(step == last)
+                def _():
+                    self.out[rows, :] = more
 
             @pl.when(step < last)
             def _():
-                self.own[step, rows, :] = total.astype(BF)
                 self.passed(step, sub).start()
-
-            @pl.when(step == last)
-            def _():
-                self.out[rows, :] = total
 
     def finish(self):
         @pl.loop(0, self.ring.pairs - 1)
@@ -458,7 +472,7 @@
 
     @staticmethod
     def scratch(pairs, rows):
-        return [pltpu.VMEM((pairs, rows, D), BF) for _ in range(3)] + [
+        return [pltpu.VMEM((pairs - late, rows, D), BF) for late in (0, 0, 1)] + [
             pltpu.SemaphoreType.DMA((pairs, SUBS)),
             pltpu.SemaphoreType.DMA((pairs, SUBS)),
             pltpu.SemaphoreType.DMA((pairs,)),
@@ -498,6 +512,44 @@
         return [pltpu.SemaphoreType.DMA((count,)) for _ in range(2)] + [pltpu.SemaphoreType.DMA]
 
 
+class Spread:
+    def __init__(self, ring, count, groups, src, came, sems):
+        self.ring, self.count, self.groups, self.src, self.came = ring, count, groups, src, came
+        self.send, self.recv = sems
+        self.total = count * groups
+        self.shared = self.total // src.shape[0]
+
+    def copies(self):
+        me = self.ring.batch * self.count + self.ring.me
+        for step in range(1, self.total):
+            flat = lax.rem(me + step, self.total)
+            yield pltpu.make_async_remote_copy(
+                src_ref=self.src.at[flat // self.shared],
+                dst_ref=self.came.at[step],
+                send_sem=self.send.at[step],
+                recv_sem=self.recv.at[step],
+                device_id=(flat // self.count, lax.rem(flat, self.count)),
+                device_id_type=MESH,
+            )
+
+    def start(self):
+        for go in self.copies():
+            go.start()
+        me = self.ring.batch * self.count + self.ring.me
+        self.came[0] = self.src[me // self.shared]
+
+    def finish(self):
+        total = self.came[0]
+        for step, go in enumerate(self.copies(), 1):
+            go.wait()
+            total = total + self.came[step]
+        return total
+
+    @staticmethod
+    def scratch(total):
+        return [pltpu.SemaphoreType.DMA((total,)) for _ in range(2)]
+
+
 class GroupSum:
     def __init__(self, ring, groups, sent, came, sems, out):
         self.ring, self.groups, self.sent, self.came, self.out = ring, groups, sent, came, out
@@ -553,18 +605,59 @@
         ]
 
 
+def norm_back(normal, inverse, slope, gain):
+    scaled = slope * gain
+    back = inverse * (
+        scaled
+        - jnp.mean(scaled, axis=-1, keepdims=True)
+        - normal * jnp.mean(scaled * normal, axis=-1, keepdims=True)
+    )
+    return back, jnp.sum(slope * normal, axis=0, keepdims=True), jnp.sum(slope, axis=0, keepdims=True)
+
+
 def feed_kernel(
-    count, groups, span, b_ref, cot_ref, w_ref, db_ref, out_ref, grad_ref, bs, cs, stage, h, du, tiles, *rest
+    count,
+    groups,
+    span,
+    b_ref,
+    cot_ref,
+    w_ref,
+    w_out_ref,
+    res_ref,
+    cot_own_ref,
+    vec_ref,
+    out_ref,
+    grad_ref,
+    dr_ref,
+    vec_sum_ref,
+    do_ref,
+    dr_send,
+    bs,
+    cs,
+    stage,
+    h,
+    du,
+    tiles,
+    db_ref,
+    do_send,
+    *rest,
 ):
     ring = Ring(count)
-    own = db_ref.shape[0]
+    own = out_ref.shape[0]
     sums = [
         RingSum(ring, *rest[7 * i : 7 * i + 3], rest[7 * i + 3 : 7 * i + 7], ref)
         for i, ref in enumerate((db_ref, out_ref))
     ]
     grads = GroupSum(ring, groups, rest[14], rest[15], rest[16:18], grad_ref)
-    row_sem, tile_sem = rest[18:]
+    row_sem, tile_sem, w_sem = rest[18:21]
+    exchange = Exchange(ring, count, do_send, do_ref, rest[21:24])
     pairs = ring.pairs
+
+    def weights(index):
+        held = (bs, cs)[index // 2 % 2].at[index % 2]
+        rows = pl.ds(index * 2 * own, 2 * own)
+        return pltpu.make_async_copy(w_out_ref.at[rows], held, w_sem.at[index % 4])
+
 
     def places(step):
         return ring.at(-1 - step) * own, ring.at(1 + step, 1 - ring.core) * own
@@ -591,9 +684,7 @@
 
     for go in row_loads(0):
         go.start()
-    ring.greet_groups(groups)
-    for each in sums:
-        each.clear()
+    ring.greet_all(count)
 
     def feed(step):
         slot = lax.rem(step, 2)
@@ -646,6 +737,8 @@
 
     for go in tile_loads(0):
         go.start()
+    for index in range(4):
+        weights(index).start()
 
     @pl.loop(0, grads.tiles)
     def _(tile):
@@ -672,10 +765,28 @@
     def _(step):
         sums[0].advance(step)
 
+    normal, inverse = norm_parts(res_ref[...])
+    slope = DEEP_ALPHA * cot_own_ref[...].astype(F32) + db_ref[...]
+    dr, gain_sum, bias_sum = norm_back(normal, inverse, slope, vec_ref[2:3, :])
+    dr_ref[...] = dr
+    vec_sum_ref[...] = jnp.concatenate([gain_sum, bias_sum], axis=0)
+    dr_low = dr.astype(BF)
+    for index in range(D // (2 * own)):
+        weights(index).wait()
+        do = nt(dr_low, (bs, cs)[index // 2 % 2][index % 2]).astype(BF)
+        if (index + 4) * 2 * own < D:
+            weights(index + 4).start()
+        for part in range(0, 2 * own, HD):
+            at = index * 2 * own + part
+            do_send[at // HD] = do[:, part : part + HD]
+            dr_send[at // HD] = dr_low[:, at : at + HD]
+    exchange.start()
+
     @pl.loop(0, pairs)
     def _(step):
         sums[1].advance(step)
 
+    exchange.finish()
     grads.finish()
     for step in (pairs - 2, pairs - 1):
         for which, each in enumerate(sums):
@@ -684,17 +795,21 @@
         each.finish()
 
 
-def feed_forward(b_low, cot, w_feed, own, count, groups, ident):
+def feed_forward(b_low, cot, w_feed, w_out, residual, cot_own, vectors, count, groups, ident):
     tokens, span, pairs = b_low.shape[0], w_feed.shape[1] // 3, count // 2
+    own = residual.shape[0]
     inside, anywhere = pl.BlockSpec(memory_space=pltpu.VMEM), pl.BlockSpec(memory_space=pl.ANY)
     return pl.pallas_call(
         functools.partial(feed_kernel, count, groups, span),
-        in_specs=[anywhere, anywhere, inside],
-        out_specs=[inside] * 3,
+        in_specs=[anywhere, anywhere, inside, anywhere, inside, inside, inside],
+        out_specs=[inside] * 4 + [anywhere, inside],
         out_shape=[
             jax.ShapeDtypeStruct((own, D), F32),
+            jax.ShapeDtypeStruct((D // groups // ROWS, ROWS, 3 * span), BF),
             jax.ShapeDtypeStruct((own, D), F32),
-            jax.ShapeDtypeStruct((D // groups // ROWS, ROWS, 3 * span), BF),
+            jax.ShapeDtypeStruct((2, D), F32),
+            jax.ShapeDtypeStruct((count, own, HD), BF),
+            jax.ShapeDtypeStruct((count, own, HD), BF),
         ],
         scratch_shapes=[
             pltpu.VMEM((2, 2 * own, D), BF),
@@ -703,16 +818,19 @@
             pltpu.VMEM((tokens, span), BF),
             pltpu.VMEM((tokens, 2 * span), BF),
             pltpu.VMEM((2, 2, tokens, ROWS), BF),
+            pltpu.VMEM((own, D), F32),
+            pltpu.VMEM((count, own, HD), BF),
         ]
         + RingSum.scratch(pairs, own) * 2
         + GroupSum.scratch(groups, 3 * span)
-        + [pltpu.SemaphoreType.DMA((2, 4)), pltpu.SemaphoreType.DMA((2, 2))],
-        compiler_params=vmem(60 * 1024 * 1024, collective_id=ident, has_side_effects=True),
+        + [pltpu.SemaphoreType.DMA((2, 4)), pltpu.SemaphoreType.DMA((2, 2)), pltpu.SemaphoreType.DMA((4,))]
+        + Exchange.scratch(count),
+        compiler_params=vmem(62 * 1024 * 1024, collective_id=ident, has_side_effects=True),
         cost_estimate=pl.CostEstimate(
             flops=18 * tokens * D * span, bytes_accessed=250_000_000, transcendentals=0
         ),
         name="feed_forward",
-    )(b_low, cot, w_feed)
+    )(b_low, cot, w_feed, w_out, residual, cot_own, vectors)
 
 
 def project_kernel(
@@ -724,11 +842,19 @@
     heads_ref,
     dr_ref,
     feed_ref,
-    da_ref,
+    x_ref,
+    dr_own_ref,
+    vec_ref,
+    vec_sum_ref,
+    back_ref,
     grad_ref,
     feed_out_ref,
+    vec_out_ref,
     stage,
     tiles,
+    da_ref,
+    vec_send,
+    vec_came,
     *rest,
 ):
     ring = Ring(count)
@@ -737,6 +863,7 @@
     grads = GroupSum(ring, groups, rest[7], rest[8], rest[9:11], grad_ref)
     tile_sem = rest[11]
     feed = Exchange(ring, count, feed_ref, feed_out_ref, rest[12:15])
+    spread = Spread(ring, count, groups, vec_send, vec_came, rest[15:17])
     pairs, width = ring.pairs, heads_ref.shape[2]
 
     def places(step):
@@ -762,9 +889,8 @@
 
     for go in tile_loads(0):
         go.start()
-    ring.greet_all(count)
+    ring.greet_whole(count)
     feed.start()
-    sums.clear()
 
     def terms_of(step):
         slot = lax.rem(step, 2)
@@ -814,40 +940,57 @@
     def _(step):
         sums.advance(step)
 
+    normal, inverse = norm_parts(x_ref[...].astype(F32))
+    slope = DEEP_ALPHA * dr_own_ref[...] + da_ref[...]
+    back, gain_sum, bias_sum = norm_back(normal, inverse, slope, vec_ref[0:1, :])
+    back_ref[...] = back.astype(BF)
+    kinds = [gain_sum, bias_sum, vec_sum_ref[0:1, :], vec_sum_ref[1:2, :]]
+    for tile in range(D // LANES):
+        for kind, values in enumerate(kinds):
+            vec_send[tile, kind : kind + 1, :] = values[:, tile * LANES : (tile + 1) * LANES]
+    spread.start()
     grads.finish()
     for step in (pairs - 2, pairs - 1):
         sums.given(step, stage.at[step % 2]).wait_send()
     sums.finish()
+    vec_out_ref[...] = spread.finish()
     feed.finish()
 
 
-def project_back(dp, w_qkv, a_low, heads, dr_cols, grad_feed, own, count, groups, ident):
+def project_back(
+    dp, w_qkv, a_low, heads, dr_cols, grad_feed, states, dr, vectors, vec_sums, count, groups, ident
+):
     tokens, pairs = dp.shape[0], count // 2
-    width = 3 * HD + dr_cols.shape[1]
+    own, width = dr.shape[0], 3 * HD + dr_cols.shape[1]
     inside, anywhere = pl.BlockSpec(memory_space=pltpu.VMEM), pl.BlockSpec(memory_space=pl.ANY)
     return pl.pallas_call(
         functools.partial(project_kernel, count, groups),
-        in_specs=[inside, inside, anywhere, anywhere, inside, anywhere],
-        out_specs=[inside, inside, anywhere],
+        in_specs=[inside, inside, anywhere, anywhere, inside, anywhere] + [inside] * 4,
+        out_specs=[inside, inside, anywhere, inside],
         out_shape=[
-            jax.ShapeDtypeStruct((own, D), F32),
+            jax.ShapeDtypeStruct((own, D), BF),
             jax.ShapeDtypeStruct((D // groups // ROWS, ROWS, width), BF),
             jax.ShapeDtypeStruct(grad_feed.shape, BF),
+            jax.ShapeDtypeStruct((8, LANES), F32),
         ],
         scratch_shapes=[
             pltpu.VMEM((2, own, D), BF),
             pltpu.VMEM((2, 2, tokens, ROWS), BF),
+            pltpu.VMEM((own, D), F32),
+            pltpu.VMEM((D // LANES, 8, LANES), F32),
+            pltpu.VMEM((count * groups, 8, LANES), F32),
         ]
         + RingSum.scratch(pairs, own)
         + GroupSum.scratch(groups, width)
         + [pltpu.SemaphoreType.DMA((2, 1 + ROWS // HD))]
-        + Exchange.scratch(count),
+        + Exchange.scratch(count)
+        + Spread.scratch(count * groups),
         compiler_params=vmem(collective_id=ident, has_side_effects=True),
         cost_estimate=pl.CostEstimate(
             flops=4 * tokens * D * 3 * HD, bytes_accessed=200_000_000, transcendentals=0
         ),
         name="project_back",
-    )(dp, w_qkv, a_low, heads, dr_cols, grad_feed)
+    )(dp, w_qkv, a_low, heads, dr_cols, grad_feed, states, dr, vectors, vec_sums)
 
 
 def norm_parts(values):
@@ -856,7 +999,7 @@
     return centre * inverse, inverse
 
 
-def qkv_kernel(x_ref, w_ref, vec_ref, cos_ref, sin_ref, a_ref, q_ref, k_ref, v_ref):
+def qkv_kernel(x_ref, w_ref, vec_ref, cos_ref, sin_ref, a_ref, q_ref, k_ref, v_ref, kt_ref, vt_ref):
     normal, _ = norm_parts(x_ref[...].astype(F32))
     low = (normal * vec_ref[0:1, :] + vec_ref[1:2, :]).astype(BF)
     a_ref[...] = low
@@ -865,20 +1008,24 @@
         part = projected[:, index * HD : (index + 1) * HD]
         turned = part * cos_ref[...] + pltpu.roll(part, HD // 2, 1) * sin_ref[...]
         ref[...] = turned.astype(BF)
+    kt_ref[...] = turned.T.astype(BF)[None]
     v_ref[...] = projected[:, 2 * HD :].astype(BF)
+    vt_ref[...] = projected[:, 2 * HD :].T.astype(BF)[None]
 
 
 def norm_and_project(states, w_qkv, vectors, cosine, sine):
     tokens = states.shape[0]
     whole = lambda shape: pl.BlockSpec(shape, lambda i: (0, 0))
     rows = lambda width: pl.BlockSpec((ROWS, width), lambda i: (i, 0))
+    turned = pl.BlockSpec((1, HD, ROWS), lambda i: (i * ROWS // KEYS, 0, i % (KEYS // ROWS)))
     return pl.pallas_call(
         qkv_kernel,
         grid=(tokens // ROWS,),
         in_specs=[rows(D), whole((D, 3 * HD)), whole(vectors.shape), rows(HD), rows(HD)],
-        out_specs=[rows(D), rows(HD), rows(HD), rows(HD)],
+        out_specs=[rows(D), rows(HD), rows(HD), rows(HD), turned, turned],
         out_shape=[jax.ShapeDtypeStruct((tokens, D), BF)]
-        + [jax.ShapeDtypeStruct((tokens, HD), BF) for _ in range(3)],
+        + [jax.ShapeDtypeStruct((tokens, HD), BF) for _ in range(3)]
+        + [jax.ShapeDtypeStruct((tokens // KEYS, HD, KEYS), BF) for _ in range(2)],
         compiler_params=vmem(),
         cost_estimate=pl.CostEstimate(
             flops=2 * tokens * D * 3 * HD, bytes_accessed=24_000_000, transcendentals=0
@@ -887,70 +1034,77 @@
     )(states, w_qkv, vectors, cosine, sine)
 
 
-def seen(block, first_ref, last_ref, keys):
-    query = block * ROWS + lax.broadcasted_iota(jnp.int32, (ROWS, ROWS), 0)
-    return (query >= first_ref[keys]) & (query < last_ref[keys])
+def masked_scores(block, query, k_ref, first_ref, last_ref, keys):
+    place = block * ROWS + lax.broadcasted_iota(jnp.int32, (1, LANES), 1)
+    scores = nt(k_ref[keys], query) * HD ** (-0.5)
+    parts = []
+    for at in range(0, ROWS, LANES):
+        seen = (place + at >= first_ref[keys]) & (place + at < last_ref[keys])
+        parts.append(jnp.where(seen, scores[:, at : at + LANES], NEG_LARGE))
+    return jnp.concatenate(parts, axis=1)
 
 
 def attend_kernel(
-    low_ref, high_ref, q_ref, k_ref, v_ref, first_ref, last_ref, o_ref, full_ref, log_ref, held
+    low_ref, high_ref, q_ref, k_ref, vt_ref, first_ref, last_ref, o_ref, full_ref, log_ref, held
 ):
     block = pl.program_id(0)
     query = q_ref[...]
-    scale = HD ** (-0.5)
 
     def score(keys, top):
-        scores = nt(query, k_ref[keys]) * scale
-        scores = jnp.where(seen(block, first_ref, last_ref, keys), scores, NEG_LARGE)
+        scores = masked_scores(block, query, k_ref, first_ref, last_ref, keys)
         held[keys] = scores
-        return jnp.maximum(top, jnp.max(scores, axis=-1, keepdims=True))
+        return jnp.maximum(top, jnp.max(scores, axis=0, keepdims=True))
 
     def add(keys, carry):
         total, out = carry
         weight = jnp.exp(held[keys] - top)
-        total = total + jnp.sum(weight, axis=-1, keepdims=True)
-        return total, out + nn(weight.astype(BF), v_ref[keys])
+        total = total + jnp.sum(weight, axis=0, keepdims=True)
+        return total, out + nn(vt_ref[keys], weight.astype(BF))
 
     low, high = low_ref[block], high_ref[block]
-    top = lax.fori_loop(low, high, score, jnp.full((ROWS, 1), NEG_LARGE, F32))
+    top = lax.fori_loop(low, high, score, jnp.full((1, ROWS), NEG_LARGE, F32))
     total, out = lax.fori_loop(
-        low, high, add, (jnp.zeros((ROWS, 1), F32), jnp.zeros((ROWS, HD), F32))
+        low, high, add, (jnp.zeros((1, ROWS), F32), jnp.zeros((HD, ROWS), F32))
     )
     out = out / total
-    o_ref[...] = out.astype(BF)
-    full_ref[...] = out
-    log_ref[...] = jnp.broadcast_to(top + jnp.log(total), (ROWS, LANES))
-
-
-def attend(query, key, value, spans):
+    o_ref[...] = out.T.astype(BF)
+    full_ref[...] = out[None]
+    log_ref[...] = (top + jnp.log(total))[None]
+
+
+def attend(query, key, value_t, spans):
     tokens = query.shape[0]
-    blocks = tokens // ROWS
+    blocks, span = tokens // ROWS, tokens // KEYS
     first, last, low, high = spans
     rows = pl.BlockSpec((ROWS, HD), lambda i, *_: (i, 0))
+    one = lambda shape: pl.BlockSpec((1,) + shape, lambda i, *_: (i, 0, 0))
     whole = lambda shape: pl.BlockSpec(shape, lambda i, *_: (0,) * len(shape))
-    cut = lambda values: values.reshape(blocks, ROWS, HD)
     return pl.pallas_call(
         attend_kernel,
         grid_spec=pltpu.PrefetchScalarGridSpec(
             num_scalar_prefetch=2,
             grid=(blocks,),
-            in_specs=[rows]
-            + [whole((blocks, ROWS, HD)) for _ in range(2)]
-            + [whole((blocks, 1, ROWS)) for _ in range(2)],
-            out_specs=[rows, rows, rows],
-            scratch_shapes=[pltpu.VMEM((blocks, ROWS, ROWS), F32)],
+            in_specs=[
+                rows,
+                whole((span, KEYS, HD)),
+                whole((span, HD, KEYS)),
+                whole((span, KEYS, LANES)),
+                whole((span, KEYS, LANES)),
+            ],
+            out_specs=[rows, one((HD, ROWS)), one((1, ROWS))],
+            scratch_shapes=[pltpu.VMEM((span, KEYS, ROWS), F32)],
         ),
         out_shape=[
             jax.ShapeDtypeStruct((tokens, HD), BF),
-            jax.ShapeDtypeStruct((tokens, HD), F32),
-            jax.ShapeDtypeStruct((tokens, LANES), F32),
+            jax.ShapeDtypeStruct((blocks, HD, ROWS), F32),
+            jax.ShapeDtypeStruct((blocks, 1, ROWS), F32),
         ],
         compiler_params=vmem(),
         cost_estimate=pl.CostEstimate(
             flops=2 * tokens * tokens * HD, bytes_accessed=4_000_000, transcendentals=0
         ),
         name="attend",
-    )(low, high, query, cut(key), cut(value), first, last)
+    )(low, high, query, key.reshape(span, KEYS, HD), value_t, first, last)
 
 
 def attend_back_kernel(
@@ -961,6 +1115,7 @@
     full_ref,
     log_ref,
     k_ref,
+    kt_ref,
     v_ref,
     first_ref,
     last_ref,
@@ -980,57 +1135,63 @@
         dv_ref[...] = jnp.zeros_like(dv_ref)
 
     query, grad = q_ref[...], g_ref[...]
-    inner = jnp.sum(grad.astype(F32) * full_ref[...], axis=-1, keepdims=True)
-    log = log_ref[:, 0:1]
+    inner = jnp.sum(grad.astype(F32).T * full_ref[0], axis=0, keepdims=True)
+    log = log_ref[0]
 
     def one(keys, total):
-        scores = nt(query, k_ref[keys]) * scale
-        scores = jnp.where(seen(block, first_ref, last_ref, keys), scores, NEG_LARGE)
+        scores = masked_scores(block, query, k_ref, first_ref, last_ref, keys)
         weight = jnp.exp(scores - log)
-        slope = (weight * (nt(grad, v_ref[keys]) - inner)).astype(BF)
-        dv_ref[keys] += tn(weight.astype(BF), grad)
-        dk_ref[keys] += tn(slope, query)
-        return total + nn(slope, k_ref[keys])
-
-    total = lax.fori_loop(
-        low_ref[block], high_ref[block], one, jnp.zeros((ROWS, HD), F32)
-    )
+        slope = (weight * (nt(v_ref[keys], grad) - inner)).astype(BF)
+        dv_ref[keys] += nn(weight.astype(BF), grad)
+        dk_ref[keys] += nn(slope, query)
+        return total + nn(kt_ref[keys], slope)
+
+    total = lax.fori_loop(low_ref[block], high_ref[block], one, jnp.zeros((HD, ROWS), F32))
 
     def turn_back(values, cosine, sine):
         values = (values * scale).astype(BF).astype(F32)
         return (values * cosine - pltpu.roll(values, HD // 2, 1) * sine).astype(BF)
 
     rows = pl.ds(pl.multiple_of(block * ROWS, ROWS), ROWS)
-    o_ref[rows, 0:HD] = turn_back(total, cos_ref[rows, :], sin_ref[rows, :])
+    o_ref[rows, 0:HD] = turn_back(total.T, cos_ref[rows, :], sin_ref[rows, :])
 
     @pl.when(block == blocks - 1)
     def _():
         for part in range(dk_ref.shape[0]):
-            there = pl.ds(part * ROWS, ROWS)
+            there = pl.ds(part * KEYS, KEYS)
             o_ref[there, HD : 2 * HD] = turn_back(
                 dk_ref[part], cos_ref[there, :], sin_ref[there, :]
             )
             o_ref[there, 2 * HD :] = dv_ref[part].astype(BF)
 
 
-def attend_back(query, key, value, grad, full, log, spans, cosine, sine):
+def attend_back(query, key, key_t, value, grad, full, log, spans, cosine, sine):
     tokens = query.shape[0]
-    blocks = tokens // ROWS
+    blocks, span = tokens // ROWS, tokens // KEYS
     first, last, low, high = spans
     rows = pl.BlockSpec((ROWS, HD), lambda i, *_: (i, 0))
+    one = lambda shape: pl.BlockSpec((1,) + shape, lambda i, *_: (i, 0, 0))
     whole = lambda shape: pl.BlockSpec(shape, lambda i, *_: (0,) * len(shape))
-    cut = lambda values: values.reshape(blocks, ROWS, HD)
     return pl.pallas_call(
         attend_back_kernel,
         grid_spec=pltpu.PrefetchScalarGridSpec(
             num_scalar_prefetch=2,
             grid=(blocks,),
-            in_specs=[rows] * 4
-            + [whole((blocks, ROWS, HD)) for _ in range(2)]
-            + [whole((blocks, 1, ROWS)) for _ in range(2)]
-            + [whole((tokens, HD)) for _ in range(2)],
+            in_specs=[
+                rows,
+                rows,
+                one((HD, ROWS)),
+                one((1, ROWS)),
+                whole((span, KEYS, HD)),
+                whole((span, HD, KEYS)),
+                whole((span, KEYS, HD)),
+                whole((span, KEYS, LANES)),
+                whole((span, KEYS, LANES)),
+                whole((tokens, HD)),
+                whole((tokens, HD)),
+            ],
             out_specs=whole((tokens, 3 * HD)),
-            scratch_shapes=[pltpu.VMEM((blocks, ROWS, HD), F32) for _ in range(2)],
+            scratch_shapes=[pltpu.VMEM((span, KEYS, HD), F32) for _ in range(2)],
         ),
         out_shape=jax.ShapeDtypeStruct((tokens, 3 * HD), BF),
         compiler_params=vmem(),
@@ -1038,7 +1199,21 @@
             flops=5 * tokens * tokens * HD, bytes_accessed=6_000_000, transcendentals=0
         ),
         name="attend_back",
-    )(low, high, query, grad, full, log, cut(key), cut(value), first, last, cosine, sine)
+    )(
+        low,
+        high,
+        query,
+        grad,
+        full,
+        log,
+        key.reshape(span, KEYS, HD),
+        key_t,
+        value.reshape(span, KEYS, HD),
+        first,
+        last,
+        cosine,
+        sine,
+    )
 
 
 def windows(at, span, count):
@@ -1101,85 +1276,95 @@
     )(master)
 
 
-STEP_COLS = 3072
-
-
-def update_kernel(
-    count, span, attn_ref, feed_ref, vec_ref, m_ref, f_ref, s_ref, a_ref, nm_ref, nf_ref, ns_ref, na_ref, grad
-):
+STEP_COLS = 2048
+
+
+def tile_of_part(ref, part, at, begin, rows, span):
+    turn = at % LANES
+    index = (begin - at + turn) // LANES
+    tiles = span // LANES
+
+    def piece(index):
+        if index < 0 or index * LANES >= FF:
+            return None
+        device, inner = divmod(index, tiles)
+        low = part * span + inner * LANES
+        values = ref[device, :, low : low + LANES].astype(F32)
+        return pltpu.roll(values, turn, 1) if turn else values
+
+    lane = lax.broadcasted_iota(jnp.int32, (rows, LANES), 1)
+    here, before = piece(index), piece(index - 1) if turn else None
+    if here is None:
+        return before
+    return here if before is None else jnp.where(lane < turn, before, here)
+
+
+def feed_tile(begin, feed_ref, vec_ref, rows, span):
+    lane = lax.broadcasted_iota(jnp.int32, (rows, LANES), 1)
+    total = 4 * D + 3 * FF + 4
+    value = None
+    for part, at in enumerate(FEED_AT):
+        if at < begin + LANES and at + FF > begin:
+            piece = tile_of_part(feed_ref, part, at, begin, rows, span)
+            value = piece if value is None else jnp.where(lane < at - begin, value, piece)
+    if begin + LANES > total - 4:
+        vec = pltpu.roll(vec_ref[...], (total - 4) % LANES, 1)
+        value = vec if value is None else jnp.where(lane < total - 4 - begin, value, vec)
+    return value
+
+
+def update_kernel(first_step, steps, tile_at, sources, *refs):
+    grads, (m_ref, f_ref, s_ref, a_ref), outs = refs[:sources], refs[sources : sources + 4], refs[-4:]
+    nm_ref, nf_ref, ns_ref, na_ref = outs
     rows = m_ref.shape[0]
-    step = pl.program_id(0)
     total = 4 * D + 3 * FF + 4
 
-    @pl.when(step == 0)
-    def _():
-        for index in range(count):
-            for part in range(4):
-                at = part * D + index * HD
-                grad[:, at : at + HD] = attn_ref[index, :, part * HD : (part + 1) * HD].astype(F32)
-        lane = lax.broadcasted_iota(jnp.int32, (rows, LANES), 1)
-        tiles = span // LANES
-        last = None
-        for part, at in enumerate(FEED_AT):
-            turn = at % LANES
-            for tile in range(-(-(FF + turn) // LANES)):
-                begin = at - turn + tile * LANES
-                index, inner = divmod(tile, tiles)
-                here = feed_ref[index, :, part * span + inner * LANES : part * span + (inner + 1) * LANES]
-                here = here.astype(F32)
-                if turn:
-                    here = pltpu.roll(here, turn, 1)
-                    before = last if tile == 0 else previous
-                    value = here if before is None else jnp.where(lane < turn, before, here)
-                    previous = here
-                else:
-                    value = here
-                if begin + LANES <= total:
-                    grad[:, begin : begin + LANES] = value
-                    last = value
-        edge = (total - 4) // LANES * LANES
-        shift = (total - 4) % LANES
-        both = jnp.concatenate([last, jnp.zeros_like(last)], axis=1)
-        vec = jnp.concatenate([vec_ref[...], jnp.zeros_like(last)], axis=1)
-        vec = pltpu.roll(vec, shift, 1)
-        wide = lax.broadcasted_iota(jnp.int32, (rows, 2 * LANES), 1)
-        both = jnp.where(wide < shift, both, vec)
-        grad[:, edge : edge + 2 * LANES] = both
-
-    begin = pl.multiple_of(step * STEP_COLS, LANES)
-    g = grad[:, pl.ds(begin, STEP_COLS)]
-    vector = step * STEP_COLS + lax.broadcasted_iota(jnp.int32, (1, STEP_COLS), 1) >= total - 4
-    rate = jnp.where(vector, LR_VEC, LR_MAT)
-    decay = jnp.where(vector, 0.0, DECAY_MAT)
-    new_first = BETA_ONE * f_ref[...] + (1.0 - BETA_ONE) * g
-    new_second = BETA_TWO * s_ref[...] + (1.0 - BETA_TWO) * g * g
-    nf_ref[...] = new_first
-    ns_ref[...] = new_second
-    root = jnp.sqrt(new_second * (1.0 / (1.0 - BETA_TWO**STEP))) + ADAM_EPS
-    corrected = new_first * (1.0 / (1.0 - BETA_ONE**STEP)) / root
-    master = m_ref[...]
-    new_master = master - rate * (corrected + decay * master)
-    nm_ref[...] = new_master
-    na_ref[...] = EMA_RATE * a_ref[...] + (1.0 - EMA_RATE) * new_master
-
-
-def update(attn, feed, vec, master, first, second, average, span):
-    count, rows = feed.shape[:2]
-    columns = master.shape[1]
-    steps = -(-columns // STEP_COLS)
+    def one(begin, cols):
+        g = tile_at(begin, *grads)
+        rate, decay = LR_MAT, DECAY_MAT
+        if begin + LANES > total - 4:
+            vector = begin + lax.broadcasted_iota(jnp.int32, (1, LANES), 1) >= total - 4
+            rate, decay = jnp.where(vector, LR_VEC, LR_MAT), jnp.where(vector, 0.0, DECAY_MAT)
+        new_first = BETA_ONE * f_ref[:, cols] + (1.0 - BETA_ONE) * g
+        new_second = BETA_TWO * s_ref[:, cols] + (1.0 - BETA_TWO) * g * g
+        nf_ref[:, cols] = new_first
+        ns_ref[:, cols] = new_second
+        root = jnp.sqrt(new_second * (1.0 / (1.0 - BETA_TWO**STEP))) + ADAM_EPS
+        corrected = new_first * (1.0 / (1.0 - BETA_ONE**STEP)) / root
+        master = m_ref[:, cols]
+        new_master = master - rate * (corrected + decay * master)
+        nm_ref[:, cols] = new_master
+        na_ref[:, cols] = EMA_RATE * a_ref[:, cols] + (1.0 - EMA_RATE) * new_master
+
+    for step in range(steps):
+
+        @pl.when(pl.program_id(0) == step)
+        def _():
+            for at in range(0, STEP_COLS, LANES):
+                begin = (first_step + step) * STEP_COLS + at
+                if begin < total:
+                    one(begin, slice(at, at + LANES))
+
+
+def update(grads, tile_at, state, first_step, steps, done=()):
+    rows, columns = state[0].shape
     whole = lambda values: pl.BlockSpec(values.shape, lambda i: (0,) * values.ndim)
-    cols = pl.BlockSpec((rows, STEP_COLS), lambda i: (0, i))
+    cols = pl.BlockSpec((rows, STEP_COLS), lambda i: (0, first_step + i))
     return pl.pallas_call(
-        functools.partial(update_kernel, count, span),
+        functools.partial(update_kernel, first_step, steps, tile_at, len(grads)),
         grid=(steps,),
-        in_specs=[whole(attn), whole(feed), whole(vec)] + [cols] * 4,
+        in_specs=[whole(g) for g in grads]
+        + [cols] * 4
+        + [pl.BlockSpec(memory_space=pl.ANY)] * len(done),
         out_specs=[cols] * 4,
-        out_shape=[jax.ShapeDtypeStruct(master.shape, F32) for _ in range(4)],
-        scratch_shapes=[pltpu.VMEM((rows, steps * STEP_COLS), F32)],
+        out_shape=[jax.ShapeDtypeStruct((rows, columns), F32) for _ in range(4)],
+        input_output_aliases={len(grads) + 4 + i: i for i in range(len(done))},
         compiler_params=vmem(),
-        cost_estimate=pl.CostEstimate(flops=0, bytes_accessed=56_000_000, transcendentals=0),
-        name="update",
-    )(attn, feed, vec, master, first, second, average)
+        cost_estimate=pl.CostEstimate(
+            flops=0, bytes_accessed=36 * rows * steps * STEP_COLS, transcendentals=0
+        ),
+        name=f"update_{first_step}",
+    )(*grads, *state, *done)
 
 
 def chain_spans(lengths, prefix, padding, total):
@@ -1192,10 +1377,9 @@
     place = token - start
     first = jnp.where(place < pre, start, token)
     first = jnp.where(place < live, first, 2 * total)
-    blocks = total // ROWS
-    low = start[::ROWS] // ROWS
-    high = (end[ROWS - 1 :: ROWS] + ROWS - 1) // ROWS
-    cut = lambda values: values.reshape(blocks, 1, ROWS)
+    low = start[::ROWS] // KEYS
+    high = (end[ROWS - 1 :: ROWS] + KEYS - 1) // KEYS
+    cut = lambda values: jnp.broadcast_to(values[:, None], (total, LANES)).reshape(-1, KEYS, LANES)
     return (cut(first), cut(end), low, high), place
 
 
@@ -1207,34 +1391,9 @@
     return jnp.concatenate([cosine, cosine], axis=1), jnp.concatenate([-sine, sine], axis=1)
 
 
-def over_batch(block_of, own):
-    count = lax.axis_size("batch")
-    me = lax.axis_index("batch")
-    arrived = [
-        lax.ppermute(
-            block_of(lax.rem(me + shift, count)),
-            "batch",
-            [(i, (i + shift) % count) for i in range(count)],
-        )
-        for shift in range(1, count)
-    ]
-    return functools.reduce(lambda total, part: total + part.astype(F32), arrived, own())
-
-
 def to_rows(grad):
     blocks = grad.reshape(lax.axis_size("seq"), -1, grad.shape[-1])
     return lax.all_to_all(blocks, "seq", split_axis=0, concat_axis=0, tiled=True)
-
-
-def vector_rows(sums):
-    batch, seq = lax.axis_size("batch"), lax.axis_size("seq")
-    me = lax.axis_index("batch")
-    kinds = sums.shape[0]
-    cut = sums.reshape(kinds, batch, seq, -1).transpose(2, 1, 0, 3)
-    came = lax.all_to_all(cut, "seq", split_axis=0, concat_axis=0, tiled=True)
-    totals = jnp.sum(came, axis=0)
-    part = lambda place: lax.dynamic_index_in_dim(totals, place, 0, keepdims=False)
-    return over_batch(part, lambda: part(me)).T
 
 
 def on_device(hidden_in, cotangent, master, first, second, average, lengths, prefix, padding):
@@ -1255,53 +1414,54 @@
 
     spans, place = chain_spans(lengths[0], prefix[0], padding[0], tokens)
     cosine, sine = rotary_tables(place)
-    a_low, query, key, value = norm_and_project(states, w_qkv, vectors, cosine, sine)
-    attended, full, log = attend(query, key, value, spans)
+    a_low, query, key, value, key_t, value_t = norm_and_project(states, w_qkv, vectors, cosine, sine)
+    attended, full, log = attend(query, key, value_t, spans)
     heads, w_feed, b_low, residual = gather_residual(
         attended, feed_cut, states, w_out, vectors, own, seq, 2
     )
     w_feed = w_feed.reshape(D, 3 * span)
-    db_sum, out_sum, grad_feed = feed_forward(b_low, cot_all, w_feed, own, seq, groups, 3)
-    grad_feed = grad_feed.reshape(seq, rows, 3 * span)
-    gain_one, bias_one, gain_two, bias_two = (vectors[i][None, :] for i in range(4))
-
-    def norm_back(normal, inverse, slope, gain):
-        scaled = slope * gain
-        back = inverse * (
-            scaled
-            - jnp.mean(scaled, axis=-1, keepdims=True)
-            - normal * jnp.mean(scaled * normal, axis=-1, keepdims=True)
-        )
-        return back, jnp.stack([jnp.sum(slope * normal, axis=0), jnp.sum(slope, axis=0)])
-
-    normal_two, inverse_two = norm_parts(residual)
-    output = DEEP_ALPHA * (normal_two * gain_two + bias_two) + out_sum
-    db = DEEP_ALPHA * cotangent.astype(F32) + db_sum
-    dr, sums_two = norm_back(normal_two, inverse_two, db, gain_two)
-    dr_low = dr.astype(BF)
-    do = nt(dr_low, w_out).astype(BF)
-    to_heads = lambda values: lax.all_to_all(
-        values.reshape(own, seq, HD).transpose(1, 0, 2), "seq", split_axis=0, concat_axis=0, tiled=True
-    ).reshape(tokens, HD)
-    do_head = to_heads(do)
-    dr_cols = to_heads(dr_low)
-
-    dp = attend_back(query, key, value, do_head, full, log, spans, cosine, sine)
-    da_sum, grad_attn, grad_feed = project_back(
-        dp, w_qkv, a_low, heads, dr_cols, grad_feed, own, seq, groups, 4
+    out_sum, grad_feed, dr, vec_sums, do, dr_cut = feed_forward(
+        b_low, cot_all, w_feed, w_out, residual, cotangent, vectors, seq, groups, 3
+    )
+    dr_cols = lax.all_to_all(dr_cut, "seq", split_axis=0, concat_axis=0, tiled=True)
+    normal_two, _ = norm_parts(residual)
+    output = DEEP_ALPHA * (normal_two * vectors[2:3] + vectors[3:4]) + out_sum
+
+    dp = attend_back(query, key, key_t, value, do.reshape(tokens, HD), full, log, spans, cosine, sine)
+    input_grad, grad_attn, grad_feed, grad_vec = project_back(
+        dp,
+        w_qkv,
+        a_low,
+        heads,
+        dr_cols.reshape(tokens, HD),
+        grad_feed.reshape(seq, rows, 3 * span),
+        hidden_in,
+        dr,
+        vectors,
+        vec_sums,
+        seq,
+        groups,
+        4,
     )
     grad_attn = to_rows(grad_attn)
-
-    normal_one, inverse_one = norm_parts(hidden_in.astype(F32))
-    da = DEEP_ALPHA * dr + da_sum
-    input_grad, sums_one = norm_back(normal_one, inverse_one, da, gain_one)
-    vector_grad = vector_rows(jnp.concatenate([sums_one, sums_two]))
-
-    vector_grad = jnp.pad(vector_grad, ((0, 0), (0, LANES - vector_grad.shape[1])))
-    updated = update(grad_attn, grad_feed, vector_grad, master, first, second, average, span)
+    place = lax.rem(lax.axis_index("batch") * seq + lax.axis_index("seq"), LANES // rows) * rows
+    grad_vec = lax.dynamic_slice_in_dim(grad_vec, place, rows, 1)[:4].T
+    grad_vec = jnp.pad(grad_vec, ((0, 0), (0, LANES - 4)))
+
+    def attn_tile(begin, ref):
+        part, index = divmod(begin // HD, seq)
+        return ref[index, :, part * HD : (part + 1) * HD].astype(F32)
+
+    def other_tile(begin, feed_ref, vec_ref):
+        return feed_tile(begin, feed_ref, vec_ref, rows, span)
+
+    state = (master, first, second, average)
+    steps, attn_steps = -(-master.shape[1] // STEP_COLS), 4 * D // STEP_COLS
+    updated = update([grad_feed, grad_vec], other_tile, state, attn_steps, steps - attn_steps)
+    updated = update([grad_attn], attn_tile, state, 0, attn_steps, updated)
     return (
         output.astype(BF),
-        input_grad.astype(BF),
+        input_grad,
         *updated,
     )
 

time: 645 us -> 605 us (0.938)
  waiting for transfers between devices: 32.2 us -> 7.03 us
  Pallas kernels: 523 us -> 548 us
  blocking collectives: 11.4 us -> 0 us
  other arithmetic: 19.6 us -> 8.74 us
  starting transfers between devices: 20.5 us -> 9.77 us
    pallas_call x1, Pallas kernels: 106 us -> 126 us  [feed_forward(): pl.pallas_call(functools.partial(feed_kernel, count, groups, span), in_sp...]
    all_to_all x2 -> x1, waiting for transfers between devices: 13.2 us -> 0.01 us  [on_device(): lax.all_to_all(dr_cut, 'seq', split_axis=0, concat_axis=0, tiled=True)]
    all_to_all x1, waiting for transfers between devices: 18.3 us -> 6.3 us  [to_rows(): lax.all_to_all(blocks, 'seq', split_axis=0, concat_axis=0, tiled=True)]
    all_to_all x1 -> x0, blocking collectives: 11.4 us -> none  [vector_rows(): came = lax.all_to_all(cut, 'seq', split_axis=0, concat_axis=0, tiled=True)]
    pallas_call x1, Pallas kernels: 104 us -> 115 us  [project_back(): pl.pallas_call(functools.partial(project_kernel, count, groups), in_specs...]
    all_to_all x2 -> x1, starting transfers between devices: 12.1 us -> 4.54 us  [on_device(): lax.all_to_all(dr_cut, 'seq', split_axis=0, concat_axis=0, tiled=True)]
    pallas_call x1 -> x2, Pallas kernels: 23.1 us -> 23.9 us  [update(): pl.pallas_call(functools.partial(update_kernel, first_step, steps, tile_a...]
  transfers between devices with their start and end apart: 6 -> 4, of which waited for: 2 -> 1; matrix products, arithmetic and copies ran while one was open for 3% -> 3% of each run, Pallas kernels for 45% -> 49%
where the time goes in v3:
time: 605 us; the launch traced here: 597 us
  Pallas kernels  548 us (91%)
  between operations  14.5 us (2%)
  starting transfers between devices  9.77 us (2%)
  local copies, waits for them, and re-layouts  9.06 us (1%)
  other arithmetic  8.74 us (1%)
  waiting for transfers between devices  7.03 us (1%)
    pallas_call x1, Pallas kernels, feed_forward(): pl.pallas_call(functools.partial(feed_kernel, count, groups, span), in_sp...  126 us
    pallas_call x1, Pallas kernels, gather_residual(): pl.pallas_call(functools.partial(residual_kernel, count), out_shape=[jax....  124 us
    pallas_call x1, Pallas kernels, project_back(): pl.pallas_call(functools.partial(project_kernel, count, groups), in_specs...  115 us
    pallas_call x1, Pallas kernels, ring_gather(): pl.pallas_call(functools.partial(gather_kernel, count, len(blocks)), out_...  110 us
    pallas_call x2, Pallas kernels, update(): pl.pallas_call(functools.partial(update_kernel, first_step, steps, tile_a...  23.9 us
    pallas_call x1, Pallas kernels, norm_and_project(): pl.pallas_call(qkv_kernel, grid=(tokens // ROWS,), in_specs=[rows(D), who...  16.1 us
    pallas_call x1, Pallas kernels, attend_back(): pl.pallas_call(attend_back_kernel, grid_spec=pltpu.PrefetchScalarGridSpec...  16 us
  transfers between devices with their start and end apart: 4, of which 1 were waited for; matrix products, arithmetic and copies ran while one was open for 3% of the time, Pallas kernels for 49%

profile of v3, /device:TPU:9, one launch (start us, length us, event | category | flops | bytes accessed | tf_op | source)
XLA Modules:
  0.0 597.4 jit_solution(2996853107367535834)
XLA Ops:
  7.2 0.0 copy-start.7
  7.2 0.0 copy-start.8
  7.2 0.0 copy-start.6
  7.2 0.0 all-gather.3.cloned.1.call-start
  7.2 5.1 lay_out.1
  12.3 0.0 all-gather.3.cloned.1.call-update
  12.4 0.0 all-gather.5.cloned.1.call-start
  12.4 0.7 all-gather.5.cloned.1.call-update
  13.1 0.9 slice.38
  14.0 0.0 copy-done.7
  14.0 0.2 reduce-window.4
  14.2 0.0 copy-done.8
  14.2 0.0 copy-done.6
  14.2 0.2 select_reduce_fusion.1
  14.4 0.1 slice.24
  14.5 0.1 slice.25
  14.6 0.1 copy.28
  14.7 0.6 bitcast_convert_fusion.refs_1_
  15.3 110.2 %ring_gather_1.1 = (bf16[16,128,2048]{2,1,0:T(8,128)(2,1)}, bf16[2,16,64,384]{3,2,1,0:T(8,128)(2,1)}, f32[2,16,8,128]{3,2,1,0:T(8,128)}) custom-call(bf16[128,2048]{1,0:T(8,128)(2,1)} %x_ref.3, bf16[16,64,384]{2,1,0:T(8,128)(2,1)} %get-tuple-element.43.refs_0_, f32[1,8,128]{2,1,0:T(8,128)} %bitcast_convert_fusion.refs_1_), custom_call_target="tpu_custom_call" | custom-call | bytes 150000000 | tf_op jit(solution)/shard_map/ring_gather_1/pallas_call | solution.py:245
  125.5 0.9 slice_bitcast_fusion
  126.4 0.7 reshape.116.vec_ref
  127.2 0.6 and_select_fusion
  127.8 3.7 fusion
  131.5 1.9 pad_maximum_fusion
  133.4 16.1 %norm_and_project.1 = (bf16[2048,2048]{1,0:T(8,128)(2,1)}, bf16[2048,128]{1,0:T(8,128)(2,1)}, bf16[2048,128]{1,0:T(8,128)(2,1)}, bf16[2048,128]{1,0:T(8,128)(2,1...) custom-call(bf16[2048,2048]{1,0:T(8,128)(2,1)} %bitcast.30, bf16[2048,384]{1,0:T(8,128)(2,1)} %bitcast.32, ...), custom_call_target="tpu_custom_call" | custom-call | flops 3221225472 | bytes 24000000 | tf_op jit(solution)/shard_map/norm_and_project/pallas_call | solution.py:1021
  149.6 1.3 broadcast_in_dim.72.first_ref
  150.9 1.3 broadcast_in_dim.74.last_ref
  152.2 11.9 %attend.1 = (bf16[2048,128]{1,0:T(8,128)(2,1)}, f32[8,128,256]{2,1,0:T(8,128)}, f32[8,1,256]{2,1,0:T(1,128)}) custom-call(s32[8]{0:T(128)} %get-tuple-element.94.low_ref, s32[8]{0:T(128)} %get-tuple-element.93.high_ref, bf16[2048,128]{1,0:T(8,128)(2,1)} %get-tuple-element.47.q_ref, bf16[4,512,128]{2,1,0:T(8,128)(2,1)} %bitcast.41, ...), custom_call_target="tpu_custom_call" | custom-call | flops 1073741824 | bytes 4000000 | tf_op jit(solution)/shard_map/attend/pallas_call | solution.py:1082
  164.1 0.0 all-gather.3.cloned.1.call-done.w_ref.w_out_ref
  164.1 123.8 %gather_residual.1 = (bf16[16,2048,128]{2,1,0:T(8,128)(2,1)}, bf16[2,16,64,1152]{3,2,1,0:T(8,128)(2,1)}, bf16[2048,2048]{1,0:T(8,128)(2,1)}, f32[128,2048]{1,0:T(8,128)}) custom-call(bf16[2048,128]{1,0:T(8,128)(2,1)} %get-tuple-element.50.x_ref, bf16[16,64,1152]{2,1,0:T(8,128)(2,1)} %get-tuple-element.51.part_ref, bf16[2048,2048]{1,0:T(8,128)(2,1)} %bitcast.31, ...), custom_call_target="tpu_custom_call" | custom-call | flops 17179869184 | bytes 200000000 | tf_op jit(solution)/shard_map/gather_residual/pallas_call | solution.py:386
  287.9 0.0 all-gather.5.cloned.1.call-done.cot_ref
  287.9 126.4 %feed_forward.1 = (f32[128,2048]{1,0:T(8,128)}, bf16[4,256,1152]{2,1,0:T(8,128)(2,1)}, f32[128,2048]{1,0:T(8,128)}, f32[2,2048]{1,0:T(2,128)}, bf16[16,128,128]{...) custom-call(bf16[2048,2048]{1,0:T(8,128)(2,1)} %get-tuple-element.54.b_ref, ...), custom_call_target="tpu_custom_call" | custom-call | flops 28991029248 | bytes 250000000 | tf_op jit(solution)/shard_map/feed_forward/pallas_call | solution.py:802
  414.3 4.5 all-to-all-start
  418.8 16.0 %attend_back.1.dp_ref = bf16[2048,384]{1,0:T(8,128)(2,1)} custom-call(s32[8]{0:T(128)} %get-tuple-element.94.low_ref, s32[8]{0:T(128)} %get-tuple-element.93.high_ref, bf16[2048,128]{1,0:T(8,128)(2,1)} %get-tuple-element.47.q_ref, bf16[2048,128]{1,0:T(8,128)(2,1)} %bitcast.45, f32[8,128,256]{2,1,0:T(8,128)} %get-tuple-element.58.full_ref, ...), custom_call_target="tpu_custom_call" | custom-call | flops 2684354560 | bytes 6000000 | tf_op jit(solution)/shard_map/attend_back/pallas_call | solution.py:1175
  434.8 0.0 all-to-all-done
  434.8 0.0 copy-start.2
  434.8 0.8 copy-done.2
  435.6 0.0 copy-start
  435.6 0.0 copy-start.3
  435.6 115.0 %project_back.1 = (bf16[128,2048]{1,0:T(8,128)(2,1)}, bf16[4,256,512]{2,1,0:T(8,128)(2,1)}, bf16[16,64,1152]{2,1,0:T(8,128)(2,1)}, f32[8,128]{1,0:T(8,128)}) custom-call(bf16[2048,384]{1,0:T(8,128)(2,1)} %attend_back.1.dp_ref, bf16[2048,384]{1,0:T(8,128)(2,1)} %bitcast.33, bf16[2048,2048]{1,0:T(8,128)(2,1)} %get-tuple-element.62.a_ref, ...), custom_call_target="tpu_custom_call" | custom-call | flops 6442450944 | bytes 200000000 | tf_op jit(solution)/shard_map/project_back/pallas_call | solution.py:966
  550.6 0.0 copy-start.5
  550.6 5.2 all-to-all-start.1
  555.8 0.1 slice_reduce_fusion.1
  555.9 0.1 add.44
  555.9 0.1 mul.52
  556.0 0.0 copy-done
  556.0 0.1 reduce_sum.67
  556.2 0.3 multiply_reduce_fusion
  556.4 0.0 copy-done.3
  556.4 1.1 add_convert_fusion
  557.5 0.0 copy-done.5
  557.6 0.1 copy.27
  557.7 0.6 pad.10.refs_1_
  558.3 15.9 %update_4.1 = (f32[64,24579]{1,0:T(8,128)}, f32[64,24579]{1,0:T(8,128)}, f32[64,24579]{1,0:T(8,128)}, f32[64,24579]{1,0:T(8,128)}) custom-call(bf16[16,64,1152]{2,1,0:T(8,128)(2,1)} %get-tuple-element.70.refs_0_, f32[64,128]{1,0:T(8,128)} %pad.10.refs_1_, f32[64,24579]{1,0:T(8,128)} %refs_1_.1, f32[64,24579]{1,0:T(8,128)} %refs_2_.3, f32[64,24579]{1,0:T(8,128)} %refs_3_.3, ...), custom_call_target="tpu_custom_call" | custom-call | bytes 42467328 | tf_op jit(solution)/shard_map/update_4/pallas_call | solution.py:1353
  574.2 6.3 %all-to-all-done.1.refs_0_ = bf16[16,64,512]{2,1,0:T(8,128)(2,1)S(1)} async-done(((bf16[16,64,512]{2,1,0:T(8,128)(2,1)}), bf16[16,64,512]{2,1,0:T(8,128)(2,1)S(1)}, u32[]{:S(2)}, u32[]{:S(2)}) %all-to-all-start.1) | async-done | bytes 1048608 | tf_op jit(solution)/shard_map/all_to_all | solution.py:1396
  580.5 0.0 copy-start.1
  580.5 1.0 copy-done.1
  581.5 0.0 copy-start.4
  581.5 8.0 %update_0.1 = (f32[64,24579]{1,0:T(8,128)}, f32[64,24579]{1,0:T(8,128)}, f32[64,24579]{1,0:T(8,128)}, f32[64,24579]{1,0:T(8,128)}) custom-call(bf16[16,64,512]{2,1,0:T(8,128)(2,1)} %copy-done.1, f32[64,24579]{1,0:T(8,128)} %refs_1_.1, f32[64,24579]{1,0:T(8,128)} %refs_2_.3, ...), custom_call_target="tpu_custom_call", output_to_operand_aliasing={{0}: (5, {}), {1}: (6, {}), {2}: (7, {}), {3}: (8, {})} | custom-call | bytes 18874368 | tf_op jit(solution)/shard_map/update_0/pallas_call | solution.py:1353
  589.5 0.0 copy-done.4
  589.5 0.8 copy.34
  (12 shorter events, 0.1 us)
Async XLA Ops:
  7.2 6.9 %copy-start.7 = (s32[1,4]{1,0:T(1,128)S(1)}, s32[1,4]{1,0:T(1,128)}, u32[]{:S(2)}) copy-start(s32[1,4]{1,0:T(1,128)} %param.15) | copy-start | bytes 52
  7.2 7.0 %copy-start.8 = (s32[1,4]{1,0:T(1,128)S(1)}, s32[1,4]{1,0:T(1,128)}, u32[]{:S(2)}) copy-start(s32[1,4]{1,0:T(1,128)} %param.17) | copy-start | bytes 52
  7.2 7.0 %copy-start.6 = (s32[1,4]{1,0:T(1,128)S(1)}, s32[1,4]{1,0:T(1,128)}, u32[]{:S(2)}) copy-start(s32[1,4]{1,0:T(1,128)} %param.16) | copy-start | bytes 52
  7.2 156.9 %all-gather.3.cloned.1.call-start = ((), (), s32[]{:S(2)}) async-start(), calls=%async_computation.2 | async-start | bytes 8650752 | tf_op jit(solution)/shard_map/all_gather | solution.py:1412
  12.4 275.6 %all-gather.5.cloned.1.call-start = ((), (), s32[]{:S(2)}) async-start(), calls=%async_computation.3 | async-start | bytes 8912896 | tf_op jit(solution)/shard_map/all_gather | solution.py:1413
  414.3 20.5 %all-to-all-start = ((bf16[16,128,128]{2,1,0:T(8,128)(2,1)}), bf16[16,128,128]{2,1,0:T(8,128)(2,1)S(1)}, u32[]{:S(2)}, u32[]{:S(2)}) async-start(bf16[16,128,128]{2,1,0:T(8,128)(2,1)} %get-tuple-element.64), calls=%async_computation | async-start | bytes 1048576 | tf_op jit(solution)/shard_map/all_to_all | solution.py:1426
  434.8 0.8 copy-start.2
  435.6 120.4 %copy-start = (f32[128,2048]{1,0:T(8,128)S(1)}, f32[128,2048]{1,0:T(8,128)}, u32[]{:S(2)}) copy-start(f32[128,2048]{1,0:T(8,128)} %get-tuple-element.53.res_ref) | copy-start | bytes 3145732
  435.6 120.8 %copy-start.3 = (f32[128,2048]{1,0:T(8,128)S(1)}, f32[128,2048]{1,0:T(8,128)}, u32[]{:S(2)}) copy-start(f32[128,2048]{1,0:T(8,128)} %get-tuple-element.56) | copy-start | bytes 3145732
  550.6 7.0 %copy-start.5 = (f32[8,128]{1,0:T(8,128)S(1)}, f32[8,128]{1,0:T(8,128)}, u32[]{:S(2)}) copy-start(f32[8,128]{1,0:T(8,128)} %get-tuple-element.71) | copy-start | bytes 12292
  550.6 29.9 %all-to-all-start.1 = ((bf16[16,64,512]{2,1,0:T(8,128)(2,1)}), bf16[16,64,512]{2,1,0:T(8,128)(2,1)S(1)}, u32[]{:S(2)}, u32[]{:S(2)}) async-start(bf16[16,64,512]{2,1,0:T(8,128)(2,1)} %bitcast.36), calls=%async_computation.1 | async-start | bytes 2097152 | tf_op jit(solution)/shard_map/all_to_all | solution.py:1396
  580.5 1.0 copy-start.1
  581.5 8.0 %copy-start.4 = (bf16[128,2048]{1,0:T(8,128)(2,1)S(1)}, bf16[128,2048]{1,0:T(8,128)(2,1)}, u32[]{:S(2)}) copy-start(bf16[128,2048]{1,0:T(8,128)(2,1)} %get-tuple-element.102) | copy-start | bytes 1572868
Sparse Core Ops, SparseCore 0:
  12.5 94.5 all-gather.2
  109.2 83.2 all-gather.4

commit v4 on v3

--- a/solution.py
+++ b/solution.py
@@ -181,7 +181,7 @@
         self.mine.wait()
 
 
-def pass_round(ring, count, x_ref, o_ref, sems, columns, work):
+def pass_round(ring, count, lag, x_ref, o_ref, sems, columns, work):
     ring_s, ring_r, sib_s, sib_r, own_sem = sems
     piece = x_ref.shape[0] // SUBS
     own = pltpu.make_async_copy(x_ref, o_ref.at[ring.me], own_sem)
@@ -189,6 +189,18 @@
     ring.greet_all(count)
     following, sends = ring.at(1), []
     ahead = 1
+
+    def complete(step):
+        if step == 0:
+            own.wait()
+        other = ring.at(step, 1 - ring.core)
+        for sub in range(SUBS):
+            dst = o_ref.at[other].at[pl.ds(sub * piece, piece)]
+            ring.copy(
+                dst, dst, sib_s.at[step, sub], sib_r.at[step, sub], ring.sibling
+            ).wait_recv()
+        work(ring.at(-step), other)
+
     for step in range(ring.pairs):
         block = ring.at(-step)
         for sub in range(SUBS):
@@ -209,32 +221,118 @@
         if step == 0:
             for column in columns:
                 column.start()
-            own.wait()
         else:
             upto = count if step == ring.pairs - 1 else min(count, 1 + 2 * step)
             for passed in range(ahead, max(ahead, upto)):
                 for column in columns:
                     column.pass_on(passed)
             ahead = max(ahead, upto)
-        other = ring.at(step, 1 - ring.core)
+        if step >= lag:
+            complete(step - lag)
+    for step in range(max(0, ring.pairs - lag), ring.pairs):
+        complete(step)
+    return sends
+
+
+class Line:
+    def __init__(self, ring, count):
+        self.ring, self.length = ring, count // 4
+        self.y, self.z = lax.rem(ring.me // 2, 2), ring.me // 4
+
+    def nearest(self, index):
+        order = [sorted(range(self.length), key=lambda q: (abs(q - z), q)) for z in range(self.length)]
+        place = order[0][index] + 0 * self.z
+        for z in range(1, self.length):
+            place = jnp.where(self.z == z, order[z][index], place)
+        return place
+
+    def device(self, z, row=0, core=0):
+        y = self.y if row == 0 else 1 - self.y
+        return (z * 2 + y) * 2 + (self.ring.core if core == 0 else 1 - self.ring.core)
+
+
+def pass_along(ring, count, x_ref, o_ref, sems, columns):
+    line_s, line_r, over_s, over_r, sib_s, sib_r, own_sem = sems
+    line = Line(ring, count)
+    piece = x_ref.shape[0] // SUBS
+    own = pltpu.make_async_copy(x_ref, o_ref.at[ring.me], own_sem)
+    own.start()
+    ring.greet_all(count)
+    across = line.device(line.z, 1)
+    sends = []
+
+    def send(condition, src, dst, send_sem, recv_sem, device):
+        go = ring.copy(src, dst, send_sem, recv_sem, device)
+        if condition is None:
+            go.start()
+        else:
+            pl.when(condition)(go.start)
+        sends.append((condition, go))
+
+    order = sorted(((row, index) for row in (0, 1) for index in range(line.length)), key=lambda p: (p[0] + p[1], p[0]))
+    ahead = 1
+    for turn, (row, index) in enumerate(order):
+        z = line.nearest(index)
+        block = line.device(z, row)
+        for sub in range(SUBS):
+            rows = pl.ds(sub * piece, piece)
+            dst = o_ref.at[block].at[rows]
+            first = row == 0 and index == 0
+            src = x_ref.at[rows] if first else dst
+            if row == 1:
+                ring.copy(dst, dst, over_s.at[z, sub], over_r.at[z, sub], across).wait_recv()
+            elif not first:
+                ring.copy(dst, dst, line_s.at[0, z, sub], line_r.at[z, sub], across).wait_recv()
+            if row == 0:
+                if first:
+                    for side, step in enumerate((1, -1)):
+                        there = line.z + step
+                        go_on = (there >= 0) & (there < line.length)
+                        there = jnp.where(go_on, there, line.z - step)
+                        send(go_on, src, dst, line_s.at[side, z, sub], line_r.at[z, sub], line.device(there))
+                else:
+                    there = jnp.where(z < line.z, line.z + 1, line.z - 1)
+                    go_on = (there >= 0) & (there < line.length)
+                    there = jnp.where(go_on, there, jnp.where(z < line.z, line.z - 1, line.z + 1))
+                    send(go_on, src, dst, line_s.at[0, z, sub], line_r.at[z, sub], line.device(there))
+                send(None, src, dst, over_s.at[z, sub], over_r.at[z, sub], across)
+            send(None, src, dst, sib_s.at[row, z, sub], sib_r.at[row, z, sub], ring.sibling)
+        if turn == 0:
+            for column in columns:
+                column.start()
+        else:
+            upto = count if turn == len(order) - 1 else min(count, 1 + 2 * turn)
+            for passed in range(ahead, max(ahead, upto)):
+                for column in columns:
+                    column.pass_on(passed)
+            ahead = max(ahead, upto)
+    for row, index in order:
+        z = line.nearest(index)
+        other = line.device(z, row, 1)
         for sub in range(SUBS):
             dst = o_ref.at[other].at[pl.ds(sub * piece, piece)]
             ring.copy(
-                dst, dst, sib_s.at[step, sub], sib_r.at[step, sub], ring.sibling
+                dst, dst, sib_s.at[row, z, sub], sib_r.at[row, z, sub], ring.sibling
             ).wait_recv()
-        work(step, block, other)
+    own.wait()
     return sends
+
+
+def wait_sends(sends):
+    for condition, go in sends:
+        if condition is None:
+            go.wait_send()
+        else:
+            pl.when(condition)(go.wait_send)
 
 
 def gather_kernel(count, extra, x_ref, *refs):
     parts, (o_ref, *outs), sems = refs[:extra], refs[extra : 2 * extra + 1], refs[2 * extra + 1 :]
     ring = Ring(count)
     columns = [
-        Columns(ring, count, parts[i], outs[i], sems[5 + 5 * i : 10 + 5 * i]) for i in range(extra)
+        Columns(ring, count, parts[i], outs[i], sems[7 + 5 * i : 12 + 5 * i]) for i in range(extra)
     ]
-    sends = pass_round(ring, count, x_ref, o_ref, sems[:5], columns, lambda *_: None)
-    for go in sends:
-        go.wait_send()
+    wait_sends(pass_along(ring, count, x_ref, o_ref, sems[:7], columns))
     for column in columns:
         column.finish()
 
@@ -248,7 +346,7 @@
         + [jax.ShapeDtypeStruct((groups, count) + b.shape[1:], b.dtype) for b in blocks],
         in_specs=[anywhere] * (1 + len(blocks)),
         out_specs=[anywhere] * (1 + len(blocks)),
-        scratch_shapes=ring_sems(pairs) + column_sems(count, groups) * len(blocks),
+        scratch_shapes=line_sems(count) + column_sems(count, groups) * len(blocks),
         compiler_params=pltpu.CompilerParams(collective_id=ident, has_side_effects=True),
         cost_estimate=pl.CostEstimate(flops=0, bytes_accessed=150_000_000, transcendentals=0),
         name=f"ring_gather_{ident}",
@@ -257,6 +355,12 @@
 
 def ring_sems(pairs):
     return [pltpu.SemaphoreType.DMA((pairs, SUBS)) for _ in range(4)] + [pltpu.SemaphoreType.DMA]
+
+
+def line_sems(count):
+    dma = pltpu.SemaphoreType.DMA
+    shapes = [(2, count // 4, SUBS)] + [(count // 4, SUBS)] * 3 + [(2, count // 4, SUBS)] * 2
+    return [dma(shape) for shape in shapes] + [dma]
 
 
 def column_sems(count, groups):
@@ -272,12 +376,12 @@
 def residual_kernel(
     count,
     x_ref,
-    part_ref,
+    feed_ref,
     states_ref,
     w_ref,
     vec_ref,
     heads_ref,
-    feed_ref,
+    feed_far_ref,
     b_ref,
     own_ref,
     heads,
@@ -296,7 +400,17 @@
     blocks = tokens // ROWS
     weights = pltpu.make_async_copy(w_ref, w_out, w_sem)
     weights.start()
-    columns = [Columns(ring, count, part_ref, feed_ref, sems[5:10])]
+    groups = lax.axis_size("batch")
+
+    def onward(shift):
+        return pltpu.make_async_remote_copy(
+            src_ref=feed_ref,
+            dst_ref=feed_far_ref.at[shift - 1],
+            send_sem=sems[5].at[shift - 1],
+            recv_sem=sems[6].at[shift - 1],
+            device_id=(lax.rem(ring.batch + shift, groups), ring.me),
+            device_id_type=MESH,
+        )
 
     def rows_of(block):
         return pl.ds(pl.multiple_of(block * ROWS, ROWS), ROWS)
@@ -313,60 +427,57 @@
 
     load(0).start()
 
-    def begin():
+    kept, waiting = [], []
+
+    def add(group, first, last):
+        wide = 512
+
         @pl.loop(0, blocks)
         def _(block):
-            @pl.when(block + 1 < blocks)
-            def _():
-                load(block + 1).start()
-
-            load(block).wait()
-            normal, _ = norm_parts(states[lax.rem(block, 2)].astype(F32))
-            total[rows_of(block), :] = DEEP_ALPHA * (normal * vec_ref[0:1, :] + vec_ref[1:2, :])
-
-        weights.wait()
-
-    def saves(step, block, other):
-        return [
-            pltpu.make_async_copy(heads.at[head], heads_ref.at[head], heads_sem.at[step, part])
-            for part, head in enumerate((block, other))
-        ]
-
-    kept = []
-
-    def work(step, block, other):
-        if step == 0:
-            begin()
-        for go in saves(step, block, other):
+            rows = rows_of(block)
+            left = jnp.concatenate([heads[head, rows, :] for head in group], axis=1)
+            if first:
+
+                @pl.when(block + 1 < blocks)
+                def _():
+                    load(block + 1).start()
+
+                load(block).wait()
+                normal, _ = norm_parts(states[lax.rem(block, 2)].astype(F32))
+                total[rows, :] = DEEP_ALPHA * (normal * vec_ref[0:1, :] + vec_ref[1:2, :])
+            for at in range(0, D, wide):
+                right = [
+                    w_out[pl.ds(pl.multiple_of(head * HD, HD), HD), at : at + wide]
+                    for head in group
+                ]
+                total[rows, at : at + wide] += nn(left, jnp.concatenate(right, axis=0))
+            if last:
+
+                @pl.when(block >= 2)
+                def _():
+                    store(block - 2).wait()
+
+                normal, _ = norm_parts(total[rows, :])
+                low[lax.rem(block, 2)] = (normal * vec_ref[2:3, :] + vec_ref[3:4, :]).astype(BF)
+                store(block).start()
+
+    def work(block, other):
+        turn, turns = len(kept) // 2, count // 2
+        if turn == 0:
+            for shift in range(1, groups):
+                onward(shift).start()
+        for part, head in enumerate((block, other)):
+            go = pltpu.make_async_copy(heads.at[head], heads_ref.at[head], heads_sem.at[turn, part])
             go.start()
             kept.append(go)
-        wide = 512
-
-        @pl.loop(0, blocks)
-        def _(part):
-            rows = rows_of(part)
-            left = jnp.concatenate([heads[block, rows, :], heads[other, rows, :]], axis=1)
-            for at in range(0, D, wide):
-                right = jnp.concatenate(
-                    [
-                        w_out[pl.ds(pl.multiple_of(head * HD, HD), HD), at : at + wide]
-                        for head in (block, other)
-                    ],
-                    axis=0,
-                )
-                total[rows, at : at + wide] += nn(left, right)
-
-    sends = pass_round(ring, count, x_ref, heads, sems[:5], columns, work)
-
-    @pl.loop(0, blocks)
-    def _(block):
-        @pl.when(block >= 2)
-        def _():
-            store(block - 2).wait()
-
-        normal, _ = norm_parts(total[rows_of(block), :])
-        low[lax.rem(block, 2)] = (normal * vec_ref[2:3, :] + vec_ref[3:4, :]).astype(BF)
-        store(block).start()
+            waiting.append(head)
+        if turn == 1:
+            weights.wait()
+        if turn == turns - 1 or turn in (1, turns // 2, turns - 2):
+            add(list(waiting), turn == 1, turn == turns - 1)
+            waiting.clear()
+
+    sends = pass_round(ring, count, 2, x_ref, heads, sems[:5], [], work)
 
     own_ref[...] = total[pl.ds(pl.multiple_of(ring.me * own, own), own), :]
     for block in (blocks - 2, blocks - 1):
@@ -375,11 +486,11 @@
         go.wait()
     for go in sends:
         go.wait_send()
-    for column in columns:
-        column.finish()
-
-
-def gather_residual(attended, feed_cut, states, w_out, vectors, own, count, ident):
+    for shift in range(1, groups):
+        onward(shift).wait()
+
+
+def gather_residual(attended, feed_own, states, w_out, vectors, own, count, ident):
     tokens = attended.shape[0]
     pairs, groups = count // 2, lax.axis_size("batch")
     inside, anywhere = pl.BlockSpec(memory_space=pltpu.VMEM), pl.BlockSpec(memory_space=pl.ANY)
@@ -387,7 +498,7 @@
         functools.partial(residual_kernel, count),
         out_shape=[
             jax.ShapeDtypeStruct((count, tokens, HD), BF),
-            jax.ShapeDtypeStruct((groups,) + feed_cut.shape, BF),
+            jax.ShapeDtypeStruct((groups - 1,) + feed_own.shape, BF),
             jax.ShapeDtypeStruct((tokens, D), BF),
             jax.ShapeDtypeStruct((own, D), F32),
         ],
@@ -405,13 +516,13 @@
             pltpu.SemaphoreType.DMA((pairs, 2)),
         ]
         + ring_sems(pairs)
-        + column_sems(count, groups),
+        + [pltpu.SemaphoreType.DMA((max(1, groups - 1),)) for _ in range(2)],
         compiler_params=vmem(collective_id=ident, has_side_effects=True),
         cost_estimate=pl.CostEstimate(
             flops=2 * tokens * D * D, bytes_accessed=200_000_000, transcendentals=0
         ),
         name="gather_residual",
-    )(attended, feed_cut, states, w_out, vectors)
+    )(attended, feed_own, states, w_out, vectors)
 
 
 class RingSum:
@@ -621,7 +732,8 @@
     span,
     b_ref,
     cot_ref,
-    w_ref,
+    feed_own_ref,
+    feed_far_ref,
     w_out_ref,
     res_ref,
     cot_own_ref,
@@ -638,6 +750,7 @@
     h,
     du,
     tiles,
+    w_ref,
     db_ref,
     do_send,
     *rest,
@@ -682,9 +795,21 @@
             for which, ref in enumerate((b_ref, cot_ref))
         ]
 
+    def feed_rows(shift):
+        part = D // groups
+        begin = lax.rem(ring.batch - shift + groups, groups) * part
+        src = feed_own_ref if shift == 0 else feed_far_ref.at[shift - 1]
+        return pltpu.make_async_copy(
+            src, w_ref.at[pl.ds(pl.multiple_of(begin, part), part)], rest[24].at[shift]
+        )
+
     for go in row_loads(0):
         go.start()
+    for shift in range(groups):
+        feed_rows(shift).start()
     ring.greet_all(count)
+    for shift in range(groups):
+        feed_rows(shift).wait()
 
     def feed(step):
         slot = lax.rem(step, 2)
@@ -753,18 +878,19 @@
             go.wait()
         values = jnp.concatenate([tn(tiles[slot, 0], du[...]), tn(tiles[slot, 1], h[...])], axis=1)
         grads.put(tile, values)
-        later = pairs // 2 + tile // 3
-
-        @pl.when((lax.rem(tile, 3) == 1) & (later < pairs))
+        later = pairs // 2 + tile // 2
+
+        @pl.when((lax.rem(tile, 2) == 1) & (later < pairs))
         def _():
             sums[0].advance(later)
 
-    passed = pairs // 2 + len([t for t in range(grads.tiles) if t % 3 == 1])
+    passed = pairs // 2 + grads.tiles // 2
 
     @pl.loop(min(passed, pairs), pairs)
     def _(step):
         sums[0].advance(step)
 
+    sums[1].advance(0)
     normal, inverse = norm_parts(res_ref[...])
     slope = DEEP_ALPHA * cot_own_ref[...].astype(F32) + db_ref[...]
     dr, gain_sum, bias_sum = norm_back(normal, inverse, slope, vec_ref[2:3, :])
@@ -782,7 +908,7 @@
             dr_send[at // HD] = dr_low[:, at : at + HD]
     exchange.start()
 
-    @pl.loop(0, pairs)
+    @pl.loop(1, pairs)
     def _(step):
         sums[1].advance(step)
 
@@ -795,13 +921,15 @@
         each.finish()
 
 
-def feed_forward(b_low, cot, w_feed, w_out, residual, cot_own, vectors, count, groups, ident):
-    tokens, span, pairs = b_low.shape[0], w_feed.shape[1] // 3, count // 2
+def feed_forward(
+    b_low, cot, feed_own, feed_far, w_out, residual, cot_own, vectors, count, groups, ident
+):
+    tokens, span, pairs = b_low.shape[0], feed_own.shape[1] // 3, count // 2
     own = residual.shape[0]
     inside, anywhere = pl.BlockSpec(memory_space=pltpu.VMEM), pl.BlockSpec(memory_space=pl.ANY)
     return pl.pallas_call(
         functools.partial(feed_kernel, count, groups, span),
-        in_specs=[anywhere, anywhere, inside, anywhere, inside, inside, inside],
+        in_specs=[anywhere] * 5 + [inside] * 3,
         out_specs=[inside] * 4 + [anywhere, inside],
         out_shape=[
             jax.ShapeDtypeStruct((own, D), F32),
@@ -818,19 +946,21 @@
             pltpu.VMEM((tokens, span), BF),
             pltpu.VMEM((tokens, 2 * span), BF),
             pltpu.VMEM((2, 2, tokens, ROWS), BF),
+            pltpu.VMEM((D, 3 * span), BF),
             pltpu.VMEM((own, D), F32),
             pltpu.VMEM((count, own, HD), BF),
         ]
         + RingSum.scratch(pairs, own) * 2
         + GroupSum.scratch(groups, 3 * span)
         + [pltpu.SemaphoreType.DMA((2, 4)), pltpu.SemaphoreType.DMA((2, 2)), pltpu.SemaphoreType.DMA((4,))]
-        + Exchange.scratch(count),
+        + Exchange.scratch(count)
+        + [pltpu.SemaphoreType.DMA((groups,))],
         compiler_params=vmem(62 * 1024 * 1024, collective_id=ident, has_side_effects=True),
         cost_estimate=pl.CostEstimate(
             flops=18 * tokens * D * span, bytes_accessed=250_000_000, transcendentals=0
         ),
         name="feed_forward",
-    )(b_low, cot, w_feed, w_out, residual, cot_own, vectors)
+    )(b_low, cot, feed_own, feed_far, w_out, residual, cot_own, vectors)
 
 
 def project_kernel(
@@ -932,11 +1062,11 @@
         def _():
             terms_of(tile + 1)
 
-        @pl.when((lax.rem(tile, 4) == 3) & (tile // 4 + 1 < pairs))
+        @pl.when((lax.rem(tile, 2) == 1) & (tile // 2 + 1 < pairs))
         def _():
-            sums.advance(tile // 4 + 1)
-
-    @pl.loop(1 + grads.tiles // 4, pairs)
+            sums.advance(tile // 2 + 1)
+
+    @pl.loop(1 + grads.tiles // 2, pairs)
     def _(step):
         sums.advance(step)
 
@@ -1410,18 +1540,20 @@
     w_qkv = w_qkv.reshape(D, 3 * HD)
     vectors = vectors[..., :rows].transpose(2, 0, 1, 3).reshape(8, D)
     w_out = lax.all_gather(out_cut, ("batch", "seq"), axis=0, tiled=True)
+    feed_cut, w_qkv = lax.optimization_barrier((feed_cut, w_qkv))
+    feed_own = lax.all_to_all(feed_cut, "seq", split_axis=0, concat_axis=0, tiled=True)
+    feed_own = feed_own.reshape(D // groups, 3 * span)
     cot_all = lax.all_gather(cotangent, "seq", axis=0, tiled=True)
 
     spans, place = chain_spans(lengths[0], prefix[0], padding[0], tokens)
     cosine, sine = rotary_tables(place)
     a_low, query, key, value, key_t, value_t = norm_and_project(states, w_qkv, vectors, cosine, sine)
     attended, full, log = attend(query, key, value_t, spans)
-    heads, w_feed, b_low, residual = gather_residual(
-        attended, feed_cut, states, w_out, vectors, own, seq, 2
+    heads, feed_far, b_low, residual = gather_residual(
+        attended, feed_own, states, w_out, vectors, own, seq, 2
     )
-    w_feed = w_feed.reshape(D, 3 * span)
     out_sum, grad_feed, dr, vec_sums, do, dr_cut = feed_forward(
-        b_low, cot_all, w_feed, w_out, residual, cotangent, vectors, seq, groups, 3
+        b_low, cot_all, feed_own, feed_far, w_out, residual, cotangent, vectors, seq, groups, 3
     )
     dr_cols = lax.all_to_all(dr_cut, "seq", split_axis=0, concat_axis=0, tiled=True)
     normal_two, _ = norm_parts(residual)

time: 605 us -> 590 us (0.975)
  Pallas kernels: 548 us -> 475 us
  waiting for transfers between devices: 7.03 us -> 48.4 us
  starting transfers between devices: 9.77 us -> 27.3 us
    all_to_all x0 -> x1, waiting for transfers between devices: none -> 41.4 us  [on_device(): lax.all_to_all(feed_cut, 'seq', split_axis=0, concat_axis=0, tiled=True)]
    pallas_call x1, Pallas kernels: 124 us -> 85.8 us  [gather_residual(): pl.pallas_call(functools.partial(residual_kernel, count), out_shape=[jax....]
    pallas_call x1, Pallas kernels: 110 us -> 85.8 us  [ring_gather(): pl.pallas_call(functools.partial(gather_kernel, count, len(blocks)), out_...]
    all_to_all x0 -> x1, starting transfers between devices: none -> 17.5 us  [on_device(): lax.all_to_all(feed_cut, 'seq', split_axis=0, concat_axis=0, tiled=True)]
    pallas_call x1, Pallas kernels: 115 us -> 107 us  [project_back(): pl.pallas_call(functools.partial(project_kernel, count, groups), in_specs...]
  transfers between devices with their start and end apart: 4 -> 5, of which waited for: 1 -> 2; matrix products, arithmetic and copies ran while one was open for 3% -> 3% of each run, Pallas kernels for 49% -> 40%
where the time goes in v4:
time: 590 us; the launch traced here: 584 us
  Pallas kernels  475 us (81%)
  waiting for transfers between devices  48.4 us (8%)
  starting transfers between devices  27.3 us (5%)
  between operations  14.5 us (2%)
  local copies, waits for them, and re-layouts  10.4 us (2%)
  other arithmetic  8.74 us (1%)
    pallas_call x1, Pallas kernels, feed_forward(): pl.pallas_call(functools.partial(feed_kernel, count, groups, span), in_sp...  122 us
    pallas_call x1, Pallas kernels, project_back(): pl.pallas_call(functools.partial(project_kernel, count, groups), in_specs...  107 us
    pallas_call x1, Pallas kernels, ring_gather(): pl.pallas_call(functools.partial(gather_kernel, count, len(blocks)), out_...  85.8 us
    pallas_call x1, Pallas kernels, gather_residual(): pl.pallas_call(functools.partial(residual_kernel, count), out_shape=[jax....  85.8 us
    all_to_all x1, waiting for transfers between devices, on_device(): lax.all_to_all(feed_cut, 'seq', split_axis=0, concat_axis=0, tiled=True)  41.4 us
    pallas_call x2, Pallas kernels, update(): pl.pallas_call(functools.partial(update_kernel, first_step, steps, tile_a...  23.9 us
    all_to_all x1, starting transfers between devices, on_device(): lax.all_to_all(feed_cut, 'seq', split_axis=0, concat_axis=0, tiled=True)  17.5 us
    pallas_call x1, Pallas kernels, attend_back(): pl.pallas_call(attend_back_kernel, grid_spec=pltpu.PrefetchScalarGridSpec...  16.6 us
  transfers between devices with their start and end apart: 5, of which 2 were waited for; matrix products, arithmetic and copies ran while one was open for 3% of the time, Pallas kernels for 40%

profile of v4, /device:TPU:9, one launch (start us, length us, event | category | flops | bytes accessed | tf_op | source)
XLA Modules:
  0.0 584.4 jit_solution(1849748437823672215)
XLA Ops:
  7.2 0.0 copy-start.8
  7.2 0.0 copy-start.9
  7.2 0.0 copy-start.7
  7.2 0.0 all-gather.3.cloned.1.call-start
  7.2 5.1 lay_out.1
  12.3 0.0 all-gather.3.cloned.1.call-update
  12.4 0.0 all-gather.5.cloned.1.call-start
  12.4 0.7 all-gather.5.cloned.1.call-update
  13.1 0.9 slice.38
  14.0 0.1 copy.28
  14.1 0.6 bitcast_convert_fusion.refs_1_
  14.7 85.8 %ring_gather_1.1 = (bf16[16,128,2048]{2,1,0:T(8,128)(2,1)}, bf16[2,16,64,384]{3,2,1,0:T(8,128)(2,1)}, f32[2,16,8,128]{3,2,1,0:T(8,128)}) custom-call(bf16[128,2048]{1,0:T(8,128)(2,1)} %x_ref.3, bf16[16,64,384]{2,1,0:T(8,128)(2,1)} %get-tuple-element.45.refs_0_, f32[1,8,128]{2,1,0:T(8,128)} %bitcast_convert_fusion.refs_1_), custom_call_target="tpu_custom_call" | custom-call | bytes 150000000 | tf_op jit(solution)/shard_map/ring_gather_1/pallas_call | solution.py:343
  100.5 17.5 %all-to-all-start = ((bf16[16,64,1152]{2,1,0:T(8,128)(2,1)}), bf16[16,64,1152]{2,1,0:T(8,128)(2,1)S(1)}, u32[]{:S(2)}, u32[]{:S(2)}) async-start(bf16[16,64,1152]{2,1,0:T(8,128)(2,1)} %get-tuple-element.55), calls=%async_computation | async-start | bytes 4718592 | tf_op jit(solution)/shard_map/all_to_all | solution.py:1544
  118.0 0.0 copy-done.8
  118.0 0.2 reduce-window.4
  118.2 0.0 copy-done.9
  118.2 0.0 copy-done.7
  118.2 0.2 select_reduce_fusion.1
  118.4 0.1 slice.24
  118.5 0.1 slice.25
  118.6 0.9 slice_bitcast_fusion
  119.6 0.7 reshape.116.vec_ref
  120.3 0.6 and_select_fusion
  120.9 3.7 fusion
  124.6 1.9 pad_maximum_fusion
  126.6 15.5 %norm_and_project.1 = (bf16[2048,2048]{1,0:T(8,128)(2,1)}, bf16[2048,128]{1,0:T(8,128)(2,1)}, bf16[2048,128]{1,0:T(8,128)(2,1)}, bf16[2048,128]{1,0:T(8,128)(2,1...) custom-call(bf16[2048,2048]{1,0:T(8,128)(2,1)} %bitcast.30, bf16[2048,384]{1,0:T(8,128)(2,1)} %bitcast.32, ...), custom_call_target="tpu_custom_call" | custom-call | flops 3221225472 | bytes 24000000 | tf_op jit(solution)/shard_map/norm_and_project/pallas_call | solution.py:1151
  142.1 1.3 broadcast_in_dim.72.first_ref
  143.4 1.3 broadcast_in_dim.74.last_ref
  144.7 12.4 %attend.1 = (bf16[2048,128]{1,0:T(8,128)(2,1)}, f32[8,128,256]{2,1,0:T(8,128)}, f32[8,1,256]{2,1,0:T(1,128)}) custom-call(s32[8]{0:T(128)} %get-tuple-element.98.low_ref, s32[8]{0:T(128)} %get-tuple-element.97.high_ref, bf16[2048,128]{1,0:T(8,128)(2,1)} %get-tuple-element.51.q_ref, bf16[4,512,128]{2,1,0:T(8,128)(2,1)} %bitcast.43, ...), custom_call_target="tpu_custom_call" | custom-call | flops 1073741824 | bytes 4000000 | tf_op jit(solution)/shard_map/attend/pallas_call | solution.py:1212
  157.1 41.4 %all-to-all-done = bf16[16,64,1152]{2,1,0:T(8,128)(2,1)S(1)} async-done(((bf16[16,64,1152]{2,1,0:T(8,128)(2,1)}), bf16[16,64,1152]{2,1,0:T(8,128)(2,1)S(1)}, u32[]{:S(2)}, u32[]{:S(2)}) %all-to-all-start) | async-done | bytes 2359328 | tf_op jit(solution)/shard_map/all_to_all | solution.py:1544
  198.5 0.0 copy-start.2
  198.5 0.0 all-gather.3.cloned.1.call-done.w_ref.w_out_ref
  198.5 1.4 copy-done.2
  199.9 85.8 %gather_residual.1 = (bf16[16,2048,128]{2,1,0:T(8,128)(2,1)}, bf16[1,1024,1152]{2,1,0:T(8,128)(2,1)}, bf16[2048,2048]{1,0:T(8,128)(2,1)}, f32[128,2048]{1,0:T(8,128)}) custom-call(bf16[2048,128]{1,0:T(8,128)(2,1)} %get-tuple-element.54.x_ref, bf16[1024,1152]{1,0:T(8,128)(2,1)} %bitcast.34, bf16[2048,2048]{1,0:T(8,128)(2,1)} %bitcast.31, ...), custom_call_target="tpu_custom_call" | custom-call | flops 17179869184 | bytes 200000000 | tf_op jit(solution)/shard_map/gather_residual/pallas_call | solution.py:497
  285.7 0.0 all-gather.5.cloned.1.call-done.cot_ref
  285.7 122.5 %feed_forward.1 = (f32[128,2048]{1,0:T(8,128)}, bf16[4,256,1152]{2,1,0:T(8,128)(2,1)}, f32[128,2048]{1,0:T(8,128)}, f32[2,2048]{1,0:T(2,128)}, bf16[16,128,128]{...) custom-call(bf16[2048,2048]{1,0:T(8,128)(2,1)} %get-tuple-element.58.b_ref, ...), custom_call_target="tpu_custom_call" | custom-call | flops 28991029248 | bytes 250000000 | tf_op jit(solution)/shard_map/feed_forward/pallas_call | solution.py:930
  408.2 4.3 all-to-all-start.1
  412.6 16.6 %attend_back.1.dp_ref = bf16[2048,384]{1,0:T(8,128)(2,1)} custom-call(s32[8]{0:T(128)} %get-tuple-element.98.low_ref, s32[8]{0:T(128)} %get-tuple-element.97.high_ref, bf16[2048,128]{1,0:T(8,128)(2,1)} %get-tuple-element.51.q_ref, bf16[2048,128]{1,0:T(8,128)(2,1)} %bitcast.46, f32[8,128,256]{2,1,0:T(8,128)} %get-tuple-element.62.full_ref, ...), custom_call_target="tpu_custom_call" | custom-call | flops 2684354560 | bytes 6000000 | tf_op jit(solution)/shard_map/attend_back/pallas_call | solution.py:1305
  429.1 0.0 all-to-all-done.1
  429.1 0.0 copy-start.3
  429.1 0.8 copy-done.3
  429.9 0.0 copy-start
  429.9 0.0 copy-start.4
  429.9 107.3 %project_back.1 = (bf16[128,2048]{1,0:T(8,128)(2,1)}, bf16[4,256,512]{2,1,0:T(8,128)(2,1)}, bf16[16,64,1152]{2,1,0:T(8,128)(2,1)}, f32[8,128]{1,0:T(8,128)}) custom-call(bf16[2048,384]{1,0:T(8,128)(2,1)} %attend_back.1.dp_ref, bf16[2048,384]{1,0:T(8,128)(2,1)} %bitcast.33, bf16[2048,2048]{1,0:T(8,128)(2,1)} %get-tuple-element.66.a_ref, ...), custom_call_target="tpu_custom_call" | custom-call | flops 6442450944 | bytes 200000000 | tf_op jit(solution)/shard_map/project_back/pallas_call | solution.py:1096
  537.3 0.0 copy-start.6
  537.3 5.4 all-to-all-start.2
  542.7 0.1 slice_reduce_fusion.1
  542.8 0.1 add.44
  542.9 0.1 mul.52
  543.0 0.0 copy-done
  543.0 0.1 reduce_sum.67
  543.1 0.3 multiply_reduce_fusion
  543.4 0.0 copy-done.4
  543.4 1.1 add_convert_fusion
  544.5 0.0 copy-done.6
  544.5 0.1 copy.27
  544.6 0.6 pad.10.refs_1_
  545.3 15.9 %update_4.1 = (f32[64,24579]{1,0:T(8,128)}, f32[64,24579]{1,0:T(8,128)}, f32[64,24579]{1,0:T(8,128)}, f32[64,24579]{1,0:T(8,128)}) custom-call(bf16[16,64,1152]{2,1,0:T(8,128)(2,1)} %get-tuple-element.74.refs_0_, f32[64,128]{1,0:T(8,128)} %pad.10.refs_1_, f32[64,24579]{1,0:T(8,128)} %refs_1_.1, f32[64,24579]{1,0:T(8,128)} %refs_2_.3, f32[64,24579]{1,0:T(8,128)} %refs_3_.3, ...), custom_call_target="tpu_custom_call" | custom-call | bytes 42467328 | tf_op jit(solution)/shard_map/update_4/pallas_call | solution.py:1483
  561.2 6.3 %all-to-all-done.2.refs_0_ = bf16[16,64,512]{2,1,0:T(8,128)(2,1)S(1)} async-done(((bf16[16,64,512]{2,1,0:T(8,128)(2,1)}), bf16[16,64,512]{2,1,0:T(8,128)(2,1)S(1)}, u32[]{:S(2)}, u32[]{:S(2)}) %all-to-all-start.2) | async-done | bytes 1048608 | tf_op jit(solution)/shard_map/all_to_all | solution.py:1526
  567.5 0.0 copy-start.1
  567.5 1.0 copy-done.1
  568.4 8.0 %update_0.1 = (f32[64,24579]{1,0:T(8,128)}, f32[64,24579]{1,0:T(8,128)}, f32[64,24579]{1,0:T(8,128)}, f32[64,24579]{1,0:T(8,128)}) custom-call(bf16[16,64,512]{2,1,0:T(8,128)(2,1)} %copy-done.1, f32[64,24579]{1,0:T(8,128)} %refs_1_.1, f32[64,24579]{1,0:T(8,128)} %refs_2_.3, ...), custom_call_target="tpu_custom_call", output_to_operand_aliasing={{0}: (5, {}), {1}: (6, {}), {2}: (7, {}), {3}: (8, {})} | custom-call | bytes 18874368 | tf_op jit(solution)/shard_map/update_0/pallas_call | solution.py:1483
  576.4 0.0 copy-done.5
  576.4 0.8 copy.34
  (13 shorter events, 0.1 us)
Async XLA Ops:
  7.2 110.9 %copy-start.8 = (s32[1,4]{1,0:T(1,128)S(1)}, s32[1,4]{1,0:T(1,128)}, u32[]{:S(2)}) copy-start(s32[1,4]{1,0:T(1,128)} %param.15) | copy-start | bytes 52
  7.2 111.0 %copy-start.9 = (s32[1,4]{1,0:T(1,128)S(1)}, s32[1,4]{1,0:T(1,128)}, u32[]{:S(2)}) copy-start(s32[1,4]{1,0:T(1,128)} %param.17) | copy-start | bytes 52
  7.2 111.0 %copy-start.7 = (s32[1,4]{1,0:T(1,128)S(1)}, s32[1,4]{1,0:T(1,128)}, u32[]{:S(2)}) copy-start(s32[1,4]{1,0:T(1,128)} %param.16) | copy-start | bytes 52
  7.2 191.3 %all-gather.3.cloned.1.call-start = ((), (), s32[]{:S(2)}) async-start(), calls=%async_computation.3 | async-start | bytes 8650752 | tf_op jit(solution)/shard_map/all_gather | solution.py:1542
  12.4 273.4 %all-gather.5.cloned.1.call-start = ((), (), s32[]{:S(2)}) async-start(), calls=%async_computation.4 | async-start | bytes 8912896 | tf_op jit(solution)/shard_map/all_gather | solution.py:1546
  100.5 98.0 %all-to-all-start = ((bf16[16,64,1152]{2,1,0:T(8,128)(2,1)}), bf16[16,64,1152]{2,1,0:T(8,128)(2,1)S(1)}, u32[]{:S(2)}, u32[]{:S(2)}) async-start(bf16[16,64,1152]{2,1,0:T(8,128)(2,1)} %get-tuple-element.55), calls=%async_computation | async-start | bytes 4718592 | tf_op jit(solution)/shard_map/all_to_all | solution.py:1544
  198.5 1.4 copy-start.2
  408.2 20.9 %all-to-all-start.1 = ((bf16[16,128,128]{2,1,0:T(8,128)(2,1)}), bf16[16,128,128]{2,1,0:T(8,128)(2,1)S(1)}, u32[]{:S(2)}, u32[]{:S(2)}) async-start(bf16[16,128,128]{2,1,0:T(8,128)(2,1)} %get-tuple-element.68), calls=%async_computation.1 | async-start | bytes 1048576 | tf_op jit(solution)/shard_map/all_to_all | solution.py:1558
  429.1 0.8 copy-start.3
  429.9 113.1 %copy-start = (f32[128,2048]{1,0:T(8,128)S(1)}, f32[128,2048]{1,0:T(8,128)}, u32[]{:S(2)}) copy-start(f32[128,2048]{1,0:T(8,128)} %get-tuple-element.57.res_ref) | copy-start | bytes 3145732
  429.9 113.5 %copy-start.4 = (f32[128,2048]{1,0:T(8,128)S(1)}, f32[128,2048]{1,0:T(8,128)}, u32[]{:S(2)}) copy-start(f32[128,2048]{1,0:T(8,128)} %get-tuple-element.60) | copy-start | bytes 3145732
  537.3 7.3 %copy-start.6 = (f32[8,128]{1,0:T(8,128)S(1)}, f32[8,128]{1,0:T(8,128)}, u32[]{:S(2)}) copy-start(f32[8,128]{1,0:T(8,128)} %get-tuple-element.75) | copy-start | bytes 12292
  537.3 30.2 %all-to-all-start.2 = ((bf16[16,64,512]{2,1,0:T(8,128)(2,1)}), bf16[16,64,512]{2,1,0:T(8,128)(2,1)S(1)}, u32[]{:S(2)}, u32[]{:S(2)}) async-start(bf16[16,64,512]{2,1,0:T(8,128)(2,1)} %bitcast.38), calls=%async_computation.2 | async-start | bytes 2097152 | tf_op jit(solution)/shard_map/all_to_all | solution.py:1526
  567.5 1.0 copy-start.1
  568.4 8.0 %copy-start.5 = (bf16[128,2048]{1,0:T(8,128)(2,1)S(1)}, bf16[128,2048]{1,0:T(8,128)(2,1)}, u32[]{:S(2)}) copy-start(bf16[128,2048]{1,0:T(8,128)(2,1)} %get-tuple-element.106) | copy-start | bytes 1572868
Sparse Core Ops, SparseCore 0:
  12.5 104.7 all-gather.2
  119.4 107.4 all-gather.4

commit v5 on v4

--- a/solution.py
+++ b/solution.py
@@ -373,34 +373,39 @@
     ]
 
 
-def residual_kernel(
-    count,
-    x_ref,
-    feed_ref,
-    states_ref,
-    w_ref,
-    vec_ref,
-    heads_ref,
-    feed_far_ref,
-    b_ref,
-    own_ref,
-    heads,
-    w_out,
-    total,
-    states,
-    low,
-    w_sem,
-    load_sem,
-    store_sem,
-    heads_sem,
-    *sems,
-):
+def residual_kernel(count, groups, x_ref, feed_ref, states_ref, vec_ref, plane_ref, *refs):
+    far_refs, refs = refs[: groups - 1], refs[groups - 1 :]
+    heads_ref, feed_far_ref, b_ref, w_ref, own_ref, heads, w_out, total, states, low = refs[:10]
+    w_sem, load_sem, store_sem, heads_sem, *sems = refs[10:]
     ring = Ring(count)
     tokens, own = total.shape[0], own_ref.shape[0]
     blocks = tokens // ROWS
-    weights = pltpu.make_async_copy(w_ref, w_out, w_sem)
-    weights.start()
-    groups = lax.axis_size("batch")
+    part = D // groups
+    half = part // 2
+
+    def held_rows(shift):
+        begin = lax.rem(ring.batch - shift + groups, groups) * part
+        if shift == 0:
+            return w_out.at[pl.ds(pl.multiple_of(begin, part), part)]
+        return w_out.at[pl.ds(pl.multiple_of(begin + ring.core * half, half), half)]
+
+    weights = [
+        pltpu.make_async_copy(ref, held_rows(shift), w_sem.at[shift])
+        for shift, ref in enumerate((plane_ref,) + far_refs)
+    ]
+    for go in weights:
+        go.start()
+
+    def handed(shift):
+        return ring.copy(
+            far_refs[shift - 1],
+            held_rows(shift),
+            sems[7].at[shift - 1],
+            sems[8].at[shift - 1],
+            ring.sibling,
+        )
+
+    keep = pltpu.make_async_copy(w_out, w_ref, w_sem.at[groups])
 
     def onward(shift):
         return pltpu.make_async_remote_copy(
@@ -465,6 +470,7 @@
         turn, turns = len(kept) // 2, count // 2
         if turn == 0:
             for shift in range(1, groups):
+                handed(shift).start()
                 onward(shift).start()
         for part, head in enumerate((block, other)):
             go = pltpu.make_async_copy(heads.at[head], heads_ref.at[head], heads_sem.at[turn, part])
@@ -472,7 +478,11 @@
             kept.append(go)
             waiting.append(head)
         if turn == 1:
-            weights.wait()
+            for go in weights:
+                go.wait()
+            for shift in range(1, groups):
+                handed(shift).wait()
+            keep.start()
         if turn == turns - 1 or turn in (1, turns // 2, turns - 2):
             add(list(waiting), turn == 1, turn == turns - 1)
             waiting.clear()
@@ -488,41 +498,43 @@
         go.wait_send()
     for shift in range(1, groups):
         onward(shift).wait()
-
-
-def gather_residual(attended, feed_own, states, w_out, vectors, own, count, ident):
+    keep.wait()
+
+
+def gather_residual(attended, feed_own, states, vectors, w_plane, w_far, own, count, ident):
     tokens = attended.shape[0]
     pairs, groups = count // 2, lax.axis_size("batch")
     inside, anywhere = pl.BlockSpec(memory_space=pltpu.VMEM), pl.BlockSpec(memory_space=pl.ANY)
     return pl.pallas_call(
-        functools.partial(residual_kernel, count),
+        functools.partial(residual_kernel, count, groups),
         out_shape=[
             jax.ShapeDtypeStruct((count, tokens, HD), BF),
             jax.ShapeDtypeStruct((groups - 1,) + feed_own.shape, BF),
             jax.ShapeDtypeStruct((tokens, D), BF),
+            jax.ShapeDtypeStruct((D, D), BF),
             jax.ShapeDtypeStruct((own, D), F32),
         ],
-        in_specs=[anywhere] * 4 + [inside],
-        out_specs=[anywhere] * 3 + [inside],
+        in_specs=[anywhere] * 3 + [inside] + [anywhere] * (1 + len(w_far)),
+        out_specs=[anywhere] * 4 + [inside],
         scratch_shapes=[
             pltpu.VMEM((count, tokens, HD), BF),
             pltpu.VMEM((D, D), BF),
             pltpu.VMEM((tokens, D), F32),
             pltpu.VMEM((2, ROWS, D), BF),
             pltpu.VMEM((2, ROWS, D), BF),
-            pltpu.SemaphoreType.DMA,
+            pltpu.SemaphoreType.DMA((groups + 1,)),
             pltpu.SemaphoreType.DMA((2,)),
             pltpu.SemaphoreType.DMA((2,)),
             pltpu.SemaphoreType.DMA((pairs, 2)),
         ]
         + ring_sems(pairs)
-        + [pltpu.SemaphoreType.DMA((max(1, groups - 1),)) for _ in range(2)],
+        + [pltpu.SemaphoreType.DMA((max(1, groups - 1),)) for _ in range(4)],
         compiler_params=vmem(collective_id=ident, has_side_effects=True),
         cost_estimate=pl.CostEstimate(
             flops=2 * tokens * D * D, bytes_accessed=200_000_000, transcendentals=0
         ),
         name="gather_residual",
-    )(attended, feed_own, states, w_out, vectors)
+    )(attended, feed_own, states, vectors, w_plane, *w_far)
 
 
 class RingSum:
@@ -1539,8 +1551,14 @@
     states = states.reshape(tokens, D)
     w_qkv = w_qkv.reshape(D, 3 * HD)
     vectors = vectors[..., :rows].transpose(2, 0, 1, 3).reshape(8, D)
-    w_out = lax.all_gather(out_cut, ("batch", "seq"), axis=0, tiled=True)
-    feed_cut, w_qkv = lax.optimization_barrier((feed_cut, w_qkv))
+    w_plane = lax.all_gather(out_cut, "seq", axis=0, tiled=True)
+    feed_cut, w_plane, w_qkv = lax.optimization_barrier((feed_cut, w_plane, w_qkv))
+    half = w_plane.shape[0] // 2
+    half_mine = lax.dynamic_slice_in_dim(w_plane, lax.rem(lax.axis_index("seq"), 2) * half, half, 0)
+    w_far = []
+    for shift in range(1, groups):
+        far = [(index, (index + shift) % groups) for index in range(groups)]
+        w_far.append(lax.ppermute(half_mine, "batch", far))
     feed_own = lax.all_to_all(feed_cut, "seq", split_axis=0, concat_axis=0, tiled=True)
     feed_own = feed_own.reshape(D // groups, 3 * span)
     cot_all = lax.all_gather(cotangent, "seq", axis=0, tiled=True)
@@ -1549,8 +1567,8 @@
     cosine, sine = rotary_tables(place)
     a_low, query, key, value, key_t, value_t = norm_and_project(states, w_qkv, vectors, cosine, sine)
     attended, full, log = attend(query, key, value_t, spans)
-    heads, feed_far, b_low, residual = gather_residual(
-        attended, feed_own, states, w_out, vectors, own, seq, 2
+    heads, feed_far, b_low, w_out, residual = gather_residual(
+        attended, feed_own, states, vectors, w_plane, w_far, own, seq, 2
     )
     out_sum, grad_feed, dr, vec_sums, do, dr_cut = feed_forward(
         b_low, cot_all, feed_own, feed_far, w_out, residual, cotangent, vectors, seq, groups, 3

time: 590 us -> 580 us (0.983)
  Pallas kernels: 475 us -> 463 us
    pallas_call x1, Pallas kernels: 85.8 us -> 75 us  [gather_residual(): pl.pallas_call(functools.partial(residual_kernel, count, groups), out_sha...]
    ppermute x0 -> x1, waiting for transfers between devices: none -> 9.3 us  [on_device(): w_far.append(lax.ppermute(half_mine, 'batch', far))]
    all_to_all x1, waiting for transfers between devices: 41.4 us -> 35.3 us  [on_device(): lax.all_to_all(feed_cut, 'seq', split_axis=0, concat_axis=0, tiled=True)]
  transfers between devices with their start and end apart: 5 -> 6, of which waited for: 2 -> 3; matrix products, arithmetic and copies ran while one was open for 3% -> 3% of each run, Pallas kernels for 40% -> 38%
where the time goes in v5:
time: 580 us; the launch traced here: 576 us
  Pallas kernels  463 us (80%)
  waiting for transfers between devices  51.7 us (9%)
  starting transfers between devices  24.4 us (4%)
  between operations  14.5 us (2%)
  local copies, waits for them, and re-layouts  13.6 us (2%)
  other arithmetic  8.7 us (1%)
    pallas_call x1, Pallas kernels, feed_forward(): pl.pallas_call(functools.partial(feed_kernel, count, groups, span), in_sp...  120 us
    pallas_call x1, Pallas kernels, project_back(): pl.pallas_call(functools.partial(project_kernel, count, groups), in_specs...  111 us
    pallas_call x1, Pallas kernels, ring_gather(): pl.pallas_call(functools.partial(gather_kernel, count, len(blocks)), out_...  84.3 us
    pallas_call x1, Pallas kernels, gather_residual(): pl.pallas_call(functools.partial(residual_kernel, count, groups), out_sha...  75 us
    all_to_all x1, waiting for transfers between devices, on_device(): lax.all_to_all(feed_cut, 'seq', split_axis=0, concat_axis=0, tiled=True)  35.3 us
    pallas_call x2, Pallas kernels, update(): pl.pallas_call(functools.partial(update_kernel, first_step, steps, tile_a...  23.9 us
    pallas_call x1, Pallas kernels, attend_back(): pl.pallas_call(attend_back_kernel, grid_spec=pltpu.PrefetchScalarGridSpec...  16 us
    pallas_call x1, Pallas kernels, norm_and_project(): pl.pallas_call(qkv_kernel, grid=(tokens // ROWS,), in_specs=[rows(D), who...  15.6 us
  transfers between devices with their start and end apart: 6, of which 3 were waited for; matrix products, arithmetic and copies ran while one was open for 3% of the time, Pallas kernels for 38%

profile of v5, /device:TPU:9, one launch (start us, length us, event | category | flops | bytes accessed | tf_op | source)
XLA Modules:
  0.0 575.8 jit_solution(11255238648430621321)
XLA Ops:
  7.2 0.0 copy-start.8
  7.2 0.0 copy-start.9
  7.2 0.0 all-gather.3.cloned.1.call-start
  7.2 5.1 lay_out.1
  12.3 0.0 copy-start.7
  12.3 0.0 all-gather.3.cloned.1.call-update
  12.3 0.0 all-gather.5.cloned.1.call-start
  12.4 0.7 all-gather.5.cloned.1.call-update
  13.1 0.9 slice.38
  14.0 0.1 copy.28
  14.1 0.6 bitcast_convert_fusion.refs_1_
  14.7 84.3 %ring_gather_1.1 = (bf16[16,128,2048]{2,1,0:T(8,128)(2,1)}, bf16[2,16,64,384]{3,2,1,0:T(8,128)(2,1)}, f32[2,16,8,128]{3,2,1,0:T(8,128)}) custom-call(bf16[128,2048]{1,0:T(8,128)(2,1)} %x_ref.3, bf16[16,64,384]{2,1,0:T(8,128)(2,1)} %get-tuple-element.47.refs_0_, f32[1,8,128]{2,1,0:T(8,128)} %bitcast_convert_fusion.refs_1_), custom_call_target="tpu_custom_call" | custom-call | bytes 150000000 | tf_op jit(solution)/shard_map/ring_gather_1/pallas_call | solution.py:343
  99.0 0.0 all-gather.3.cloned.1.call-done.plane_ref
  99.1 13.7 %all-to-all-start = ((bf16[16,64,1152]{2,1,0:T(8,128)(2,1)}), bf16[16,64,1152]{2,1,0:T(8,128)(2,1)S(1)}, u32[]{:S(2)}, u32[]{:S(2)}) async-start(bf16[16,64,1152]{2,1,0:T(8,128)(2,1)} %get-tuple-element.58), calls=%async_computation | async-start | bytes 4718592 | tf_op jit(solution)/shard_map/all_to_all | solution.py:1562
  112.8 0.0 copy-done.8
  112.8 0.2 reduce-window.4
  113.0 0.0 copy-done.9
  113.0 0.9 slice_bitcast_fusion
  113.9 3.2 constant_dynamic-slice_fusion
  117.1 0.3 collective-permute-start
  117.4 0.0 copy-done.7
  117.4 0.2 select_reduce_fusion.1
  117.6 0.1 slice.24
  117.7 0.1 slice.25
  117.8 0.7 reshape.116.vec_ref
  118.6 0.6 and_select_fusion
  119.1 3.7 fusion
  122.9 1.9 pad_maximum_fusion
  124.8 15.6 %norm_and_project.1 = (bf16[2048,2048]{1,0:T(8,128)(2,1)}, bf16[2048,128]{1,0:T(8,128)(2,1)}, bf16[2048,128]{1,0:T(8,128)(2,1)}, bf16[2048,128]{1,0:T(8,128)(2,1...) custom-call(bf16[2048,2048]{1,0:T(8,128)(2,1)} %bitcast.30, bf16[2048,384]{1,0:T(8,128)(2,1)} %bitcast.32, ...), custom_call_target="tpu_custom_call" | custom-call | flops 3221225472 | bytes 24000000 | tf_op jit(solution)/shard_map/norm_and_project/pallas_call | solution.py:1163
  140.4 1.3 broadcast_in_dim.72.first_ref
  141.7 1.3 broadcast_in_dim.74.last_ref
  143.1 11.9 %attend.1 = (bf16[2048,128]{1,0:T(8,128)(2,1)}, f32[8,128,256]{2,1,0:T(8,128)}, f32[8,1,256]{2,1,0:T(1,128)}) custom-call(s32[8]{0:T(128)} %get-tuple-element.100.low_ref, s32[8]{0:T(128)} %get-tuple-element.99.high_ref, bf16[2048,128]{1,0:T(8,128)(2,1)} %get-tuple-element.54.q_ref, bf16[4,512,128]{2,1,0:T(8,128)(2,1)} %bitcast.43, ...), custom_call_target="tpu_custom_call" | custom-call | flops 1073741824 | bytes 4000000 | tf_op jit(solution)/shard_map/attend/pallas_call | solution.py:1224
  154.9 9.3 %collective-permute-done.refs_0_ = bf16[512,2048]{1,0:T(8,128)(2,1)} collective-permute-done((bf16[512,2048]{1,0:T(8,128)(2,1)}, bf16[512,2048]{1,0:T(8,128)(2,1)}, u32[]{:S(2)}, u32[]{:S(2)}) %collective-permute-start) | collective-permute-done | bytes 2097184 | tf_op jit(solution)/shard_map/ppermute | solution.py:1561
  164.2 35.3 %all-to-all-done = bf16[16,64,1152]{2,1,0:T(8,128)(2,1)S(1)} async-done(((bf16[16,64,1152]{2,1,0:T(8,128)(2,1)}), bf16[16,64,1152]{2,1,0:T(8,128)(2,1)S(1)}, u32[]{:S(2)}, u32[]{:S(2)}) %all-to-all-start) | async-done | bytes 2359328 | tf_op jit(solution)/shard_map/all_to_all | solution.py:1562
  199.6 0.0 copy-start.2
  199.6 1.4 copy-done.2
  201.0 75.0 %gather_residual.1 = (bf16[16,2048,128]{2,1,0:T(8,128)(2,1)}, bf16[1,1024,1152]{2,1,0:T(8,128)(2,1)}, bf16[2048,2048]{1,0:T(8,128)(2,1)}, bf16[2048,2048]{1,0:T(8,128)(2,1)}, f32[128,2048]{1,0:T(8,128)}) custom-call(bf16[2048,128]{1,0:T(8,128)(2,1)} %get-tuple-element.57.x_ref, bf16[1024,1152]{1,0:T(8,128)(2,1)} %bitcast.34, bf16[2048,2048]{1,0:T(8,128)(2,1)} %bitcast.31, ...), custom_call_target="tpu_custom_call" | custom-call | flops 17179869184 | bytes 200000000 | tf_op jit(solution)/shard_map/gather_residual/pallas_call | solution.py:508
  276.0 0.0 all-gather.5.cloned.1.call-done.cot_ref
  276.0 119.7 %feed_forward.1 = (f32[128,2048]{1,0:T(8,128)}, bf16[4,256,1152]{2,1,0:T(8,128)(2,1)}, f32[128,2048]{1,0:T(8,128)}, f32[2,2048]{1,0:T(2,128)}, bf16[16,128,128]{...) custom-call(bf16[2048,2048]{1,0:T(8,128)(2,1)} %get-tuple-element.61.b_ref, ...), custom_call_target="tpu_custom_call" | custom-call | flops 28991029248 | bytes 250000000 | tf_op jit(solution)/shard_map/feed_forward/pallas_call | solution.py:942
  395.7 5.1 all-to-all-start.1
  400.8 16.0 %attend_back.1.dp_ref = bf16[2048,384]{1,0:T(8,128)(2,1)} custom-call(s32[8]{0:T(128)} %get-tuple-element.100.low_ref, s32[8]{0:T(128)} %get-tuple-element.99.high_ref, bf16[2048,128]{1,0:T(8,128)(2,1)} %get-tuple-element.54.q_ref, bf16[2048,128]{1,0:T(8,128)(2,1)} %bitcast.46, f32[8,128,256]{2,1,0:T(8,128)} %get-tuple-element.66.full_ref, ...), custom_call_target="tpu_custom_call" | custom-call | flops 2684354560 | bytes 6000000 | tf_op jit(solution)/shard_map/attend_back/pallas_call | solution.py:1317
  416.8 0.0 all-to-all-done.1
  416.8 0.0 copy-start.3
  416.8 0.8 copy-done.3
  417.6 111.3 %project_back.1 = (bf16[128,2048]{1,0:T(8,128)(2,1)}, bf16[4,256,512]{2,1,0:T(8,128)(2,1)}, bf16[16,64,1152]{2,1,0:T(8,128)(2,1)}, f32[8,128]{1,0:T(8,128)}) custom-call(bf16[2048,384]{1,0:T(8,128)(2,1)} %attend_back.1.dp_ref, bf16[2048,384]{1,0:T(8,128)(2,1)} %bitcast.33, bf16[2048,2048]{1,0:T(8,128)(2,1)} %get-tuple-element.70.a_ref, ...), custom_call_target="tpu_custom_call" | custom-call | flops 6442450944 | bytes 200000000 | tf_op jit(solution)/shard_map/project_back/pallas_call | solution.py:1108
  528.9 0.0 copy-start.6
  528.9 5.2 all-to-all-start.2
  534.2 0.1 slice_reduce_fusion.1
  534.3 0.1 add.48
  534.3 0.1 mul.56
  534.4 0.0 copy-done
  534.4 0.1 reduce_sum.67
  534.6 0.3 multiply_reduce_fusion
  534.8 0.0 copy-done.4
  534.8 1.1 add_convert_fusion
  535.9 0.0 copy-done.6
  535.9 0.1 copy.27
  536.1 0.6 pad.10.refs_1_
  536.7 15.9 %update_4.1 = (f32[64,24579]{1,0:T(8,128)}, f32[64,24579]{1,0:T(8,128)}, f32[64,24579]{1,0:T(8,128)}, f32[64,24579]{1,0:T(8,128)}) custom-call(bf16[16,64,1152]{2,1,0:T(8,128)(2,1)} %get-tuple-element.78.refs_0_, f32[64,128]{1,0:T(8,128)} %pad.10.refs_1_, f32[64,24579]{1,0:T(8,128)} %refs_1_.1, f32[64,24579]{1,0:T(8,128)} %refs_2_.3, f32[64,24579]{1,0:T(8,128)} %refs_3_.3, ...), custom_call_target="tpu_custom_call" | custom-call | bytes 42467328 | tf_op jit(solution)/shard_map/update_4/pallas_call | solution.py:1495
  552.6 6.3 %all-to-all-done.2.refs_0_ = bf16[16,64,512]{2,1,0:T(8,128)(2,1)S(1)} async-done(((bf16[16,64,512]{2,1,0:T(8,128)(2,1)}), bf16[16,64,512]{2,1,0:T(8,128)(2,1)S(1)}, u32[]{:S(2)}, u32[]{:S(2)}) %all-to-all-start.2) | async-done | bytes 1048608 | tf_op jit(solution)/shard_map/all_to_all | solution.py:1538
  558.9 1.0 copy-done.1
  559.9 8.0 %update_0.1 = (f32[64,24579]{1,0:T(8,128)}, f32[64,24579]{1,0:T(8,128)}, f32[64,24579]{1,0:T(8,128)}, f32[64,24579]{1,0:T(8,128)}) custom-call(bf16[16,64,512]{2,1,0:T(8,128)(2,1)} %copy-done.1, f32[64,24579]{1,0:T(8,128)} %refs_1_.1, f32[64,24579]{1,0:T(8,128)} %refs_2_.3, ...), custom_call_target="tpu_custom_call", output_to_operand_aliasing={{0}: (5, {}), {1}: (6, {}), {2}: (7, {}), {3}: (8, {})} | custom-call | bytes 18874368 | tf_op jit(solution)/shard_map/update_0/pallas_call | solution.py:1495
  567.9 0.0 copy-done.5
  567.9 0.8 copy.34
  (16 shorter events, 0.1 us)
Async XLA Ops:
  7.2 105.6 %copy-start.8 = (s32[1,4]{1,0:T(1,128)S(1)}, s32[1,4]{1,0:T(1,128)}, u32[]{:S(2)}) copy-start(s32[1,4]{1,0:T(1,128)} %param.15) | copy-start | bytes 52
  7.2 105.8 %copy-start.9 = (s32[1,4]{1,0:T(1,128)S(1)}, s32[1,4]{1,0:T(1,128)}, u32[]{:S(2)}) copy-start(s32[1,4]{1,0:T(1,128)} %param.17) | copy-start | bytes 52
  7.2 91.9 %all-gather.3.cloned.1.call-start = ((), (), s32[]{:S(2)}) async-start(), calls=%async_computation.3 | async-start | bytes 4456448 | tf_op jit(solution)/shard_map/all_gather | solution.py:1554
  12.3 105.1 %copy-start.7 = (s32[1,4]{1,0:T(1,128)S(1)}, s32[1,4]{1,0:T(1,128)}, u32[]{:S(2)}) copy-start(s32[1,4]{1,0:T(1,128)} %param.16) | copy-start | bytes 52
  12.3 263.7 %all-gather.5.cloned.1.call-start = ((), (), s32[]{:S(2)}) async-start(), calls=%async_computation.4 | async-start | bytes 8912896 | tf_op jit(solution)/shard_map/all_gather | solution.py:1564
  99.1 100.5 %all-to-all-start = ((bf16[16,64,1152]{2,1,0:T(8,128)(2,1)}), bf16[16,64,1152]{2,1,0:T(8,128)(2,1)S(1)}, u32[]{:S(2)}, u32[]{:S(2)}) async-start(bf16[16,64,1152]{2,1,0:T(8,128)(2,1)} %get-tuple-element.58), calls=%async_computation | async-start | bytes 4718592 | tf_op jit(solution)/shard_map/all_to_all | solution.py:1562
  117.1 47.2 %collective-permute-start = (bf16[512,2048]{1,0:T(8,128)(2,1)}, bf16[512,2048]{1,0:T(8,128)(2,1)}, u32[]{:S(2)}, u32[]{:S(2)}) collective-permute-start(bf16[512,2048]{1,0:T(8,128)(2,1)} %constant_dynamic-slice_fusion), channel_id=1, source_target_pairs={{0,16},{16,0},{1,17},{17,1},{2,18},{18,2},{3,19},{19,3},{4,20},{20... | collective-permute-start | bytes 6291464 | tf_op jit(solution)/shard_map/ppermute | solution.py:1561
  199.6 1.4 copy-start.2
  395.7 21.1 %all-to-all-start.1 = ((bf16[16,128,128]{2,1,0:T(8,128)(2,1)}), bf16[16,128,128]{2,1,0:T(8,128)(2,1)S(1)}, u32[]{:S(2)}, u32[]{:S(2)}) async-start(bf16[16,128,128]{2,1,0:T(8,128)(2,1)} %get-tuple-element.72), calls=%async_computation.1 | async-start | bytes 1048576 | tf_op jit(solution)/shard_map/all_to_all | solution.py:1576
  416.8 0.8 copy-start.3
  417.6 116.8 %copy-start = (f32[128,2048]{1,0:T(8,128)S(1)}, f32[128,2048]{1,0:T(8,128)}, u32[]{:S(2)}) copy-start(f32[128,2048]{1,0:T(8,128)} %get-tuple-element.60.res_ref) | copy-start | bytes 3145732
  417.6 117.2 %copy-start.4 = (f32[128,2048]{1,0:T(8,128)S(1)}, f32[128,2048]{1,0:T(8,128)}, u32[]{:S(2)}) copy-start(f32[128,2048]{1,0:T(8,128)} %get-tuple-element.64) | copy-start | bytes 3145732
  528.9 7.0 %copy-start.6 = (f32[8,128]{1,0:T(8,128)S(1)}, f32[8,128]{1,0:T(8,128)}, u32[]{:S(2)}) copy-start(f32[8,128]{1,0:T(8,128)} %get-tuple-element.79) | copy-start | bytes 12292
  528.9 29.9 %all-to-all-start.2 = ((bf16[16,64,512]{2,1,0:T(8,128)(2,1)}), bf16[16,64,512]{2,1,0:T(8,128)(2,1)S(1)}, u32[]{:S(2)}, u32[]{:S(2)}) async-start(bf16[16,64,512]{2,1,0:T(8,128)(2,1)} %bitcast.38), calls=%async_computation.2 | async-start | bytes 2097152 | tf_op jit(solution)/shard_map/all_to_all | solution.py:1538
  558.9 1.0 copy-start.1
  559.9 8.0 %copy-start.5 = (bf16[128,2048]{1,0:T(8,128)(2,1)S(1)}, bf16[128,2048]{1,0:T(8,128)(2,1)}, u32[]{:S(2)}) copy-start(bf16[128,2048]{1,0:T(8,128)(2,1)} %get-tuple-element.110) | copy-start | bytes 1572868
Sparse Core Ops, SparseCore 0:
  12.5 72.2 all-gather.2
  86.9 112.3 all-gather.4

commit v6 on v5

--- a/solution.py
+++ b/solution.py
@@ -181,7 +181,47 @@
         self.mine.wait()
 
 
-def pass_round(ring, count, lag, x_ref, o_ref, sems, columns, work):
+class Lap:
+    def __init__(self, ring, x_ref, o_ref, sems):
+        self.ring, self.x_ref, self.o_ref = ring, x_ref, o_ref
+        self.ring_s, self.ring_r, self.sib_s, self.sib_r, own_sem = sems
+        self.piece = x_ref.shape[0] // SUBS
+        self.own = pltpu.make_async_copy(x_ref, o_ref.at[ring.me], own_sem)
+        self.sends = []
+
+    def step(self, step):
+        ring = self.ring
+        if step == 0:
+            self.own.start()
+        for sub in range(SUBS):
+            rows = pl.ds(sub * self.piece, self.piece)
+            dst = self.o_ref.at[ring.at(-step)].at[rows]
+            src = self.x_ref.at[rows] if step == 0 else dst
+            if step > 0:
+                before = self.ring_s.at[step - 1, sub], self.ring_r.at[step - 1, sub]
+                ring.copy(dst, dst, *before, ring.at(1)).wait_recv()
+            if step < ring.pairs - 1:
+                now = self.ring_s.at[step, sub], self.ring_r.at[step, sub]
+                self.sends.append(ring.copy(src, dst, *now, ring.at(1)))
+                self.sends[-1].start()
+            across = self.sib_s.at[step, sub], self.sib_r.at[step, sub]
+            self.sends.append(ring.copy(src, dst, *across, ring.sibling))
+            self.sends[-1].start()
+
+    def finish(self):
+        ring = self.ring
+        for step in range(ring.pairs):
+            other = ring.at(step, 1 - ring.core)
+            for sub in range(SUBS):
+                dst = self.o_ref.at[other].at[pl.ds(sub * self.piece, self.piece)]
+                across = self.sib_s.at[step, sub], self.sib_r.at[step, sub]
+                ring.copy(dst, dst, *across, ring.sibling).wait_recv()
+        for go in self.sends:
+            go.wait_send()
+        self.own.wait()
+
+
+def pass_round(ring, count, lag, x_ref, o_ref, sems, columns, work, lap):
     ring_s, ring_r, sib_s, sib_r, own_sem = sems
     piece = x_ref.shape[0] // SUBS
     own = pltpu.make_async_copy(x_ref, o_ref.at[ring.me], own_sem)
@@ -227,6 +267,7 @@
                 for column in columns:
                     column.pass_on(passed)
             ahead = max(ahead, upto)
+        lap.step(step)
         if step >= lag:
             complete(step - lag)
     for step in range(max(0, ring.pairs - lag), ring.pairs):
@@ -373,11 +414,12 @@
     ]
 
 
-def residual_kernel(count, groups, x_ref, feed_ref, states_ref, vec_ref, plane_ref, *refs):
+def residual_kernel(count, groups, x_ref, feed_ref, states_ref, vec_ref, cot_ref, plane_ref, *refs):
     far_refs, refs = refs[: groups - 1], refs[groups - 1 :]
-    heads_ref, feed_far_ref, b_ref, w_ref, own_ref, heads, w_out, total, states, low = refs[:10]
-    w_sem, load_sem, store_sem, heads_sem, *sems = refs[10:]
+    heads_ref, feed_far_ref, b_ref, w_ref, cot_all_ref, own_ref = refs[:6]
+    heads, w_out, total, states, low, w_sem, load_sem, store_sem, heads_sem, *sems = refs[6:]
     ring = Ring(count)
+    lap = Lap(ring, cot_ref, cot_all_ref, sems[9:14])
     tokens, own = total.shape[0], own_ref.shape[0]
     blocks = tokens // ROWS
     part = D // groups
@@ -487,7 +529,7 @@
             add(list(waiting), turn == 1, turn == turns - 1)
             waiting.clear()
 
-    sends = pass_round(ring, count, 2, x_ref, heads, sems[:5], [], work)
+    sends = pass_round(ring, count, 2, x_ref, heads, sems[:5], [], work, lap)
 
     own_ref[...] = total[pl.ds(pl.multiple_of(ring.me * own, own), own), :]
     for block in (blocks - 2, blocks - 1):
@@ -499,9 +541,10 @@
     for shift in range(1, groups):
         onward(shift).wait()
     keep.wait()
-
-
-def gather_residual(attended, feed_own, states, vectors, w_plane, w_far, own, count, ident):
+    lap.finish()
+
+
+def gather_residual(attended, feed_own, states, vectors, cot, w_plane, w_far, own, count, ident):
     tokens = attended.shape[0]
     pairs, groups = count // 2, lax.axis_size("batch")
     inside, anywhere = pl.BlockSpec(memory_space=pltpu.VMEM), pl.BlockSpec(memory_space=pl.ANY)
@@ -512,10 +555,11 @@
             jax.ShapeDtypeStruct((groups - 1,) + feed_own.shape, BF),
             jax.ShapeDtypeStruct((tokens, D), BF),
             jax.ShapeDtypeStruct((D, D), BF),
+            jax.ShapeDtypeStruct((count,) + cot.shape, BF),
             jax.ShapeDtypeStruct((own, D), F32),
         ],
-        in_specs=[anywhere] * 3 + [inside] + [anywhere] * (1 + len(w_far)),
-        out_specs=[anywhere] * 4 + [inside],
+        in_specs=[anywhere] * 3 + [inside] + [anywhere] * (2 + len(w_far)),
+        out_specs=[anywhere] * 5 + [inside],
         scratch_shapes=[
             pltpu.VMEM((count, tokens, HD), BF),
             pltpu.VMEM((D, D), BF),
@@ -528,13 +572,14 @@
             pltpu.SemaphoreType.DMA((pairs, 2)),
         ]
         + ring_sems(pairs)
-        + [pltpu.SemaphoreType.DMA((max(1, groups - 1),)) for _ in range(4)],
+        + [pltpu.SemaphoreType.DMA((max(1, groups - 1),)) for _ in range(4)]
+        + ring_sems(pairs),
         compiler_params=vmem(collective_id=ident, has_side_effects=True),
         cost_estimate=pl.CostEstimate(
             flops=2 * tokens * D * D, bytes_accessed=200_000_000, transcendentals=0
         ),
         name="gather_residual",
-    )(attended, feed_own, states, vectors, w_plane, *w_far)
+    )(attended, feed_own, states, vectors, cot, w_plane, *w_far)
 
 
 class RingSum:
@@ -1418,7 +1463,7 @@
     )(master)
 
 
-STEP_COLS = 2048
+STEP_COLS = 4096
 
 
 def tile_of_part(ref, part, at, begin, rows, span):
@@ -1561,15 +1606,15 @@
         w_far.append(lax.ppermute(half_mine, "batch", far))
     feed_own = lax.all_to_all(feed_cut, "seq", split_axis=0, concat_axis=0, tiled=True)
     feed_own = feed_own.reshape(D // groups, 3 * span)
-    cot_all = lax.all_gather(cotangent, "seq", axis=0, tiled=True)
 
     spans, place = chain_spans(lengths[0], prefix[0], padding[0], tokens)
     cosine, sine = rotary_tables(place)
     a_low, query, key, value, key_t, value_t = norm_and_project(states, w_qkv, vectors, cosine, sine)
     attended, full, log = attend(query, key, value_t, spans)
-    heads, feed_far, b_low, w_out, residual = gather_residual(
-        attended, feed_own, states, vectors, w_plane, w_far, own, seq, 2
+    heads, feed_far, b_low, w_out, cot_all, residual = gather_residual(
+        attended, feed_own, states, vectors, cotangent, w_plane, w_far, own, seq, 2
     )
+    cot_all = cot_all.reshape(tokens, D)
     out_sum, grad_feed, dr, vec_sums, do, dr_cut = feed_forward(
         b_low, cot_all, feed_own, feed_far, w_out, residual, cotangent, vectors, seq, groups, 3
     )

time: 580 us -> 574 us (0.990)
  waiting for transfers between devices: 51.7 us -> 18.3 us
  Pallas kernels: 463 us -> 486 us
    all_to_all x1, waiting for transfers between devices: 35.3 us -> 0.01 us  [on_device(): lax.all_to_all(feed_cut, 'seq', split_axis=0, concat_axis=0, tiled=True)]
    pallas_call x1, Pallas kernels: 75 us -> 107 us  [gather_residual(): pl.pallas_call(functools.partial(residual_kernel, count, groups), out_sha...]
  transfers between devices with their start and end apart: 6 -> 5, of which waited for: 3 -> 2; matrix products, arithmetic and copies ran while one was open for 3% -> 3% of each run, Pallas kernels for 38% -> 25%
where the time goes in v6:
time: 574 us; the launch traced here: 568 us
  Pallas kernels  486 us (85%)
  starting transfers between devices  26.6 us (5%)
  waiting for transfers between devices  18.3 us (3%)
  between operations  14.5 us (3%)
  local copies, waits for them, and re-layouts  13.7 us (2%)
  other arithmetic  8.74 us (2%)
    pallas_call x1, Pallas kernels, feed_forward(): pl.pallas_call(functools.partial(feed_kernel, count, groups, span), in_sp...  121 us
    pallas_call x1, Pallas kernels, project_back(): pl.pallas_call(functools.partial(project_kernel, count, groups), in_specs...  107 us
    pallas_call x1, Pallas kernels, gather_residual(): pl.pallas_call(functools.partial(residual_kernel, count, groups), out_sha...  107 us
    pallas_call x1, Pallas kernels, ring_gather(): pl.pallas_call(functools.partial(gather_kernel, count, len(blocks)), out_...  82.8 us
    pallas_call x2, Pallas kernels, update(): pl.pallas_call(functools.partial(update_kernel, first_step, steps, tile_a...  20.4 us
    pallas_call x1, Pallas kernels, attend_back(): pl.pallas_call(attend_back_kernel, grid_spec=pltpu.PrefetchScalarGridSpec...  16 us
    all_to_all x1, starting transfers between devices, on_device(): lax.all_to_all(feed_cut, 'seq', split_axis=0, concat_axis=0, tiled=True)  15.9 us
    pallas_call x1, Pallas kernels, norm_and_project(): pl.pallas_call(qkv_kernel, grid=(tokens // ROWS,), in_specs=[rows(D), who...  15.4 us
  transfers between devices with their start and end apart: 5, of which 2 were waited for; matrix products, arithmetic and copies ran while one was open for 3% of the time, Pallas kernels for 25%

profile of v6, /device:TPU:9, one launch (start us, length us, event | category | flops | bytes accessed | tf_op | source)
XLA Modules:
  0.0 567.9 jit_solution(15100909666952929572)
XLA Ops:
  7.2 0.0 copy-start.8
  7.2 0.0 copy-start.9
  7.2 0.0 all-gather.2.cloned.1.call-start
  7.2 5.1 lay_out.1
  12.3 0.0 all-gather.2.cloned.1.call-update
  12.3 0.9 slice.38
  13.3 0.1 copy.28
  13.4 0.6 bitcast_convert_fusion.refs_1_
  14.0 82.8 %ring_gather_1.1 = (bf16[16,128,2048]{2,1,0:T(8,128)(2,1)}, bf16[2,16,64,384]{3,2,1,0:T(8,128)(2,1)}, f32[2,16,8,128]{3,2,1,0:T(8,128)}) custom-call(bf16[128,2048]{1,0:T(8,128)(2,1)} %x_ref.3, bf16[16,64,384]{2,1,0:T(8,128)(2,1)} %get-tuple-element.48.refs_0_, f32[1,8,128]{2,1,0:T(8,128)} %bitcast_convert_fusion.refs_1_), custom_call_target="tpu_custom_call" | custom-call | bytes 150000000 | tf_op jit(solution)/shard_map/ring_gather_1/pallas_call | solution.py:384
  96.8 0.0 all-gather.2.cloned.1.call-done.plane_ref
  96.8 15.9 %all-to-all-start = ((bf16[16,64,1152]{2,1,0:T(8,128)(2,1)}), bf16[16,64,1152]{2,1,0:T(8,128)(2,1)S(1)}, u32[]{:S(2)}, u32[]{:S(2)}) async-start(bf16[16,64,1152]{2,1,0:T(8,128)(2,1)} %get-tuple-element.59), calls=%async_computation | async-start | bytes 4718592 | tf_op jit(solution)/shard_map/all_to_all | solution.py:1607
  112.7 0.0 copy-done.8
  112.7 0.2 reduce-window.4
  112.9 0.0 copy-done.9
  112.9 0.9 slice_bitcast_fusion
  113.8 3.2 constant_dynamic-slice_fusion
  117.0 0.3 collective-permute-start
  117.3 0.0 copy-done.7
  117.3 0.2 select_reduce_fusion.1
  117.4 0.1 slice.25
  117.5 0.1 slice.24
  117.7 0.7 reshape.119.vec_ref
  118.4 0.6 and_select_fusion
  119.0 3.7 fusion
  122.8 1.9 pad_maximum_fusion
  124.7 15.4 %norm_and_project.1 = (bf16[2048,2048]{1,0:T(8,128)(2,1)}, bf16[2048,128]{1,0:T(8,128)(2,1)}, bf16[2048,128]{1,0:T(8,128)(2,1)}, bf16[2048,128]{1,0:T(8,128)(2,1...) custom-call(bf16[2048,2048]{1,0:T(8,128)(2,1)} %bitcast.31, bf16[2048,384]{1,0:T(8,128)(2,1)} %bitcast.33, ...), custom_call_target="tpu_custom_call" | custom-call | flops 3221225472 | bytes 24000000 | tf_op jit(solution)/shard_map/norm_and_project/pallas_call | solution.py:1208
  140.1 1.3 broadcast_in_dim.72.first_ref
  141.4 1.3 broadcast_in_dim.74.last_ref
  142.7 11.9 %attend.1 = (bf16[2048,128]{1,0:T(8,128)(2,1)}, f32[8,128,256]{2,1,0:T(8,128)}, f32[8,1,256]{2,1,0:T(1,128)}) custom-call(s32[8]{0:T(128)} %get-tuple-element.102.low_ref, s32[8]{0:T(128)} %get-tuple-element.101.high_ref, bf16[2048,128]{1,0:T(8,128)(2,1)} %get-tuple-element.55.q_ref, bf16[4,512,128]{2,1,0:T(8,128)(2,1)} %bitcast.44, ...), custom_call_target="tpu_custom_call" | custom-call | flops 1073741824 | bytes 4000000 | tf_op jit(solution)/shard_map/attend/pallas_call | solution.py:1269
  154.6 9.5 %collective-permute-done.refs_0_ = bf16[512,2048]{1,0:T(8,128)(2,1)} collective-permute-done((bf16[512,2048]{1,0:T(8,128)(2,1)}, bf16[512,2048]{1,0:T(8,128)(2,1)}, u32[]{:S(2)}, u32[]{:S(2)}) %collective-permute-start) | collective-permute-done | bytes 2097184 | tf_op jit(solution)/shard_map/ppermute | solution.py:1606
  164.2 0.0 all-to-all-done
  164.2 0.0 copy-start.2
  164.2 1.4 copy-done.2
  165.6 106.6 %gather_residual.1 = (bf16[16,2048,128]{2,1,0:T(8,128)(2,1)}, bf16[1,1024,1152]{2,1,0:T(8,128)(2,1)}, bf16[2048,2048]{1,0:T(8,128)(2,1)}, bf16[2048,2048]{1,0:T(...) custom-call(bf16[2048,128]{1,0:T(8,128)(2,1)} %get-tuple-element.58.x_ref, bf16[1024,1152]{1,0:T(8,128)(2,1)} %bitcast.35, ...), custom_call_target="tpu_custom_call" | custom-call | flops 17179869184 | bytes 200000000 | tf_op jit(solution)/shard_map/gather_residual/pallas_call | solution.py:551
  272.2 120.8 %feed_forward.1 = (f32[128,2048]{1,0:T(8,128)}, bf16[4,256,1152]{2,1,0:T(8,128)(2,1)}, f32[128,2048]{1,0:T(8,128)}, f32[2,2048]{1,0:T(2,128)}, bf16[16,128,128]{...) custom-call(bf16[2048,2048]{1,0:T(8,128)(2,1)} %get-tuple-element.62.b_ref, bf16[2048,2048]{1,0:T(8,128)(2,1)} %bitcast.47, ...), custom_call_target="tpu_custom_call" | custom-call | flops 28991029248 | bytes 250000000 | tf_op jit(solution)/shard_map/feed_forward/pallas_call | solution.py:987
  392.9 4.9 all-to-all-start.1
  397.8 16.0 %attend_back.1.dp_ref = bf16[2048,384]{1,0:T(8,128)(2,1)} custom-call(s32[8]{0:T(128)} %get-tuple-element.102.low_ref, s32[8]{0:T(128)} %get-tuple-element.101.high_ref, bf16[2048,128]{1,0:T(8,128)(2,1)} %get-tuple-element.55.q_ref, bf16[2048,128]{1,0:T(8,128)(2,1)} %bitcast.48, f32[8,128,256]{2,1,0:T(8,128)} %get-tuple-element.68.full_ref, ...), custom_call_target="tpu_custom_call" | custom-call | flops 2684354560 | bytes 6000000 | tf_op jit(solution)/shard_map/attend_back/pallas_call | solution.py:1362
  413.8 0.0 all-to-all-done.1
  413.8 0.0 copy-start.3
  413.8 0.8 copy-done.3
  414.6 0.0 copy-start
  414.6 0.0 copy-start.4
  414.6 107.4 %project_back.1 = (bf16[128,2048]{1,0:T(8,128)(2,1)}, bf16[4,256,512]{2,1,0:T(8,128)(2,1)}, bf16[16,64,1152]{2,1,0:T(8,128)(2,1)}, f32[8,128]{1,0:T(8,128)}) custom-call(bf16[2048,384]{1,0:T(8,128)(2,1)} %attend_back.1.dp_ref, bf16[2048,384]{1,0:T(8,128)(2,1)} %bitcast.34, bf16[2048,2048]{1,0:T(8,128)(2,1)} %get-tuple-element.72.a_ref, ...), custom_call_target="tpu_custom_call" | custom-call | flops 6442450944 | bytes 200000000 | tf_op jit(solution)/shard_map/project_back/pallas_call | solution.py:1153
  522.0 0.0 copy-start.6
  522.0 5.5 all-to-all-start.2
  527.5 0.1 slice_reduce_fusion.1
  527.6 0.1 mul.56
  527.7 0.1 add.48
  527.7 0.0 copy-done
  527.7 0.1 reduce_sum.67
  527.9 0.3 multiply_reduce_fusion
  528.1 0.0 copy-done.4
  528.2 1.1 add_convert_fusion
  529.3 0.0 copy-done.6
  529.3 0.1 copy.27
  529.4 0.6 pad.10.refs_1_
  530.0 13.5 %update_2.1 = (f32[64,24579]{1,0:T(8,128)}, f32[64,24579]{1,0:T(8,128)}, f32[64,24579]{1,0:T(8,128)}, f32[64,24579]{1,0:T(8,128)}) custom-call(bf16[16,64,1152]{2,1,0:T(8,128)(2,1)} %get-tuple-element.80.refs_0_, f32[64,128]{1,0:T(8,128)} %pad.10.refs_1_, f32[64,24579]{1,0:T(8,128)} %refs_1_.1, f32[64,24579]{1,0:T(8,128)} %refs_2_.3, f32[64,24579]{1,0:T(8,128)} %refs_3_.3, ...), custom_call_target="tpu_custom_call" | custom-call | bytes 47185920 | tf_op jit(solution)/shard_map/update_2/pallas_call | solution.py:1540
  543.5 8.7 %all-to-all-done.2.refs_0_ = bf16[16,64,512]{2,1,0:T(8,128)(2,1)S(1)} async-done(((bf16[16,64,512]{2,1,0:T(8,128)(2,1)}), bf16[16,64,512]{2,1,0:T(8,128)(2,1)S(1)}, u32[]{:S(2)}, u32[]{:S(2)}) %all-to-all-start.2) | async-done | bytes 1048608 | tf_op jit(solution)/shard_map/all_to_all | solution.py:1583
  552.2 0.0 copy-start.1
  552.2 1.0 copy-done.1
  553.2 0.0 copy-start.5
  553.2 6.8 %update_0.1 = (f32[64,24579]{1,0:T(8,128)}, f32[64,24579]{1,0:T(8,128)}, f32[64,24579]{1,0:T(8,128)}, f32[64,24579]{1,0:T(8,128)}) custom-call(bf16[16,64,512]{2,1,0:T(8,128)(2,1)} %copy-done.1, f32[64,24579]{1,0:T(8,128)} %refs_1_.1, f32[64,24579]{1,0:T(8,128)} %refs_2_.3, ...), custom_call_target="tpu_custom_call", output_to_operand_aliasing={{0}: (5, {}), {1}: (6, {}), {2}: (7, {}), {3}: (8, {})} | custom-call | bytes 18874368 | tf_op jit(solution)/shard_map/update_0/pallas_call | solution.py:1540
  560.0 0.0 copy-done.5
  560.0 0.8 copy.34
  (13 shorter events, 0.1 us)
Async XLA Ops:
  7.2 105.6 %copy-start.8 = (s32[1,4]{1,0:T(1,128)S(1)}, s32[1,4]{1,0:T(1,128)}, u32[]{:S(2)}) copy-start(s32[1,4]{1,0:T(1,128)} %param.15) | copy-start | bytes 52
  7.2 105.7 %copy-start.9 = (s32[1,4]{1,0:T(1,128)S(1)}, s32[1,4]{1,0:T(1,128)}, u32[]{:S(2)}) copy-start(s32[1,4]{1,0:T(1,128)} %param.17) | copy-start | bytes 52
  7.2 89.6 %all-gather.2.cloned.1.call-start = ((), (), s32[]{:S(2)}) async-start(), calls=%async_computation.3 | async-start | bytes 4456448 | tf_op jit(solution)/shard_map/all_gather | solution.py:1599
  12.3 105.0 %copy-start.7 = (s32[1,4]{1,0:T(1,128)S(1)}, s32[1,4]{1,0:T(1,128)}, u32[]{:S(2)}) copy-start(s32[1,4]{1,0:T(1,128)} %param.16) | copy-start | bytes 52
  96.8 67.4 %all-to-all-start = ((bf16[16,64,1152]{2,1,0:T(8,128)(2,1)}), bf16[16,64,1152]{2,1,0:T(8,128)(2,1)S(1)}, u32[]{:S(2)}, u32[]{:S(2)}) async-start(bf16[16,64,1152]{2,1,0:T(8,128)(2,1)} %get-tuple-element.59), calls=%async_computation | async-start | bytes 4718592 | tf_op jit(solution)/shard_map/all_to_all | solution.py:1607
  117.0 47.2 %collective-permute-start = (bf16[512,2048]{1,0:T(8,128)(2,1)}, bf16[512,2048]{1,0:T(8,128)(2,1)}, u32[]{:S(2)}, u32[]{:S(2)}) collective-permute-start(bf16[512,2048]{1,0:T(8,128)(2,1)} %constant_dynamic-slice_fusion), channel_id=1, source_target_pairs={{0,16},{16,0},{1,17},{17,1},{2,18},{18,2},{3,19},{19,3},{4,20},{20... | collective-permute-start | bytes 6291464 | tf_op jit(solution)/shard_map/ppermute | solution.py:1606
  164.2 1.4 copy-start.2
  392.9 20.9 %all-to-all-start.1 = ((bf16[16,128,128]{2,1,0:T(8,128)(2,1)}), bf16[16,128,128]{2,1,0:T(8,128)(2,1)S(1)}, u32[]{:S(2)}, u32[]{:S(2)}) async-start(bf16[16,128,128]{2,1,0:T(8,128)(2,1)} %get-tuple-element.74), calls=%async_computation.1 | async-start | bytes 1048576 | tf_op jit(solution)/shard_map/all_to_all | solution.py:1621
  413.8 0.8 copy-start.3
  414.6 113.1 %copy-start = (f32[128,2048]{1,0:T(8,128)S(1)}, f32[128,2048]{1,0:T(8,128)}, u32[]{:S(2)}) copy-start(f32[128,2048]{1,0:T(8,128)} %get-tuple-element.61.res_ref) | copy-start | bytes 3145732
  414.6 113.5 %copy-start.4 = (f32[128,2048]{1,0:T(8,128)S(1)}, f32[128,2048]{1,0:T(8,128)}, u32[]{:S(2)}) copy-start(f32[128,2048]{1,0:T(8,128)} %get-tuple-element.66) | copy-start | bytes 3145732
  522.0 7.3 %copy-start.6 = (f32[8,128]{1,0:T(8,128)S(1)}, f32[8,128]{1,0:T(8,128)}, u32[]{:S(2)}) copy-start(f32[8,128]{1,0:T(8,128)} %get-tuple-element.81) | copy-start | bytes 12292
  522.0 30.2 %all-to-all-start.2 = ((bf16[16,64,512]{2,1,0:T(8,128)(2,1)}), bf16[16,64,512]{2,1,0:T(8,128)(2,1)S(1)}, u32[]{:S(2)}, u32[]{:S(2)}) async-start(bf16[16,64,512]{2,1,0:T(8,128)(2,1)} %bitcast.39), calls=%async_computation.2 | async-start | bytes 2097152 | tf_op jit(solution)/shard_map/all_to_all | solution.py:1583
  552.2 1.0 copy-start.1
  553.2 6.8 %copy-start.5 = (bf16[128,2048]{1,0:T(8,128)(2,1)S(1)}, bf16[128,2048]{1,0:T(8,128)(2,1)}, u32[]{:S(2)}) copy-start(bf16[128,2048]{1,0:T(8,128)(2,1)} %get-tuple-element.112) | copy-start | bytes 1572868
Sparse Core Ops, SparseCore 0:
  12.5 71.6 all-gather.1

commit v7 on v6

--- a/solution.py
+++ b/solution.py
@@ -267,11 +267,13 @@
                 for column in columns:
                     column.pass_on(passed)
             ahead = max(ahead, upto)
-        lap.step(step)
+        if step < ring.pairs - 1:
+            lap.step(step)
         if step >= lag:
             complete(step - lag)
     for step in range(max(0, ring.pairs - lag), ring.pairs):
         complete(step)
+    lap.step(ring.pairs - 1)
     return sends
 
 

time: 574 us -> 574 us (level)
  transfers between devices with their start and end apart: 5 -> 5, of which waited for: 2 -> 2; matrix products, arithmetic and copies ran while one was open for 3% -> 3% of each run, Pallas kernels for 25% -> 26%
where the time goes in v7:
time: 574 us; the launch traced here: 570 us
  Pallas kernels  490 us (85%)
  starting transfers between devices  27.3 us (5%)
  waiting for transfers between devices  15.4 us (3%)
  between operations  14.5 us (3%)
  local copies, waits for them, and re-layouts  13.7 us (2%)
  other arithmetic  8.74 us (2%)
    pallas_call x1, Pallas kernels, feed_forward(): pl.pallas_call(functools.partial(feed_kernel, count, groups, span), in_sp...  119 us
    pallas_call x1, Pallas kernels, project_back(): pl.pallas_call(functools.partial(project_kernel, count, groups), in_specs...  107 us
    pallas_call x1, Pallas kernels, gather_residual(): pl.pallas_call(functools.partial(residual_kernel, count, groups), out_sha...  106 us
    pallas_call x1, Pallas kernels, ring_gather(): pl.pallas_call(functools.partial(gather_kernel, count, len(blocks)), out_...  82.8 us
    pallas_call x2, Pallas kernels, update(): pl.pallas_call(functools.partial(update_kernel, first_step, steps, tile_a...  20.4 us
    pallas_call x1, Pallas kernels, attend_back(): pl.pallas_call(attend_back_kernel, grid_spec=pltpu.PrefetchScalarGridSpec...  19.4 us
    all_to_all x1, starting transfers between devices, on_device(): lax.all_to_all(feed_cut, 'seq', split_axis=0, concat_axis=0, tiled=True)  15.9 us
    pallas_call x1, Pallas kernels, norm_and_project(): pl.pallas_call(qkv_kernel, grid=(tokens // ROWS,), in_specs=[rows(D), who...  15.4 us
  transfers between devices with their start and end apart: 5, of which 2 were waited for; matrix products, arithmetic and copies ran while one was open for 3% of the time, Pallas kernels for 26%

profile of v7, /device:TPU:9, one launch (start us, length us, event | category | flops | bytes accessed | tf_op | source)
XLA Modules:
  0.0 569.7 jit_solution(82197311821032158)
XLA Ops:
  7.2 0.0 copy-start.8
  7.2 0.0 copy-start.9
  7.2 0.0 all-gather.2.cloned.1.call-start
  7.2 5.1 lay_out.1
  12.3 0.0 copy-start.7
  12.3 0.0 all-gather.2.cloned.1.call-update
  12.3 0.9 slice.38
  13.3 0.1 copy.28
  13.4 0.6 bitcast_convert_fusion.refs_1_
  14.0 82.8 %ring_gather_1.1 = (bf16[16,128,2048]{2,1,0:T(8,128)(2,1)}, bf16[2,16,64,384]{3,2,1,0:T(8,128)(2,1)}, f32[2,16,8,128]{3,2,1,0:T(8,128)}) custom-call(bf16[128,2048]{1,0:T(8,128)(2,1)} %x_ref.3, bf16[16,64,384]{2,1,0:T(8,128)(2,1)} %get-tuple-element.48.refs_0_, f32[1,8,128]{2,1,0:T(8,128)} %bitcast_convert_fusion.refs_1_), custom_call_target="tpu_custom_call" | custom-call | bytes 150000000 | tf_op jit(solution)/shard_map/ring_gather_1/pallas_call | solution.py:386
  96.8 0.0 all-gather.2.cloned.1.call-done.plane_ref
  96.8 15.9 %all-to-all-start = ((bf16[16,64,1152]{2,1,0:T(8,128)(2,1)}), bf16[16,64,1152]{2,1,0:T(8,128)(2,1)S(1)}, u32[]{:S(2)}, u32[]{:S(2)}) async-start(bf16[16,64,1152]{2,1,0:T(8,128)(2,1)} %get-tuple-element.59), calls=%async_computation | async-start | bytes 4718592 | tf_op jit(solution)/shard_map/all_to_all | solution.py:1609
  112.7 0.0 copy-done.8
  112.7 0.2 reduce-window.4
  112.9 0.0 copy-done.9
  112.9 0.9 slice_bitcast_fusion
  113.8 3.2 constant_dynamic-slice_fusion
  117.0 0.3 collective-permute-start
  117.3 0.0 copy-done.7
  117.3 0.2 select_reduce_fusion.1
  117.4 0.1 slice.25
  117.5 0.1 slice.24
  117.7 0.7 reshape.119.vec_ref
  118.4 0.6 and_select_fusion
  119.0 3.7 fusion
  122.8 1.9 pad_maximum_fusion
  124.7 15.4 %norm_and_project.1 = (bf16[2048,2048]{1,0:T(8,128)(2,1)}, bf16[2048,128]{1,0:T(8,128)(2,1)}, bf16[2048,128]{1,0:T(8,128)(2,1)}, bf16[2048,128]{1,0:T(8,128)(2,1...) custom-call(bf16[2048,2048]{1,0:T(8,128)(2,1)} %bitcast.31, bf16[2048,384]{1,0:T(8,128)(2,1)} %bitcast.33, ...), custom_call_target="tpu_custom_call" | custom-call | flops 3221225472 | bytes 24000000 | tf_op jit(solution)/shard_map/norm_and_project/pallas_call | solution.py:1210
  140.1 1.3 broadcast_in_dim.72.first_ref
  141.4 1.3 broadcast_in_dim.74.last_ref
  142.7 14.8 %attend.1 = (bf16[2048,128]{1,0:T(8,128)(2,1)}, f32[8,128,256]{2,1,0:T(8,128)}, f32[8,1,256]{2,1,0:T(1,128)}) custom-call(s32[8]{0:T(128)} %get-tuple-element.102.low_ref, s32[8]{0:T(128)} %get-tuple-element.101.high_ref, bf16[2048,128]{1,0:T(8,128)(2,1)} %get-tuple-element.55.q_ref, bf16[4,512,128]{2,1,0:T(8,128)(2,1)} %bitcast.44, ...), custom_call_target="tpu_custom_call" | custom-call | flops 1073741824 | bytes 4000000 | tf_op jit(solution)/shard_map/attend/pallas_call | solution.py:1271
  157.5 6.6 %collective-permute-done.refs_0_ = bf16[512,2048]{1,0:T(8,128)(2,1)} collective-permute-done((bf16[512,2048]{1,0:T(8,128)(2,1)}, bf16[512,2048]{1,0:T(8,128)(2,1)}, u32[]{:S(2)}, u32[]{:S(2)}) %collective-permute-start) | collective-permute-done | bytes 2097184 | tf_op jit(solution)/shard_map/ppermute | solution.py:1608
  164.2 0.0 all-to-all-done
  164.2 0.0 copy-start.2
  164.2 1.4 copy-done.2
  165.6 106.0 %gather_residual.1 = (bf16[16,2048,128]{2,1,0:T(8,128)(2,1)}, bf16[1,1024,1152]{2,1,0:T(8,128)(2,1)}, bf16[2048,2048]{1,0:T(8,128)(2,1)}, bf16[2048,2048]{1,0:T(...) custom-call(bf16[2048,128]{1,0:T(8,128)(2,1)} %get-tuple-element.58.x_ref, bf16[1024,1152]{1,0:T(8,128)(2,1)} %bitcast.35, ...), custom_call_target="tpu_custom_call" | custom-call | flops 17179869184 | bytes 200000000 | tf_op jit(solution)/shard_map/gather_residual/pallas_call | solution.py:553
  271.6 118.9 %feed_forward.1 = (f32[128,2048]{1,0:T(8,128)}, bf16[4,256,1152]{2,1,0:T(8,128)(2,1)}, f32[128,2048]{1,0:T(8,128)}, f32[2,2048]{1,0:T(2,128)}, bf16[16,128,128]{...) custom-call(bf16[2048,2048]{1,0:T(8,128)(2,1)} %get-tuple-element.62.b_ref, bf16[2048,2048]{1,0:T(8,128)(2,1)} %bitcast.47, ...), custom_call_target="tpu_custom_call" | custom-call | flops 28991029248 | bytes 250000000 | tf_op jit(solution)/shard_map/feed_forward/pallas_call | solution.py:989
  390.5 5.7 all-to-all-start.1
  396.1 19.4 %attend_back.1.dp_ref = bf16[2048,384]{1,0:T(8,128)(2,1)} custom-call(s32[8]{0:T(128)} %get-tuple-element.102.low_ref, s32[8]{0:T(128)} %get-tuple-element.101.high_ref, bf16[2048,128]{1,0:T(8,128)(2,1)} %get-tuple-element.55.q_ref, bf16[2048,128]{1,0:T(8,128)(2,1)} %bitcast.48, f32[8,128,256]{2,1,0:T(8,128)} %get-tuple-element.68.full_ref, ...), custom_call_target="tpu_custom_call" | custom-call | flops 2684354560 | bytes 6000000 | tf_op jit(solution)/shard_map/attend_back/pallas_call | solution.py:1364
  415.6 0.0 all-to-all-done.1
  415.6 0.0 copy-start.3
  415.6 0.8 copy-done.3
  416.4 0.0 copy-start
  416.4 0.0 copy-start.4
  416.4 107.4 %project_back.1 = (bf16[128,2048]{1,0:T(8,128)(2,1)}, bf16[4,256,512]{2,1,0:T(8,128)(2,1)}, bf16[16,64,1152]{2,1,0:T(8,128)(2,1)}, f32[8,128]{1,0:T(8,128)}) custom-call(bf16[2048,384]{1,0:T(8,128)(2,1)} %attend_back.1.dp_ref, bf16[2048,384]{1,0:T(8,128)(2,1)} %bitcast.34, bf16[2048,2048]{1,0:T(8,128)(2,1)} %get-tuple-element.72.a_ref, ...), custom_call_target="tpu_custom_call" | custom-call | flops 6442450944 | bytes 200000000 | tf_op jit(solution)/shard_map/project_back/pallas_call | solution.py:1155
  523.8 0.0 copy-start.6
  523.8 5.4 all-to-all-start.2
  529.2 0.1 slice_reduce_fusion.1
  529.4 0.1 mul.56
  529.4 0.1 add.48
  529.5 0.0 copy-done
  529.5 0.1 reduce_sum.67
  529.6 0.3 multiply_reduce_fusion
  529.9 0.0 copy-done.4
  529.9 1.1 add_convert_fusion
  531.0 0.0 copy-done.6
  531.0 0.1 copy.27
  531.2 0.6 pad.10.refs_1_
  531.8 13.5 %update_2.1 = (f32[64,24579]{1,0:T(8,128)}, f32[64,24579]{1,0:T(8,128)}, f32[64,24579]{1,0:T(8,128)}, f32[64,24579]{1,0:T(8,128)}) custom-call(bf16[16,64,1152]{2,1,0:T(8,128)(2,1)} %get-tuple-element.80.refs_0_, f32[64,128]{1,0:T(8,128)} %pad.10.refs_1_, f32[64,24579]{1,0:T(8,128)} %refs_1_.1, f32[64,24579]{1,0:T(8,128)} %refs_2_.3, f32[64,24579]{1,0:T(8,128)} %refs_3_.3, ...), custom_call_target="tpu_custom_call" | custom-call | bytes 47185920 | tf_op jit(solution)/shard_map/update_2/pallas_call | solution.py:1542
  545.3 8.7 %all-to-all-done.2.refs_0_ = bf16[16,64,512]{2,1,0:T(8,128)(2,1)S(1)} async-done(((bf16[16,64,512]{2,1,0:T(8,128)(2,1)}), bf16[16,64,512]{2,1,0:T(8,128)(2,1)S(1)}, u32[]{:S(2)}, u32[]{:S(2)}) %all-to-all-start.2) | async-done | bytes 1048608 | tf_op jit(solution)/shard_map/all_to_all | solution.py:1585
  554.0 0.0 copy-start.1
  554.0 1.0 copy-done.1
  554.9 6.8 %update_0.1 = (f32[64,24579]{1,0:T(8,128)}, f32[64,24579]{1,0:T(8,128)}, f32[64,24579]{1,0:T(8,128)}, f32[64,24579]{1,0:T(8,128)}) custom-call(bf16[16,64,512]{2,1,0:T(8,128)(2,1)} %copy-done.1, f32[64,24579]{1,0:T(8,128)} %refs_1_.1, f32[64,24579]{1,0:T(8,128)} %refs_2_.3, ...), custom_call_target="tpu_custom_call", output_to_operand_aliasing={{0}: (5, {}), {1}: (6, {}), {2}: (7, {}), {3}: (8, {})} | custom-call | bytes 18874368 | tf_op jit(solution)/shard_map/update_0/pallas_call | solution.py:1542
  561.8 0.0 copy-done.5
  561.8 0.8 copy.34
  (13 shorter events, 0.1 us)
Async XLA Ops:
  7.2 105.6 %copy-start.8 = (s32[1,4]{1,0:T(1,128)S(1)}, s32[1,4]{1,0:T(1,128)}, u32[]{:S(2)}) copy-start(s32[1,4]{1,0:T(1,128)} %param.15) | copy-start | bytes 52
  7.2 105.7 %copy-start.9 = (s32[1,4]{1,0:T(1,128)S(1)}, s32[1,4]{1,0:T(1,128)}, u32[]{:S(2)}) copy-start(s32[1,4]{1,0:T(1,128)} %param.17) | copy-start | bytes 52
  7.2 89.6 %all-gather.2.cloned.1.call-start = ((), (), s32[]{:S(2)}) async-start(), calls=%async_computation.3 | async-start | bytes 4456448 | tf_op jit(solution)/shard_map/all_gather | solution.py:1601
  12.3 105.0 %copy-start.7 = (s32[1,4]{1,0:T(1,128)S(1)}, s32[1,4]{1,0:T(1,128)}, u32[]{:S(2)}) copy-start(s32[1,4]{1,0:T(1,128)} %param.16) | copy-start | bytes 52
  96.8 67.4 %all-to-all-start = ((bf16[16,64,1152]{2,1,0:T(8,128)(2,1)}), bf16[16,64,1152]{2,1,0:T(8,128)(2,1)S(1)}, u32[]{:S(2)}, u32[]{:S(2)}) async-start(bf16[16,64,1152]{2,1,0:T(8,128)(2,1)} %get-tuple-element.59), calls=%async_computation | async-start | bytes 4718592 | tf_op jit(solution)/shard_map/all_to_all | solution.py:1609
  117.0 47.2 %collective-permute-start = (bf16[512,2048]{1,0:T(8,128)(2,1)}, bf16[512,2048]{1,0:T(8,128)(2,1)}, u32[]{:S(2)}, u32[]{:S(2)}) collective-permute-start(bf16[512,2048]{1,0:T(8,128)(2,1)} %constant_dynamic-slice_fusion), channel_id=1, source_target_pairs={{0,16},{16,0},{1,17},{17,1},{2,18},{18,2},{3,19},{19,3},{4,20},{20... | collective-permute-start | bytes 6291464 | tf_op jit(solution)/shard_map/ppermute | solution.py:1608
  164.2 1.4 copy-start.2
  390.5 25.1 %all-to-all-start.1 = ((bf16[16,128,128]{2,1,0:T(8,128)(2,1)}), bf16[16,128,128]{2,1,0:T(8,128)(2,1)S(1)}, u32[]{:S(2)}, u32[]{:S(2)}) async-start(bf16[16,128,128]{2,1,0:T(8,128)(2,1)} %get-tuple-element.74), calls=%async_computation.1 | async-start | bytes 1048576 | tf_op jit(solution)/shard_map/all_to_all | solution.py:1623
  415.6 0.8 copy-start.3
  416.4 113.1 %copy-start = (f32[128,2048]{1,0:T(8,128)S(1)}, f32[128,2048]{1,0:T(8,128)}, u32[]{:S(2)}) copy-start(f32[128,2048]{1,0:T(8,128)} %get-tuple-element.61.res_ref) | copy-start | bytes 3145732
  416.4 113.5 %copy-start.4 = (f32[128,2048]{1,0:T(8,128)S(1)}, f32[128,2048]{1,0:T(8,128)}, u32[]{:S(2)}) copy-start(f32[128,2048]{1,0:T(8,128)} %get-tuple-element.66) | copy-start | bytes 3145732
  523.8 7.3 %copy-start.6 = (f32[8,128]{1,0:T(8,128)S(1)}, f32[8,128]{1,0:T(8,128)}, u32[]{:S(2)}) copy-start(f32[8,128]{1,0:T(8,128)} %get-tuple-element.81) | copy-start | bytes 12292
  523.8 30.2 %all-to-all-start.2 = ((bf16[16,64,512]{2,1,0:T(8,128)(2,1)}), bf16[16,64,512]{2,1,0:T(8,128)(2,1)S(1)}, u32[]{:S(2)}, u32[]{:S(2)}) async-start(bf16[16,64,512]{2,1,0:T(8,128)(2,1)} %bitcast.39), calls=%async_computation.2 | async-start | bytes 2097152 | tf_op jit(solution)/shard_map/all_to_all | solution.py:1585
  554.0 1.0 copy-start.1
  554.9 6.8 %copy-start.5 = (bf16[128,2048]{1,0:T(8,128)(2,1)S(1)}, bf16[128,2048]{1,0:T(8,128)(2,1)}, u32[]{:S(2)}) copy-start(bf16[128,2048]{1,0:T(8,128)(2,1)} %get-tuple-element.112) | copy-start | bytes 1572868
Sparse Core Ops, SparseCore 0:
  12.5 71.6 all-gather.1
